TPU v7x, 32 devices: a whole 2x2x4 slice. The times are simulated.
32 devices in a mesh: groups: 2 (over y), store: 4 (over x, core), tensor: 4 (over z).
Axes of the slice: x: 2, y: 2, z: 4, core: 2. Of those that a mesh axis runs over, the one named last changes fastest.
Arguments:
- cached_rows: bfloat16 [8, 2048, 8192], P(('groups', 'store'), None, 'tensor'), parts along dimension 0, may hold values from -400 to 400
- counts: int32 [8], P(('groups', 'store')), parts along dimension 0, may hold values from 0 to 16, as said below
- dest_table: int32 [8, 16], P(('groups', 'store')), parts along dimension 0, may hold values from -1 to 31, as said below
- positions: int32 [8192], P(('groups', 'store')), parts along dimension 0, may hold values from 0 to 32767
- norm_gain: float32 [8192], replicated, may hold values from 0.1 to 1.9
- key_weight: bfloat16 [8192, 4096], P(None, 'tensor'), may hold values from -0.0625 to 0.0625
- value_weight: bfloat16 [8192, 4096], P(None, 'tensor'), may hold values from -0.0625 to 0.0625
- key_bias: float32 [4096], P('tensor'), may hold values from -4 to 4
- value_bias: float32 [4096], P('tensor'), may hold values from -4 to 4
Outputs:
- key_out: bfloat16 [8192, 4096], P(('groups', 'store'), 'tensor'), parts along dimension 0
- value_out: bfloat16 [8192, 4096], P(('groups', 'store'), 'tensor'), parts along dimension 0
There are 2 independent parts, one for each index of `groups`. A program takes and returns all parts, laid end to end along the dimension named above; an argument that names none is the same for every part. Nothing has to cross between parts.
Inputs may be any that keep to these rules, and one draw needn't show every extreme that they name: `counts`: one store device holds 16 blocks; they sum to 32 over the store devices. `dest_table`: slots below a device's count name each of the 32 blocks exactly once over all store devices; slots beyond it hold -1. A device holds at most 4 blocks that belong to one index of store (blocks b with b // 8 equal), and one device holds exactly 4 for every index; a device's valid slots run in order of that index.
All inputs are finite; a program needn't handle non-finite values.
Results may differ from a plain program's by a relative error of at most 0.0041.
Values may be sent and summed in bfloat16 or wider, within the bound.
No kernel may reach another device: no remote copies, remote signals or barrier semaphores. Data moves between devices by JAX's collectives and lax.ppermute only.
A program may use at most 192 MiB of HBM per device.

v0:
```python
import jax
import jax.numpy as jnp
from jax import lax
from jax.sharding import PartitionSpec as P

HD = 128
BLOCK = 128
ROWS_DEV = 1024


rope_base = 1000000.0


def slot_ranks(dest_table, counts, per_row):
    slot_ids = jnp.arange(dest_table.shape[1], dtype=jnp.int32)
    is_valid = slot_ids[None, :] < counts[:, None]
    row_ids = jnp.where(is_valid, dest_table // per_row, -1)
    earlier = (
        (row_ids[:, :, None] == row_ids[:, None, :])
        & (slot_ids[None, None, :] < slot_ids[None, :, None])
        & is_valid[:, None, :]
    )
    row_rank = jnp.sum(earlier.astype(jnp.int32), axis=2)
    return (is_valid, row_ids, row_rank)


def rotate_keys(key_raw, positions):
    heads_here = key_raw.shape[1] // HD
    half_size = HD // 2
    per_head = key_raw.reshape(key_raw.shape[0], heads_here, HD)
    inverse = 1.0 / rope_base ** (jnp.arange(half_size, dtype=jnp.float32) * 2.0 / HD)
    angles = positions.astype(jnp.float32)[:, None] * inverse[None, :]
    cosine = jnp.cos(angles)[:, None, :]
    sine_part = jnp.sin(angles)[:, None, :]
    first_half = per_head[:, :, :half_size]
    second_half = per_head[:, :, half_size:]
    rotated = jnp.concatenate(
        [
            first_half * cosine - second_half * sine_part,
            second_half * cosine + first_half * sine_part,
        ],
        axis=2,
    )
    return rotated.reshape(key_raw.shape[0], heads_here * HD)


def shards(
    cached_rows,
    counts,
    dest_table,
    positions,
    norm_gain,
    key_weight,
    value_weight,
    key_bias,
    value_bias,
):
    stores = lax.axis_size("store")
    own_row = lax.axis_index("store")
    capacity = dest_table.shape[1]
    per_pair = capacity // stores
    per_row = ROWS_DEV // BLOCK
    width_local = cached_rows.shape[2]
    flat_slots = cached_rows.reshape(capacity, BLOCK * width_local)
    all_counts, all_table = (
        lax.all_gather(counts, "store", axis=0, tiled=True),
        lax.all_gather(dest_table, "store", axis=0, tiled=True),
    )
    is_valid, row_ids, row_rank = slot_ranks(all_table, all_counts, per_row)
    target = own_row * per_row + jnp.arange(per_row, dtype=jnp.int32)
    own_valid, own_rows, own_rank = slot_ranks(dest_table, counts, per_row)
    pick_send = (
        own_valid[0][None, None, :]
        & (own_rows[0][None, None, :] == jnp.arange(stores, dtype=jnp.int32)[:, None, None])
        & (own_rank[0][None, None, :] == jnp.arange(per_pair, dtype=jnp.int32)[None, :, None])
    ).astype(jnp.bfloat16)
    outgoing = jnp.einsum(
        "rkj,jf->rkf", pick_send, flat_slots, preferred_element_type=jnp.float32
    ).astype(jnp.bfloat16)
    arrived = lax.all_to_all(outgoing, "store", split_axis=0, concat_axis=0, tiled=True)
    placing = (
        is_valid[None, :, :, None]
        & (all_table[None, :, :, None] == target[:, None, None, None])
        & (row_rank[None, :, :, None] == jnp.arange(per_pair, dtype=jnp.int32)[None, None, None, :])
    )
    placing = jnp.sum(placing.astype(jnp.int32), axis=2).astype(jnp.bfloat16)
    collected = jnp.einsum("bsk,skf->bf", placing, arrived, preferred_element_type=jnp.float32)
    local_rows = collected.astype(jnp.bfloat16).reshape(per_row * BLOCK, width_local)
    whole_rows = lax.all_gather(local_rows, "tensor", axis=1, tiled=True)
    whole_f32 = whole_rows.astype(jnp.float32)
    inv_scale = lax.rsqrt(jnp.mean(whole_f32 * whole_f32, axis=1) + 1e-06)
    normed = (whole_f32 * inv_scale[:, None] * norm_gain[None, :]).astype(jnp.bfloat16)
    key_sum = jnp.dot(normed, key_weight, preferred_element_type=jnp.float32)
    value_sum = jnp.dot(normed, value_weight, preferred_element_type=jnp.float32)
    key_out = rotate_keys(key_sum + key_bias[None, :], positions).astype(jnp.bfloat16)
    value_out = (value_sum + value_bias[None, :]).astype(jnp.bfloat16)
    return (key_out, value_out)


def solution(mesh):
    in_specs = (
        P(("groups", "store"), None, "tensor"),
        P(("groups", "store")),
        P(("groups", "store"), None),
        P(("groups", "store")),
        P(),
        P(None, "tensor"),
        P(None, "tensor"),
        P("tensor"),
        P("tensor"),
    )
    out_specs = (P(("groups", "store"), "tensor"), P(("groups", "store"), "tensor"))
    return jax.shard_map(shards, mesh=mesh, in_specs=in_specs, out_specs=out_specs, check_vma=False)
```

profile of v0, /device:TPU:0, one launch (start us, length us, event | category | flops | bytes accessed | tf_op | source)
XLA Modules:
  0.0 505.8 jit_solution(10969518912172376401)
XLA Ops:
  7.8 0.7 fusion.23
  8.5 0.2 convert_reduce_fusion.2
  8.7 8.0 %reshape.345 = bf16[16,262144,1]{1,0,2:T(8,128)(2,1)} reshape(bf16[1,2048,2048]{2,1,0:T(8,128)(2,1)} %param.9) | data formatting | bytes 16777216 | tf_op jit(solution)/shard_map/reshape | solution.py:64
  16.7 9.6 %convolution_convert_fusion = bf16[4,4,262144]{2,1,0:T(4,128)(2,1)} fusion(bf16[16,262144,1]{1,0,2:T(8,128)(2,1)} %reshape.345, pred[4,16]{1,0:T(4,128)(4,1)S(1)} %iota_compare_fusion.3, pred[4,16]{1,0:T(4,128)(4,1)S(1)} %fusion.22), kind=kOutput, calls=%fused_computation | convolution fusion | flops 138412288 | bytes 16777344 | tf_op jit(solution)/shard_map/rkj,jf->rkf/dot_general | solution.py:77
  26.2 5.8 %all-to-all-start = ((bf16[4,4,262144]{2,1,0:T(4,128)(2,1)}), bf16[4,4,262144]{2,1,0:T(4,128)(2,1)}, u32[]{:S(2)}, u32[]{:S(2)}) async-start(bf16[4,4,262144]{2,1,0:T(4,128)(2,1)} %convolution_convert_fusion), calls=%async_computation | async-start | bytes 16777216 | tf_op jit(solution)/shard_map/all_to_all | solution.py:80
  32.1 0.6 dynamic-slice
  32.7 0.8 dynamic-update-slice
  33.4 92.4 %all-reduce = s32[4]{0:T(128)S(1)} all-reduce(s32[4]{0:T(128)S(1)} %dynamic-update-slice), channel_id=1, replica_groups=mesh['groups'=2,'store'=4,'tensor'=4] {'store'}, use_global_device_ids=true, to_apply=%add | all-reduce | flops 4 | bytes 32
  125.9 5.0 all-gather
  130.9 0.1 iota_compare_fusion.5
  131.0 0.2 convert_reduce_fusion.1
  131.3 0.1 compare_and_fusion
  131.3 0.4 convert_reduce_fusion
  131.7 9.1 %fusion = bf16[8,262144]{1,0:T(8,128)(2,1)} fusion(bf16[4,4,262144]{2,1,0:T(4,128)(2,1)} %all-to-all-done, s32[8,4,4]{0,2,1:T(4,128)S(1)} %convert_reduce_fusion), kind=kOutput, calls=%fused_computation.2 | convolution fusion | flops 69206144 | bytes 12583424 | tf_op jit(solution)/shard_map/bsk,skf->bf/dot_general | solution.py:87
  140.8 6.0 %reshape.336 = bf16[1024,2048]{1,0:T(8,128)(2,1)} reshape(bf16[8,262144]{1,0:T(8,128)(2,1)} %fusion) | data formatting | bytes 8388608 | tf_op jit(solution)/shard_map/reshape | solution.py:88
  146.9 1.0 multiply_cosine_fusion
  147.9 287.1 %all-gather.3.cloned.1.call-done = bf16[1024,8192]{1,0:T(8,128)(2,1)} async-done(((bf16[1024,2048]{1,0:T(8,128)(2,1)}), bf16[1024,8192]{1,0:T(8,128)(2,1)}) %all-gather.3.cloned.1.call-update) | async-done | bytes 16777232 | tf_op jit(solution)/shard_map/all_gather | solution.py:89
  434.9 7.5 %fusion.1 = f32[1024]{0:T(1024)S(1)} fusion(bf16[1024,8192]{1,0:T(8,128)(2,1)} %all-gather.3.cloned.1.call-done), kind=kLoop, calls=%fused_computation.5 | loop fusion | flops 25164800 | bytes 16781312 | tf_op jit(solution)/shard_map/reduce_sum | solution.py:91
  442.5 3.1 copy-done
  445.6 24.0 %fusion.8 = f32[1024,1024]{0,1:T(8,128)} fusion(bf16[8192,1024]{1,0:T(8,128)(2,1)} %param.14, bf16[1024,8192]{1,0:T(8,128)(2,1)S(1)} %copy-done, f32[8192]{0:T(1024)S(1)} %copy-done.3, f32[1024]{0:T(1024)S(1)} %add_rsqrt_fusion, f32[1024]{0:T(1024)S(1)} %copy-done.4), kind=kOutput, calls=%fused_computation.11 | convolution fusion | flops 17214472192 | bytes 37789696 | tf_op jit(solution)/shard_map/dot_general | solution.py:93
  469.6 2.9 subtract_convert_fusion
  472.5 0.2 pad_maximum_fusion
  472.7 2.8 copy.19
  475.5 23.5 %add_convert_fusion = bf16[1024,1024]{1,0:T(8,128)(2,1)} fusion(bf16[8192,1024]{1,0:T(8,128)(2,1)} %param.15, bf16[1024,8192]{1,0:T(8,128)(2,1)} %all-gather.3.cloned.1.call-done, f32[8192]{0:T(1024)S(1)} %copy-done.3, f32[1024]{0:T(1024)S(1)} %add_rsqrt_fusion, f32[1024]{0:T(1024)S(1)} %copy-done.5), kind=kOutput, calls=%fused_computation.10 | convolution fusion | flops 17215520768 | bytes 35692544 | tf_op jit(solution)/shard_map/dot_general | solution.py:94
  (27 shorter events, 0.2 us)
Async XLA Ops:
  26.2 5.9 %copy-start.6 = (u32[32]{0:T(128)S(1)}, u32[32]{0:T(128)}, u32[]{:S(2)}) copy-start(u32[32]{0:T(128)} %constant.53) | copy-start | bytes 388
  26.2 99.6 %copy-start.2 = (s32[1,16]{1,0:T(1,128)S(1)}, s32[1,16]{1,0:T(1,128)}, u32[]{:S(2)}) copy-start(s32[1,16]{1,0:T(1,128)} %param.11) | copy-start | bytes 196
  26.2 105.5 %all-to-all-start = ((bf16[4,4,262144]{2,1,0:T(4,128)(2,1)}), bf16[4,4,262144]{2,1,0:T(4,128)(2,1)}, u32[]{:S(2)}, u32[]{:S(2)}) async-start(bf16[4,4,262144]{2,1,0:T(4,128)(2,1)} %convolution_convert_fusion), calls=%async_computation | async-start | bytes 16777216 | tf_op jit(solution)/shard_map/all_to_all | solution.py:80
  32.0 402.9 %all-gather.3.cloned.1.call-start = ((), (), s32[]{:S(2)}) async-start(), calls=%async_computation.1 | async-start | bytes 20971520 | tf_op jit(solution)/shard_map/all_gather | solution.py:89
  140.8 6.0 %copy-start.1 = (s32[1024]{0:T(1024)S(1)}, s32[1024]{0:T(1024)}, u32[]{:S(2)}) copy-start(s32[1024]{0:T(1024)} %param.12) | copy-start | bytes 12292
  146.8 295.6 %copy-start.3 = (f32[8192]{0:T(1024)S(1)}, f32[8192]{0:T(1024)}, u32[]{:S(2)}) copy-start(f32[8192]{0:T(1024)} %param.13) | copy-start | bytes 98308
  147.8 294.6 %copy-start.4 = (f32[1024]{0:T(1024)S(1)}, f32[1024]{0:T(1024)}, u32[]{:S(2)}) copy-start(f32[1024]{0:T(1024)} %param.16) | copy-start | bytes 12292
  434.9 10.7 %copy-start = (bf16[1024,8192]{1,0:T(8,128)(2,1)S(1)}, bf16[1024,8192]{1,0:T(8,128)(2,1)}, u32[]{:S(2)}) copy-start(bf16[1024,8192]{1,0:T(8,128)(2,1)} %all-gather.3.cloned.1.call-done) | copy-start | bytes 50331652
  469.6 5.9 %copy-start.5 = (f32[1024]{0:T(1024)S(1)}, f32[1024]{0:T(1024)}, u32[]{:S(2)}) copy-start(f32[1024]{0:T(1024)} %param.17) | copy-start | bytes 12292
Sparse Core Ops, SparseCore 0:
  146.9 287.9 all-gather.2
where the time goes:
time: 506 us
  waiting for transfers between devices  287 us (57%)
  blocking collectives  97.4 us (19%)
  matrix products  66.1 us (13%)
  local copies, waits for them, and re-layouts  21.2 us (4%)
  between operations  14.8 us (3%)
  other arithmetic  13.3 us (3%)
  starting transfers between devices  5.83 us (1%)
    all_gather x1, waiting for transfers between devices, shards(): whole_rows = lax.all_gather(local_rows, 'tensor', axis=1, tiled=True)  287 us
    unnamed x1, blocking collectives  92.4 us
    dot_general x1, matrix products, shards(): key_sum = jnp.dot(normed, key_weight, preferred_element_type=jnp.float32)  24 us
    dot_general x1, matrix products, shards(): jnp.dot(normed, value_weight, preferred_element_type=jnp.float32)  23.5 us
  transfers between devices with their start and end apart: 2, of which 1 were waited for; matrix products, arithmetic and copies ran while one was open for 1% of the time, Pallas kernels for 0%

commit v1 on v0

v1 whole, which is shorter than its diff:
```python
import collections
import functools

import jax
import jax.numpy as jnp
from jax import lax
from jax.experimental import pallas as pl
from jax.experimental.pallas import tpu as pltpu
from jax.sharding import PartitionSpec as P

HD = 128
BLOCK = 128
ROPE_BASE = 1000000.0
EPS = 1e-06
MIB = 1 << 20
VMEM_LIMIT = 63 * MIB
COST = 4 * 10**9
FAR = 10**11
HBM = pl.BlockSpec(memory_space=pltpu.HBM)
SMEM = pl.BlockSpec(memory_space=pltpu.SMEM)
VMEM = pl.BlockSpec(memory_space=pltpu.VMEM)
TOKEN = jax.ShapeDtypeStruct((8, 128), jnp.int32)

STEPS = ((0, 0, 64), (0, 64, 64), (1, 0, 128), (2, 0, 128), (3, 0, 128))
CHUNKS = ((0, 0, 64), (0, 64, 64), (1, 0, 128), (2, 0, 128), (3, 0, 128))


def rope_tables(positions):
    half = HD // 2
    inverse = 1.0 / ROPE_BASE ** (jnp.arange(half, dtype=jnp.float32) * 2.0 / HD)
    angles = positions.astype(jnp.float32)[:, None] * inverse[None, :]
    cosine, sine = jnp.cos(angles), jnp.sin(angles)
    return (
        jnp.concatenate([cosine, cosine], axis=1),
        jnp.concatenate([-sine, sine], axis=1),
    )


class Chain:
    def __init__(self):
        self.token = None

    def __call__(self, kernel, name, args, specs, outs, out_specs, scratch=(), grid=None, aliases=None, cost=COST):
        first = self.token is None
        prefetch = 0 if grid is None else 1
        taken, given = len(args), len(outs)

        def body(*refs):
            ins = refs[:taken]
            after = taken + (0 if first else 1)
            kernel(*ins, *refs[after : after + given], *refs[after + given + 1 :])

        tokens = () if first else (self.token,)
        in_specs = list(specs) + [HBM] * len(tokens)
        out_specs = list(out_specs) + [HBM]
        if grid is None:
            where = dict(in_specs=in_specs, out_specs=out_specs, scratch_shapes=list(scratch))
        else:
            where = dict(
                grid_spec=pltpu.PrefetchScalarGridSpec(
                    num_scalar_prefetch=prefetch,
                    grid=grid,
                    in_specs=in_specs,
                    out_specs=out_specs,
                    scratch_shapes=list(scratch),
                )
            )
        result = pl.pallas_call(
            body,
            out_shape=tuple(outs) + (TOKEN,),
            input_output_aliases=aliases or {},
            compiler_params=pltpu.CompilerParams(vmem_limit_bytes=VMEM_LIMIT),
            cost_estimate=pl.CostEstimate(flops=cost, bytes_accessed=1, transcendentals=0),
            name=name,
            **where,
        )(*args, *tokens)
        self.token = result[-1]
        return result[:-1]

    def pin(self, name, arrays, cost=COST):
        outs = [jax.ShapeDtypeStruct(a.shape, a.dtype) for a in arrays]
        n = len(arrays)
        return self(
            lambda *refs: None, name, arrays, [HBM] * n, outs, [HBM] * n, aliases={i: i for i in range(n)}, cost=cost
        )


def in_row(table, low, per_row):
    start, count = jnp.int32(0), jnp.int32(0)
    for s in range(table.shape[1]):
        block = table[0, s]
        start += ((block >= 0) & (block < low)).astype(jnp.int32)
        count += ((block >= low) & (block < low + per_row)).astype(jnp.int32)
    return start, count


def plan_kernel(stores, per_row, *refs):
    tables, plan = refs[:-1], refs[-1]
    low = lax.axis_index("store") * per_row
    spans = [in_row(t, low, per_row) for t in tables]
    n = jnp.int32(0)
    for i in range(per_row):
        for f in range(3):
            plan[i, f] = jnp.int32(0)
    for r in range(tables[0].shape[1] // stores):
        for m in range(stores):
            start, count = spans[m]
            valid = r < count

            @pl.when(valid)
            def _():
                plan[n, 0] = jnp.int32(r * stores + m)
                plan[n, 1] = start + r
                plan[n, 2] = tables[m][0, start + r] - low

            n += valid.astype(jnp.int32)


def send_kernel(steps, per_row, table, cached, *refs):
    outs, sems = refs[:-1], refs[-1]
    own_row = lax.axis_index("store")
    last = table.shape[1] - 1
    starts = {m: in_row(table, (own_row ^ m) * per_row, per_row)[0] for m in {m for s in steps for _, m, _ in s}}
    copies = []
    for out, parts in zip(outs, steps):
        for at, m, (k, low, rows) in parts:
            src = pl.multiple_of(jnp.minimum(starts[m] + k, last) * BLOCK + low, 16)
            copies.append(
                pltpu.make_async_copy(cached.at[pl.ds(src, rows)], out.at[pl.ds(at, rows)], sems.at[len(copies)])
            )
            copies[-1].start()
    for c in copies:
        c.wait()


def cut_kernel(key_weight, value_weight, out, sems):
    z, y, own_row = lax.axis_index("tensor"), lax.axis_index("groups"), lax.axis_index("store")
    share = out.shape[0] // 2
    slab = jnp.where(z == 0, 2 + y, 1 - y)
    at = pl.multiple_of((slab * 4 + own_row) * share, 128)
    copies = [
        pltpu.make_async_copy(weight.at[pl.ds(at, share)], out.at[pl.ds(g * share, share)], sems.at[g])
        for g, weight in enumerate((key_weight, value_weight))
    ]
    for c in copies:
        c.start()
    for c in copies:
        c.wait()


def split_kernel(both, keys, values, sems):
    share = keys.shape[0]
    copies = [
        pltpu.make_async_copy(both.at[pl.ds(g * share, share)], out, sems.at[g])
        for g, out in enumerate((keys, values))
    ]
    for c in copies:
        c.start()
    for c in copies:
        c.wait()


def join_kernel(info, *refs):
    all_out, sems = refs[6], refs[7]
    copies = []
    for g, out in enumerate(refs[4:6]):
        share = out.shape[0] // 2
        place = info[5 + g]
        for t, src in enumerate(refs[2 * g : 2 * g + 2]):
            at = pl.multiple_of((place if t == 0 else 1 - place) * share, 128)
            copies.append(pltpu.make_async_copy(src, out.at[pl.ds(at, share)], sems.at[0, g, t]))
            there = all_out.at[pl.ds(at + 2 * g * share, share)]
            copies.append(pltpu.make_async_copy(src, there, sems.at[1, g, t]))
    for c in copies:
        c.start()
    for c in copies:
        c.wait()


def prep_kernel(low, rows, first, stores, pieces, plan, cached, *refs):
    arrived = refs[: len(pieces)]
    gain, y_out, ssq_out, held, sems = refs[len(pieces) :]
    width = held.shape[2]
    for j in range(2):
        code = plan[first + j, 0]

        @pl.when(lax.rem(code, stores) == 0)
        def _():
            start = pl.multiple_of(plan[first + j, 1] * BLOCK + low, 16)
            pltpu.make_async_copy(cached.at[pl.ds(start, rows)], held.at[j], sems.at[j]).start()

        for (r, m, p_low, p_rows, at), ref in zip(pieces, arrived):
            a, b = max(low, p_low), min(low + rows, p_low + p_rows)

            @pl.when(code == r * stores + m)
            def _():
                pltpu.make_async_copy(
                    ref.at[pl.ds(at + a - p_low, b - a)], held.at[j, pl.ds(a - low, b - a)], sems.at[j]
                ).start()

    for j in range(2):
        pltpu.make_async_copy(cached.at[pl.ds(0, rows)], held.at[j], sems.at[j]).wait()
        sums = jnp.zeros((rows, 128), jnp.float32)
        for c in range(0, width, 128):
            x = held[j, :, c : c + 128].astype(jnp.float32)
            y_out[j * rows : (j + 1) * rows, c : c + 128] = (x * gain[:, c : c + 128]).astype(jnp.bfloat16)
            sums += x * x
        ssq_out[j : j + 1, :rows] = jnp.sum(sums.T, axis=0, keepdims=True)


def sums_kernel(step, *refs):
    out = refs[-1]
    if step == 0:
        out[...] = jnp.zeros_like(out)
        for i, ref in enumerate(refs[:-1]):
            out[2 * i : 2 * i + 2, :] = ref[...]
    else:
        out[...] = refs[0][...] + refs[1][...]


def relay_kernel(own, ex, out, sems):
    rows = own.shape[0]
    copies = [
        pltpu.make_async_copy(src, out.at[pl.ds(i * rows, rows)], sems.at[i]) for i, src in enumerate((own, ex))
    ]
    for c in copies:
        c.start()
    for c in copies:
        c.wait()


def near_kernel(sizes, first, handed, info, *refs):
    n = len(sizes)
    wk, wv, acc, acts, sems = refs[-5:]
    arrays = refs[:-5]
    per = len(arrays) // n
    slabs = acts.shape[0]
    i = pl.program_id(0)
    slab, half = first + i // 2, lax.rem(i, 2)
    inner = info[4] == 1
    full = (i >= 0) if handed else inner
    starts = [sum(sizes[:c]) for c in range(n)]

    def copies(s, which, skip=0):
        return [
            pltpu.make_async_copy(
                arrays[per * c + which].at[pl.ds(skip * sizes[c], sizes[c])],
                acts.at[s - first, pl.ds(starts[c], sizes[c])],
                sems.at[s - first, c],
            )
            for c in range(n)
        ]

    @pl.when(i == 0)
    def _():
        for s in range(first, first + slabs):
            if s < 2:
                for c in copies(s, s):
                    c.start()
            else:

                @pl.when(inner)
                def _():
                    for c in copies(s, 2 - first, s - 2):
                        c.start()

                if handed:

                    @pl.when(jnp.logical_not(inner))
                    def _():
                        for c in copies(s, 3 - first, s - 2):
                            c.start()

    for s in range(first, first + slabs):

        @pl.when((half == 0) & (slab == s) & ((s < 2) | full))
        def _():
            for c in copies(s, 0):
                c.wait()

    part, cols = wk.shape

    @pl.when(i == 0)
    def _():
        if first >= 2 and not handed:
            acc[...] = jnp.zeros_like(acc)

        @pl.when((first < 2) | full)
        def _():
            a = acts[0, :, :part]
            acc[:, :cols] = jnp.dot(a, wk[...], preferred_element_type=jnp.float32)
            acc[:, cols:] = jnp.dot(a, wv[...], preferred_element_type=jnp.float32)

    @pl.when((i > 0) & ((slab < 2) | full))
    def _():
        a = acts[slab - first, :, pl.ds(pl.multiple_of(half * part, part), part)]
        acc[:, :cols] += jnp.dot(a, wk[...], preferred_element_type=jnp.float32)
        acc[:, cols:] += jnp.dot(a, wv[...], preferred_element_type=jnp.float32)


def far_kernel(sizes, info, *refs):
    n = len(sizes)
    slabs = refs[:n]
    joined_k, joined_v, came_k, came_v, joined, beside_k, beside_v = refs[n : n + 7]
    out, acts, held, act_sems, sems = refs[n + 7 :]
    starts = [sum(sizes[:c]) for c in range(n)]
    rows, cols = held.shape[1:]
    share = rows // 2
    weights = (joined_k, came_k, joined.at[pl.ds(0, rows)], beside_k)
    weights += (joined_v, came_v, joined.at[pl.ds(rows, rows)], beside_v)
    y, x, core = info[5], info[6], info[7]

    @pl.when(info[4] == 1)
    def _():
        loads = [
            pltpu.make_async_copy(
                slabs[c].at[pl.ds(s * sizes[c], sizes[c])], acts.at[s, pl.ds(starts[c], sizes[c])], act_sems.at[s, c]
            )
            for c in range(n)
            for s in range(2)
        ]
        copies = [pltpu.make_async_copy(w, held.at[i], sems.at[i]) for i, w in enumerate(weights)]
        for c in loads + copies:
            c.start()
        for c in loads:
            c.wait()
        for g in range(2):
            total = None
            for i in range(4):
                copies[4 * g + i].wait()
                here = core if i < 2 else 1 - core
                for t in range(2):
                    if g == 0:
                        slab, chip = t, (x if i % 2 == 0 else 1 - x)
                    else:
                        slab, chip = (y if i % 2 == 0 else 1 - y), t
                    at = pl.multiple_of((2 * chip + here) * share, 128)
                    a = acts[slab, :, pl.ds(at, share)]
                    w = held[4 * g + i, t * share : (t + 1) * share, :]
                    term = jnp.dot(a, w, preferred_element_type=jnp.float32)
                    total = term if total is None else total + term
            out[:, g * cols : (g + 1) * cols] = total.astype(jnp.bfloat16)


def finish_kernel(segments, whole, chained, plan, *refs):
    given = []
    at = 0
    for s in segments:
        n = len(s.accs) + len(s.parts)
        given.append(refs[at : at + n])
        at += n
    ssq_a, ssq_b, bk, bv, cosine, sine = refs[at : at + 6]
    refs = refs[at + 6 + (2 if chained else 0) :]
    k_out, v_out, acc_held, far_held, k_held, v_held, cos_held, sin_held, in_sems, rope_sems, out_sems = refs
    cols = k_held.shape[1]
    loads, spots = [], []
    for i, (s, arrays) in enumerate(zip(segments, given)):
        rows, here, count = s.rows, s.here, 2 * s.rows
        mine = [
            pltpu.make_async_copy(ref.at[pl.ds(row, count)], acc_held.at[t, pl.ds(here, count)], in_sems.at[i, t])
            for t, (row, ref) in enumerate(zip(s.accs, arrays))
        ]
        for p, ((row, col, wide), ref) in enumerate(zip(s.parts, arrays[len(s.accs) :])):
            mine.append(
                pltpu.make_async_copy(
                    ref.at[pl.ds(row, count)],
                    far_held.at[pl.ds(here, count), pl.ds(col, wide)],
                    in_sems.at[i, 2 + p],
                )
            )
        spots.append([pl.multiple_of(plan[s.first + j, 2] * BLOCK + s.low, 16) for j in range(2)])
        for j in range(2):
            for t, (src, dst) in enumerate(((cosine, cos_held), (sine, sin_held))):
                mine.append(
                    pltpu.make_async_copy(
                        src.at[pl.ds(spots[i][j], rows)], dst.at[pl.ds(here + j * rows, rows)], rope_sems.at[i, j, t]
                    )
                )
        for c in mine:
            c.start()
        loads.append(mine)
    stores = []
    for i, s in enumerate(segments):
        rows = s.rows
        for c in loads[i]:
            c.wait()
        for j in range(2):
            row = s.ssq + j
            sums = jnp.broadcast_to(ssq_a[row : row + 1, :] + ssq_b[row : row + 1, :], (8, BLOCK))
            scale = lax.rsqrt(sums.T[:rows, :1] * (1.0 / whole) + EPS)
            span = slice(s.here + j * rows, s.here + (j + 1) * rows)
            cos_rows, sin_rows = cos_held[span, :], sin_held[span, :]
            for h in range(cols // HD):
                lanes = slice(h * HD, (h + 1) * HD)
                k = acc_held[0, span, lanes]
                if len(s.accs) > 1:
                    k += acc_held[1, span, lanes]
                if s.parts:
                    k += far_held[span, lanes].astype(jnp.float32)
                k = k * scale + bk[:, lanes]
                k_held[span, lanes] = (k * cos_rows + pltpu.roll(k, HD // 2, 1) * sin_rows).astype(jnp.bfloat16)
                lanes_v = slice(cols + h * HD, cols + (h + 1) * HD)
                v = acc_held[0, span, lanes_v]
                if len(s.accs) > 1:
                    v += acc_held[1, span, lanes_v]
                if s.parts:
                    v += far_held[span, lanes_v].astype(jnp.float32)
                v_held[span, lanes] = (v * scale + bv[:, lanes]).astype(jnp.bfloat16)
            for t, (held, out) in enumerate(((k_held, k_out), (v_held, v_out))):
                stores.append(
                    pltpu.make_async_copy(
                        held.at[pl.ds(s.here + j * rows, rows)],
                        out.at[pl.ds(spots[i][j], rows)],
                        out_sems.at[i, j, t],
                    )
                )
                stores[-1].start()
    for c in stores:
        c.wait()


Segment = collections.namedtuple(
    "Segment", ("low", "rows", "first", "accs", "here", "ssq", "parts")
)


def grouped(cached_rows, counts, dest_table, positions, norm_gain, key_weight, value_weight, key_bias, value_bias):
    stores = lax.axis_size("store")
    z, y = lax.axis_index("tensor"), lax.axis_index("groups")
    tokens = positions.shape[0]
    per_row = tokens // BLOCK
    most = dest_table.shape[1] // stores
    cached = cached_rows[0]
    width = cached.shape[1]
    whole, cols = key_weight.shape
    part, share = width // 2, whole // 16
    dma = pltpu.SemaphoreType.DMA
    bf16 = functools.partial(jax.ShapeDtypeStruct, dtype=jnp.bfloat16)
    f32 = functools.partial(jax.ShapeDtypeStruct, dtype=jnp.float32)
    swap = {m: ("store", [(s, s ^ m) for s in range(stores)]) for m in range(1, stores)}
    pair = ("tensor", [(0, 1), (1, 0), (2, 3), (3, 2)])
    middle = ("tensor", [(1, 2), (2, 1)])
    inward = ("tensor", [(0, 1), (3, 2)])
    outward = ("tensor", [(1, 0), (2, 3)])
    across = ("groups", [(0, 1), (1, 0)])
    ends = ("tensor", [(0, 3), (1, 2), (2, 1), (3, 0)])

    inner = (z == 1) | (z == 2)
    other = [jnp.where(inner, 3 - z, z ^ 2), jnp.where(inner, (3 - z) ^ 1, 3 - z)]
    chip, core = lax.axis_index("store") // 2, lax.rem(lax.axis_index("store"), 2)
    info = jnp.stack([z, z ^ 1, *other, inner.astype(jnp.int32), y, chip, core]).astype(jnp.int32)
    gain = lax.dynamic_slice_in_dim(norm_gain, z * width, width, 0)[None, :]
    cosine, sine = rope_tables(positions)

    call = Chain()
    came, own, ssq, ex, mr, fw, accs, far = {}, {}, {}, {}, {}, {}, {}, {}
    done = []

    def move(label, array, way):
        with jax.named_scope(label):
            return lax.ppermute(array, *way)

    def send(*parts):
        shapes = [bf16((sum(s[2] for _, _, s in p), width)) for p in parts]
        return call(
            functools.partial(send_kernel, parts, per_row),
            "send",
            (dest_table, cached),
            [SMEM, HBM],
            shapes,
            [VMEM] * len(shapes),
            [dma((sum(len(p) for p in parts),))],
        )

    def prep(c):
        k, low, rows = CHUNKS[c]
        pieces, arrays = [], []
        for r in range(k + 1):
            pieces.append((r, 1, 0, BLOCK, r * BLOCK))
            arrays.append(beside)
        for i, (r, p_low, p_rows) in enumerate(STEPS):
            if r <= k and p_low < low + rows and low < p_low + p_rows:
                for m in (2, 3):
                    array, at = came[i][m]
                    pieces.append((r, m, p_low, p_rows, at))
                    arrays.append(array)
        own[c], ssq[c] = call(
            functools.partial(prep_kernel, low, rows, 2 * k, stores, pieces),
            "prep",
            (plan, cached, *arrays, gain),
            [SMEM, HBM] + [HBM] * len(pieces) + [VMEM],
            [bf16((2 * rows, width)), f32((2, BLOCK))],
            [VMEM, VMEM],
            [pltpu.VMEM((2, rows, width), jnp.bfloat16), dma((2,))],
        )

    def pass_own(c):
        ex[c] = move("ex%d" % c, own[c], pair)

    def relay(c):
        rows = 2 * CHUNKS[c][2]
        (both,) = call(
            relay_kernel, "relay", (own[c], ex[c]), [HBM] * 2, [bf16((2 * rows, width))], [VMEM], [dma((2,))]
        )
        mr[c] = move("mr%d" % c, both, middle)

    def pin(*arrays, cost=COST):
        return call.pin("pin", arrays, cost)

    def hand(c):
        fw[c] = move("fw%d" % c, mr[c], outward)

    def sums(step, *arrays):
        (out,) = call(
            functools.partial(sums_kernel, step), "sums", arrays, [VMEM] * len(arrays), [f32((16, BLOCK))], [VMEM]
        )
        return out

    def near(taken, first, last, handed):
        sizes = [2 * CHUNKS[c][2] for c in taken]
        total = sum(sizes)
        kinds = ((own, ex) if first == 0 else ()) + ((mr,) if last == 4 else ()) + ((fw,) if last == 4 and handed else ())
        slabs = [kind[c] for c in taken for kind in kinds]

        def weights(i, info):
            slab = first + i // 2
            skip = (slab >= 2) & (info[4] == 0) & (not handed)
            return (jnp.where(skip, info[1] * 2 + 1, info[slab] * 2 + lax.rem(i, 2)), 0)

        (acc,) = call(
            functools.partial(near_kernel, sizes, first, handed),
            "near",
            (info, *slabs, key_weight, value_weight),
            [HBM] * len(slabs) + [pl.BlockSpec((part, cols), weights)] * 2,
            [f32((total, 2 * cols))],
            [pl.BlockSpec((total, 2 * cols), lambda i, info: (0, 0))],
            [pltpu.VMEM((last - first, total, width), jnp.bfloat16), dma((last - first, len(sizes)))],
            grid=(2 * (last - first),),
        )
        for i, c in enumerate(taken):
            accs.setdefault(c, []).append((acc, sum(sizes[:i])))

    def reach(*taken):
        sizes = [2 * CHUNKS[c][2] for c in taken]
        total = sum(sizes)
        (out,) = call(
            functools.partial(far_kernel, sizes),
            "far",
            (info, *(mr[c] for c in taken), *reached),
            [SMEM] + [HBM] * (len(taken) + len(reached)),
            [bf16((total, 2 * cols))],
            [VMEM],
            [
                pltpu.VMEM((2, total, width), jnp.bfloat16),
                pltpu.VMEM((8, *reached[0].shape), jnp.bfloat16),
                dma((2, len(sizes))),
                dma((8,)),
            ],
        )
        out = move("far%d" % taken[0], out, outward)
        for i, c in enumerate(taken):
            far.setdefault(c, []).append((out, (sum(sizes[:i]), 0, 2 * cols)))

    def finish(*taken):
        segments, arrays, here = [], [], 0
        for c in taken:
            k, low, rows = CHUNKS[c]
            arrays += [a for a, _ in accs[c]] + [a for a, _ in far.get(c, [])]
            segments.append(
                Segment(low, rows, 2 * k, [r for _, r in accs[c]], here, 2 * c, [p for _, p in far.get(c, [])])
            )
            here += 2 * rows
        most_accs = max(len(s.accs) for s in segments)
        args = [plan, *arrays, *total_squares, key_bias[None, :], value_bias[None, :], cosine, sine, *done]
        done[:] = call(
            functools.partial(finish_kernel, segments, whole, bool(done)),
            "finish",
            tuple(args),
            [SMEM] + [HBM] * len(arrays) + [VMEM] * 4 + [HBM] * (2 + len(done)),
            [bf16((tokens, cols))] * 2,
            [HBM] * 2,
            [
                pltpu.VMEM((most_accs, here, 2 * cols), jnp.float32),
                pltpu.VMEM((here, 2 * cols), jnp.bfloat16),
                pltpu.VMEM((here, cols), jnp.bfloat16),
                pltpu.VMEM((here, cols), jnp.bfloat16),
                pltpu.VMEM((here, HD), jnp.float32),
                pltpu.VMEM((here, HD), jnp.float32),
                dma((len(segments), 4)),
                dma((len(segments), 2, 2)),
                dma((len(segments), 2, 2)),
            ],
            aliases={len(args) - 2: 0, len(args) - 1: 1} if done else None,
        )

    def both_ways(i):
        return [[(0, m, STEPS[i])] for m in (2, 3)]

    def exchange(i, sent):
        came[i] = {m: (move("a%d" % i, array, swap[m]), 0) for m, array in zip((2, 3), sent)}

    tables = [move("table", dest_table, swap[m]) for m in range(1, stores)]
    *s0, bulk = send(*both_ways(0), [(k * BLOCK, 1, (k, 0, BLOCK)) for k in range(most)])
    exchange(0, s0)
    beside = move("beside", bulk, swap[1])
    (plan,) = call(
        functools.partial(plan_kernel, stores, per_row),
        "plan",
        (dest_table, *tables),
        [SMEM] * stores,
        [jax.ShapeDtypeStruct((per_row, 4), jnp.int32)],
        [SMEM],
    )
    (lent,) = call(
        cut_kernel, "cut", (key_weight, value_weight), [HBM] * 2, [bf16((2 * share, cols))], [VMEM], [dma((2,))]
    )
    both = [[(m % 2 * 2 * BLOCK + t * BLOCK, m, STEPS[3 + t]) for m in (2, 3) for t in range(2)]]
    *s1, s2a, s2b, s3 = send(*both_ways(1), *both_ways(2), *both)
    exchange(1, s1)
    prep(0)
    pass_own(0)
    prep(1)
    pass_own(1)
    s2a, s2b, lent = pin(s2a, s2b, lent)
    exchange(2, (s2a, s2b))
    lent = move("in", lent, inward)
    relay(0)
    relay(1)
    prep(2)
    pass_own(2)
    (s3,) = pin(s3)
    late = move("h3", s3, swap[2])
    (mr[0],) = pin(mr[0])
    hand(0)
    near((0, 1), 0, 2, True)
    mr[1], fw[0], lent = pin(mr[1], fw[0], lent)
    hand(1)
    relay(2)
    (late,) = pin(late)
    turned = move("c3", late, swap[1])
    for t in range(2):
        came[3 + t] = {2: (late, t * BLOCK), 3: (turned, 2 * BLOCK + t * BLOCK)}
    lent_k, lent_v = call(
        split_kernel, "split", (lent,), [HBM], [bf16((share, cols))] * 2, [VMEM] * 2, [dma((2,))]
    )
    came_k, came_v = move("wk1", lent_k, across), move("wv1", lent_v, swap[2])
    prep(3)
    pass_own(3)
    prep(4)
    (fw[1],) = pin(fw[1])
    squares = sums(0, *(ssq[c] for c in range(len(CHUNKS))))
    paired = move("half", squares, pair)
    joined_k, joined_v, joined = call(
        join_kernel,
        "join",
        (info, lent_k, came_k, lent_v, came_v),
        [SMEM] + [HBM] * 4,
        [bf16((2 * share, cols))] * 2 + [bf16((4 * share, cols))],
        [VMEM] * 3,
        [dma((2, 2, 2))],
    )
    came_k, came_v = move("wk2", joined_k, swap[2]), move("wv2", joined_v, across)
    near((0, 1), 2, 4, True)
    squares = sums(1, squares, paired)
    rest = move("rest", squares, ends)
    relay(3)
    (own[4],) = pin(own[4])
    pass_own(4)
    mr[2], rest = pin(mr[2], rest)
    hand(2)
    total_squares = (squares, rest)
    near((2, 3), 0, 2, True)
    finish(0, 1)
    came_k, came_v, joined = pin(came_k, came_v, joined)
    beside_w = [move("core", w, swap[1]) for w in (joined, came_k, came_v)]
    near((4,), 0, 2, True)
    (mr[3],) = pin(mr[3])
    relay(4)
    (fw[2],) = pin(fw[2], cost=FAR)
    reached = (joined_k, joined_v, came_k, came_v, *beside_w)
    reach(3)
    near((2,), 2, 4, True)
    finish(2)
    reach(4)
    near((3, 4), 2, 4, False)
    finish(3)
    finish(4)
    return tuple(done)


def slot_ranks(dest_table, counts, per_row):
    slot_ids = jnp.arange(dest_table.shape[1], dtype=jnp.int32)
    is_valid = slot_ids[None, :] < counts[:, None]
    row_ids = jnp.where(is_valid, dest_table // per_row, -1)
    earlier = (
        (row_ids[:, :, None] == row_ids[:, None, :])
        & (slot_ids[None, None, :] < slot_ids[None, :, None])
        & is_valid[:, None, :]
    )
    return is_valid, row_ids, jnp.sum(earlier.astype(jnp.int32), axis=2)


def rotate_keys(key_raw, positions):
    rows, cols = key_raw.shape
    cosine, sine = rope_tables(positions)
    heads = key_raw.reshape(rows, cols // HD, HD)
    turned = heads * cosine[:, None, :] + jnp.roll(heads, HD // 2, axis=2) * sine[:, None, :]
    return turned.reshape(rows, cols)


def gathered(cached_rows, counts, dest_table, positions, norm_gain, key_weight, value_weight, key_bias, value_bias):
    stores = lax.axis_size("store")
    own_row = lax.axis_index("store")
    capacity = dest_table.shape[1]
    per_pair = capacity // stores
    per_row = positions.shape[0] // BLOCK
    width = cached_rows.shape[2]
    flat_slots = cached_rows.reshape(capacity, BLOCK * width)
    all_counts = lax.all_gather(counts, "store", axis=0, tiled=True)
    all_table = lax.all_gather(dest_table, "store", axis=0, tiled=True)
    is_valid, _, row_rank = slot_ranks(all_table, all_counts, per_row)
    target = own_row * per_row + jnp.arange(per_row, dtype=jnp.int32)
    own_valid, own_rows, own_rank = slot_ranks(dest_table, counts, per_row)
    pick = (
        own_valid[0][None, None, :]
        & (own_rows[0][None, None, :] == jnp.arange(stores, dtype=jnp.int32)[:, None, None])
        & (own_rank[0][None, None, :] == jnp.arange(per_pair, dtype=jnp.int32)[None, :, None])
    ).astype(jnp.bfloat16)
    outgoing = jnp.einsum("rkj,jf->rkf", pick, flat_slots, preferred_element_type=jnp.float32)
    arrived = lax.all_to_all(outgoing.astype(jnp.bfloat16), "store", split_axis=0, concat_axis=0, tiled=True)
    placing = (
        is_valid[None, :, :, None]
        & (all_table[None, :, :, None] == target[:, None, None, None])
        & (row_rank[None, :, :, None] == jnp.arange(per_pair, dtype=jnp.int32)[None, None, None, :])
    )
    placing = jnp.sum(placing.astype(jnp.int32), axis=2).astype(jnp.bfloat16)
    local = jnp.einsum("bsk,skf->bf", placing, arrived, preferred_element_type=jnp.float32)
    local = local.astype(jnp.bfloat16).reshape(per_row * BLOCK, width)
    rows = lax.all_gather(local, "tensor", axis=1, tiled=True).astype(jnp.float32)
    scale = lax.rsqrt(jnp.mean(rows * rows, axis=1) + EPS)
    normed = (rows * scale[:, None] * norm_gain[None, :]).astype(jnp.bfloat16)
    keys = jnp.dot(normed, key_weight, preferred_element_type=jnp.float32) + key_bias[None, :]
    values = jnp.dot(normed, value_weight, preferred_element_type=jnp.float32) + value_bias[None, :]
    return rotate_keys(keys, positions).astype(jnp.bfloat16), values.astype(jnp.bfloat16)


def solution(mesh):
    in_specs = (
        P(("groups", "store"), None, "tensor"),
        P(("groups", "store")),
        P(("groups", "store"), None),
        P(("groups", "store")),
        P(),
        P(None, "tensor"),
        P(None, "tensor"),
        P("tensor"),
        P("tensor"),
    )
    out_specs = (P(("groups", "store"), "tensor"), P(("groups", "store"), "tensor"))
    small = tuple(mesh.shape[axis] for axis in ("groups", "store", "tensor")) == (2, 4, 4)
    body = grouped if small else gathered
    return jax.shard_map(body, mesh=mesh, in_specs=in_specs, out_specs=out_specs, check_vma=False)
```

time: 506 us -> 332 us (0.66)
  waiting for transfers between devices: 287 us -> 120 us
  Pallas kernels: 0 us -> 149 us
  blocking collectives: 97.4 us -> 0 us
  matrix products: 66.1 us -> 0 us
  starting transfers between devices: 5.83 us -> 51.7 us
  local copies, waits for them, and re-layouts: 21.2 us -> 5.05 us
  between operations: 14.8 us -> 1.3 us
  other arithmetic: 13.3 us -> 3.31 us
    all_gather x1 -> x0, waiting for transfers between devices: 287 us -> none  [shards(): whole_rows = lax.all_gather(local_rows, 'tensor', axis=1, tiled=True)]
    pallas_call x0 -> x41, Pallas kernels: none -> 149 us  [__call__(): pl.pallas_call(body, out_shape=tuple(outs) + (TOKEN,), input_output_alias...]
    ppermute x0 -> x37, waiting for transfers between devices: none -> 120 us  [move(): return lax.ppermute(array, *way)]
    unnamed x1 -> x0, blocking collectives: 92.4 us -> none
    dot_general x4 -> x0, matrix products: 66.1 us -> none  [the longest x1 24 us: shards(): key_sum = jnp.dot(normed, key_weight, preferred_element_type=jnp.float32)]
    ppermute x0 -> x37, starting transfers between devices: none -> 51.7 us  [move(): return lax.ppermute(array, *way)]
    reshape x2 -> x0, local copies, waits for them, and re-layouts: 14 us -> none  [the longest x1 7.96 us: shards(): flat_slots = cached_rows.reshape(capacity, BLOCK * width_local)]
    reduce_sum x4 -> x0, other arithmetic: 8.28 us -> none  [the longest x1 7.51 us: shards(): inv_scale = lax.rsqrt(jnp.mean(whole_f32 * whole_f32, axis=1) + 1e-06)]
  transfers between devices with their start and end apart: 2 -> 37, of which waited for: 1 -> 13; matrix products, arithmetic and copies ran while one was open for 1% -> 2% of each run, Pallas kernels for 0% -> 41%
where the time goes in v1:
time: 332 us; the launch traced here: 330 us
  Pallas kernels  149 us (45%)
  waiting for transfers between devices  120 us (36%)
  starting transfers between devices  51.7 us (16%)
  local copies, waits for them, and re-layouts  5.05 us (2%)
    pallas_call x41, Pallas kernels, __call__(): pl.pallas_call(body, out_shape=tuple(outs) + (TOKEN,), input_output_alias...  149 us
    ppermute x37, waiting for transfers between devices, move(): return lax.ppermute(array, *way)  120 us
    ppermute x37, starting transfers between devices, move(): return lax.ppermute(array, *way)  51.7 us
  transfers between devices with their start and end apart: 37, of which 13 were waited for; matrix products, arithmetic and copies ran while one was open for 2% of the time, Pallas kernels for 41%

profile of v1, /device:TPU:0, one launch (start us, length us, event | category | flops | bytes accessed | tf_op | source)
XLA Modules:
  0.0 330.2 jit_solution(10734834105279033431)
XLA Ops:
  0.6 4.1 %send.2 = (bf16[64,2048]{1,0:T(8,128)(2,1)}, bf16[64,2048]{1,0:T(8,128)(2,1)}, bf16[512,2048]{1,0:T(8,128)(2,1)}, s32[8,128]{1,0:T(8,128)}) custom-call(s32[1,16]{1,0:T(1,128)} %refs_0_.7, bf16[2048,2048]{1,0:T(8,128)(2,1)} %bitcast.12), custom_call_target="tpu_custom_call" | custom-call | flops 4000000000 | bytes 1 | tf_op jit(solution)/shard_map/send/pallas_call | solution.py:68
  16.7 4.6 %send.3 = (bf16[64,2048]{1,0:T(8,128)(2,1)}, bf16[64,2048]{1,0:T(8,128)(2,1)}, bf16[128,2048]{1,0:T(8,128)(2,1)}, bf16[128,2048]{1,0:T(8,128)(2,1)}, bf16[512,2048]{1,0:T(8,128)(2,1)}, /*index=5*/s32[8,128]{1,0:T(8,128)}) custom-call(s32[1,16]{1,0:T(1,128)} %refs_0_.7, bf16[2048,2048]{1,0:T(8,128)(2,1)} %bitcast.13, s32[8,128]{1,0:T(8,128)} %get-tuple-element.114.refs_2_), custom_call_target="tpu_custom_call" | custom-call | flops 4000000000 | bytes 1 | tf_op jit(solution)/shard_map/send/pallas_call | solution.py:68
  30.7 4.6 %collective-permute-done.7.refs_4_.refs_7_.refs_8_.refs_9_ = bf16[64,2048]{1,0:T(8,128)(2,1)} collective-permute-done((bf16[64,2048]{1,0:T(8,128)(2,1)}, bf16[64,2048]{1,0:T(8,128)(2,1)}, u32[]{:S(2)}, u32[]{:S(2)}) %collective-permute-start.7) | collective-permute-done | bytes 262176 | tf_op jit(solution)/shard_map/a1/ppermute | solution.py:461
  49.1 3.9 %collective-permute-done.10.refs_1_.refs_4_ = bf16[128,2048]{1,0:T(8,128)(2,1)} collective-permute-done((bf16[128,2048]{1,0:T(8,128)(2,1)}, bf16[128,2048]{1,0:T(8,128)(2,1)}, u32[]{:S(2)}, u32[]{:S(2)}) %collective-permute-start.10) | collective-permute-done | bytes 524320 | tf_op jit(solution)/shard_map/ex1/ppermute | solution.py:461
  55.2 9.9 %collective-permute-done.9.refs_9_.refs_10_.refs_11_ = bf16[128,2048]{1,0:T(8,128)(2,1)} collective-permute-done((bf16[128,2048]{1,0:T(8,128)(2,1)}, bf16[128,2048]{1,0:T(8,128)(2,1)}, u32[]{:S(2)}, u32[]{:S(2)}) %collective-permute-start.9) | collective-permute-done | bytes 524320 | tf_op jit(solution)/shard_map/a2/ppermute | solution.py:461
  72.8 4.5 %collective-permute-start.13 = (bf16[256,2048]{1,0:T(8,128)(2,1)}, bf16[256,2048]{1,0:T(8,128)(2,1)}, u32[]{:S(2)}, u32[]{:S(2)}) collective-permute-start(bf16[256,2048]{1,0:T(8,128)(2,1)} %get-tuple-element.133.refs_0_.refs_1_), channel_id=1, source_target_pairs={{0,1},{1,0},{2,3},{3,2},{4,5},{5,4},{6,7},{7,6},{8,9},{9,8},{10,11... | collective-permute-start | bytes 3145736 | tf_op jit(solution)/shard_map/ex2/ppermute | solution.py:461
  77.9 12.2 %near.6 = (f32[256,2048]{1,0:T(8,128)}, s32[8,128]{1,0:T(8,128)}) custom-call(s32[8]{0:T(128)} %stack.39.refs_0_, bf16[128,2048]{1,0:T(8,128)(2,1)} %get-tuple-element.127.refs_0_.refs_1_, bf16[128,2048]{1,0:T(8,128)(2,1)} %collective-permute-done.11.refs_1_.refs_2_, bf16[128,2048]{1,0:T(8,128)(2,1)} %get-tuple-element.126.refs_0_.refs_3_, ...), custom_call_target="tpu_custom_call" | custom-call | flops 4000000000 | bytes 1 | tf_op jit(solution)/shard_map/near/pallas_call | solution.py:68
  90.1 7.1 %collective-permute-done.17.refs_2_ = bf16[1024,1024]{1,0:T(8,128)(2,1)} collective-permute-done((bf16[1024,1024]{1,0:T(8,128)(2,1)}, bf16[1024,1024]{1,0:T(8,128)(2,1)}, u32[]{:S(2)}, u32[]{:S(2)}) %collective-permute-start.17) | collective-permute-done | bytes 2097184 | tf_op jit(solution)/shard_map/in/ppermute | solution.py:461
  100.5 21.6 %collective-permute-done.13.refs_1_.refs_2_ = bf16[256,2048]{1,0:T(8,128)(2,1)} collective-permute-done((bf16[256,2048]{1,0:T(8,128)(2,1)}, bf16[256,2048]{1,0:T(8,128)(2,1)}, u32[]{:S(2)}, u32[]{:S(2)}) %collective-permute-start.13) | collective-permute-done | bytes 1048608 | tf_op jit(solution)/shard_map/ex2/ppermute | solution.py:461
  140.7 4.3 %collective-permute-start.19 = (bf16[256,2048]{1,0:T(8,128)(2,1)}, bf16[256,2048]{1,0:T(8,128)(2,1)}, u32[]{:S(2)}, u32[]{:S(2)}) collective-permute-start(bf16[256,2048]{1,0:T(8,128)(2,1)} %get-tuple-element.149.refs_0_.refs_3_), channel_id=1, source_target_pairs={{0,1},{1,0},{2,3},{3,2},{4,5},{5,4},{6,7},{7,6},{8,9},{9,8},{10,11... | collective-permute-start | bytes 3145736 | tf_op jit(solution)/shard_map/ex3/ppermute | solution.py:461
  148.3 8.9 %collective-permute-done.20.refs_0_ = bf16[256,2048]{1,0:T(8,128)(2,1)} collective-permute-done((bf16[256,2048]{1,0:T(8,128)(2,1)}, bf16[256,2048]{1,0:T(8,128)(2,1)}, u32[]{:S(2)}, u32[]{:S(2)}) %collective-permute-start.20) | collective-permute-done | bytes 1048608 | tf_op jit(solution)/shard_map/fw1/ppermute | solution.py:461
  159.8 7.8 %join.1 = (bf16[1024,1024]{1,0:T(8,128)(2,1)}, bf16[1024,1024]{1,0:T(8,128)(2,1)}, bf16[2048,1024]{1,0:T(8,128)(2,1)}, s32[8,128]{1,0:T(8,128)}) custom-call(s32[8]{0:T(128)} %stack.39.refs_0_, bf16[512,1024]{1,0:T(8,128)(2,1)} %get-tuple-element.161.refs_1_, bf16[512,1024]{1,0:T(8,128)(2,1)} %collective-permute-done.22.refs_2_, ...), custom_call_target="tpu_custom_call" | custom-call | flops 4000000000 | bytes 1 | tf_op jit(solution)/shard_map/join/pallas_call | solution.py:68
  168.9 12.3 %near.7 = (f32[256,2048]{1,0:T(8,128)}, s32[8,128]{1,0:T(8,128)}) custom-call(s32[8]{0:T(128)} %stack.39.refs_0_, bf16[256,2048]{1,0:T(8,128)(2,1)} %get-tuple-element.137.refs_1_, bf16[256,2048]{1,0:T(8,128)(2,1)} %get-tuple-element.159.refs_2_, bf16[256,2048]{1,0:T(8,128)(2,1)} %get-tuple-element.155.refs_3_, ...), custom_call_target="tpu_custom_call" | custom-call | flops 4000000000 | bytes 1 | tf_op jit(solution)/shard_map/near/pallas_call | solution.py:68
  195.4 16.5 %near.8 = (f32[512,2048]{1,0:T(8,128)}, s32[8,128]{1,0:T(8,128)}) custom-call(s32[8]{0:T(128)} %stack.39.refs_0_, bf16[256,2048]{1,0:T(8,128)(2,1)} %get-tuple-element.133.refs_0_.refs_1_, bf16[256,2048]{1,0:T(8,128)(2,1)} %collective-permute-done.13.refs_1_.refs_2_, bf16[256,2048]{1,0:T(8,128)(2,1)} %get-tuple-element.149.refs_0_.refs_3_, ...), custom_call_target="tpu_custom_call" | custom-call | flops 4000000000 | bytes 1 | tf_op jit(solution)/shard_map/near/pallas_call | solution.py:68
  212.0 4.5 %finish.4 = (bf16[1024,1024]{1,0:T(8,128)(2,1)}, bf16[1024,1024]{1,0:T(8,128)(2,1)}, s32[8,128]{1,0:T(8,128)}) custom-call(s32[8,4]{1,0:T(8,128)} %get-tuple-element.109.refs_0_, f32[256,2048]{1,0:T(8,128)} %get-tuple-element.172.refs_1_.refs_3_, f32[256,2048]{1,0:T(8,128)} %get-tuple-element.173.refs_2_.refs_4_, ...), custom_call_target="tpu_custom_call" | custom-call | flops 4000000000 | bytes 1 | tf_op jit(solution)/shard_map/finish/pallas_call | solution.py:68
  217.8 12.3 %near.9 = (f32[256,2048]{1,0:T(8,128)}, s32[8,128]{1,0:T(8,128)}) custom-call(s32[8]{0:T(128)} %stack.39.refs_0_, bf16[256,2048]{1,0:T(8,128)(2,1)} %get-tuple-element.168.refs_1_.refs_0_, bf16[256,2048]{1,0:T(8,128)(2,1)} %collective-permute-done.24.refs_2_.refs_1_, bf16[8192,1024]{1,0:T(8,128)(2,1)} %refs_3_.5, bf16[8192,1024]{1,0:T(8,128)(2,1)} %refs_4_.5, ...), custom_call_target="tpu_custom_call" | custom-call | flops 4000000000 | bytes 1 | tf_op jit(solution)/shard_map/near/pallas_call | solution.py:68
  234.9 24.3 %collective-permute-done.34.refs_0_ = bf16[512,2048]{1,0:T(8,128)(2,1)} collective-permute-done((bf16[512,2048]{1,0:T(8,128)(2,1)}, bf16[512,2048]{1,0:T(8,128)(2,1)}, u32[]{:S(2)}, u32[]{:S(2)}) %collective-permute-start.34) | collective-permute-done | bytes 2097184 | tf_op jit(solution)/shard_map/fw2/ppermute | solution.py:461
  262.3 12.2 %near.10 = (f32[256,2048]{1,0:T(8,128)}, s32[8,128]{1,0:T(8,128)}) custom-call(s32[8]{0:T(128)} %stack.39.refs_0_, bf16[512,2048]{1,0:T(8,128)(2,1)} %get-tuple-element.192.refs_1_, bf16[512,2048]{1,0:T(8,128)(2,1)} %get-tuple-element.194.refs_2_, bf16[8192,1024]{1,0:T(8,128)(2,1)} %refs_3_.5, bf16[8192,1024]{1,0:T(8,128)(2,1)} %refs_4_.5, ...), custom_call_target="tpu_custom_call" | custom-call | flops 4000000000 | bytes 1 | tf_op jit(solution)/shard_map/near/pallas_call | solution.py:68
  274.5 4.7 %finish.5 = (bf16[1024,1024]{1,0:T(8,128)(2,1)}, bf16[1024,1024]{1,0:T(8,128)(2,1)}, s32[8,128]{1,0:T(8,128)}) custom-call(s32[8,4]{1,0:T(8,128)} %get-tuple-element.109.refs_0_, f32[512,2048]{1,0:T(8,128)} %get-tuple-element.191.refs_1_, f32[256,2048]{1,0:T(8,128)} %get-tuple-element.197.refs_2_, ...), custom_call_target="tpu_custom_call", output_to_operand_aliasing={{0}: (9, {}), {1}: (10, {})} | custom-call | flops 4000000000 | bytes 1 | tf_op jit(solution)/shard_map/finish/pallas_call | solution.py:68
  282.6 5.6 %near.11 = (f32[512,2048]{1,0:T(8,128)}, s32[8,128]{1,0:T(8,128)}) custom-call(s32[8]{0:T(128)} %stack.39.refs_0_, bf16[512,2048]{1,0:T(8,128)(2,1)} %get-tuple-element.185.refs_1_, bf16[512,2048]{1,0:T(8,128)(2,1)} %collective-permute-done.30.refs_1_.refs_2_, bf16[8192,1024]{1,0:T(8,128)(2,1)} %refs_3_.5, bf16[8192,1024]{1,0:T(8,128)(2,1)} %refs_4_.5, ...), custom_call_target="tpu_custom_call" | custom-call | flops 4000000000 | bytes 1 | tf_op jit(solution)/shard_map/near/pallas_call | solution.py:68
  288.1 4.8 %collective-permute-done.36.refs_3_ = bf16[256,2048]{1,0:T(8,128)(2,1)} collective-permute-done((bf16[256,2048]{1,0:T(8,128)(2,1)}, bf16[256,2048]{1,0:T(8,128)(2,1)}, u32[]{:S(2)}, u32[]{:S(2)}) %collective-permute-start.36) | collective-permute-done | bytes 1048608 | tf_op jit(solution)/shard_map/far3/ppermute | solution.py:461
  292.9 5.0 %finish.6 = (bf16[1024,1024]{1,0:T(8,128)(2,1)}, bf16[1024,1024]{1,0:T(8,128)(2,1)}, s32[8,128]{1,0:T(8,128)}) custom-call(s32[8,4]{1,0:T(8,128)} %get-tuple-element.109.refs_0_, f32[512,2048]{1,0:T(8,128)} %get-tuple-element.191.refs_1_, f32[512,2048]{1,0:T(8,128)} %get-tuple-element.203.refs_2_, ...), custom_call_target="tpu_custom_call", output_to_operand_aliasing={{0}: (10, {}), {1}: (11, {})} | custom-call | flops 4000000000 | bytes 1 | tf_op jit(solution)/shard_map/finish/pallas_call | solution.py:68
  298.0 27.0 %collective-permute-done.35.refs_3_ = bf16[256,2048]{1,0:T(8,128)(2,1)} collective-permute-done((bf16[256,2048]{1,0:T(8,128)(2,1)}, bf16[256,2048]{1,0:T(8,128)(2,1)}, u32[]{:S(2)}, u32[]{:S(2)}) %collective-permute-start.35) | collective-permute-done | bytes 1048608 | tf_op jit(solution)/shard_map/far4/ppermute | solution.py:461
  324.9 5.1 %finish.7 = (bf16[1024,1024]{1,0:T(8,128)(2,1)}, bf16[1024,1024]{1,0:T(8,128)(2,1)}, s32[8,128]{1,0:T(8,128)}) custom-call(s32[8,4]{1,0:T(8,128)} %get-tuple-element.109.refs_0_, f32[256,2048]{1,0:T(8,128)} %get-tuple-element.182.refs_1_, f32[512,2048]{1,0:T(8,128)} %get-tuple-element.203.refs_2_, ...), custom_call_target="tpu_custom_call", output_to_operand_aliasing={{0}: (10, {}), {1}: (11, {})} | custom-call | flops 4000000000 | bytes 1 | tf_op jit(solution)/shard_map/finish/pallas_call | solution.py:68
  (119 shorter events, 101.1 us)
Async XLA Ops:
  40.7 24.4 %collective-permute-start.9 = (bf16[128,2048]{1,0:T(8,128)(2,1)}, bf16[128,2048]{1,0:T(8,128)(2,1)}, u32[]{:S(2)}, u32[]{:S(2)}) collective-permute-start(bf16[128,2048]{1,0:T(8,128)(2,1)} %get-tuple-element.124), channel_id=1, source_target_pairs={{0,12},{4,8},{8,4},{12,0},{1,13},{5,9},{9,5},{13,1},{2,14},{6,10},... | collective-permute-start | bytes 1572872 | tf_op jit(solution)/shard_map/a2/ppermute | solution.py:461
  41.5 55.7 %collective-permute-start.17 = (bf16[1024,1024]{1,0:T(8,128)(2,1)}, bf16[1024,1024]{1,0:T(8,128)(2,1)}, u32[]{:S(2)}, u32[]{:S(2)}) collective-permute-start(bf16[1024,1024]{1,0:T(8,128)(2,1)} %get-tuple-element.138), channel_id=1, source_target_pairs={{0,1},{3,2},{4,5},{7,6},{8,9},{11,10},{12,13},{15,14},{16,17},{19,... | collective-permute-start | bytes 6291464 | tf_op jit(solution)/shard_map/in/ppermute | solution.py:461
  47.4 24.1 %collective-permute-start.15 = (bf16[256,2048]{1,0:T(8,128)(2,1)}, bf16[256,2048]{1,0:T(8,128)(2,1)}, u32[]{:S(2)}, u32[]{:S(2)}) collective-permute-start(bf16[256,2048]{1,0:T(8,128)(2,1)} %get-tuple-element.135), channel_id=1, source_target_pairs={{1,2},{2,1},{5,6},{6,5},{9,10},{10,9},{13,14},{14,13},{17,18},{18,... | collective-permute-start | bytes 3145736 | tf_op jit(solution)/shard_map/mr0/ppermute | solution.py:461
  68.3 56.7 %collective-permute-start.12 = (bf16[512,2048]{1,0:T(8,128)(2,1)}, bf16[512,2048]{1,0:T(8,128)(2,1)}, u32[]{:S(2)}, u32[]{:S(2)}) collective-permute-start(bf16[512,2048]{1,0:T(8,128)(2,1)} %get-tuple-element.132), channel_id=1, source_target_pairs={{0,8},{4,12},{8,0},{12,4},{1,9},{5,13},{9,1},{13,5},{2,10},{6,14},... | collective-permute-start | bytes 6291464 | tf_op jit(solution)/shard_map/h3/ppermute | solution.py:461
  69.8 20.2 %collective-permute-start.14 = (bf16[256,2048]{1,0:T(8,128)(2,1)}, bf16[256,2048]{1,0:T(8,128)(2,1)}, u32[]{:S(2)}, u32[]{:S(2)}) collective-permute-start(bf16[256,2048]{1,0:T(8,128)(2,1)} %get-tuple-element.134), channel_id=1, source_target_pairs={{1,2},{2,1},{5,6},{6,5},{9,10},{10,9},{13,14},{14,13},{17,18},{18,... | collective-permute-start | bytes 3145736 | tf_op jit(solution)/shard_map/mr1/ppermute | solution.py:461
  71.5 29.0 %collective-permute-start.16 = (bf16[256,2048]{1,0:T(8,128)(2,1)}, bf16[256,2048]{1,0:T(8,128)(2,1)}, u32[]{:S(2)}, u32[]{:S(2)}) collective-permute-start(bf16[256,2048]{1,0:T(8,128)(2,1)} %get-tuple-element.137.refs_1_), channel_id=1, source_target_pairs={{1,0},{2,3},{5,4},{6,7},{9,8},{10,11},{13,12},{14,15},{17,16},{18,... | collective-permute-start | bytes 3145736 | tf_op jit(solution)/shard_map/fw0/ppermute | solution.py:461
  72.8 49.3 %collective-permute-start.13 = (bf16[256,2048]{1,0:T(8,128)(2,1)}, bf16[256,2048]{1,0:T(8,128)(2,1)}, u32[]{:S(2)}, u32[]{:S(2)}) collective-permute-start(bf16[256,2048]{1,0:T(8,128)(2,1)} %get-tuple-element.133.refs_0_.refs_1_), channel_id=1, source_target_pairs={{0,1},{1,0},{2,3},{3,2},{4,5},{5,4},{6,7},{7,6},{8,9},{9,8},{10,11... | collective-permute-start | bytes 3145736 | tf_op jit(solution)/shard_map/ex2/ppermute | solution.py:461
  129.0 28.2 %collective-permute-start.20 = (bf16[256,2048]{1,0:T(8,128)(2,1)}, bf16[256,2048]{1,0:T(8,128)(2,1)}, u32[]{:S(2)}, u32[]{:S(2)}) collective-permute-start(bf16[256,2048]{1,0:T(8,128)(2,1)} %get-tuple-element.155.refs_3_), channel_id=1, source_target_pairs={{1,0},{2,3},{5,4},{6,7},{9,8},{10,11},{13,12},{14,15},{17,16},{18,... | collective-permute-start | bytes 3145736 | tf_op jit(solution)/shard_map/fw1/ppermute | solution.py:461
  133.2 25.4 %collective-permute-start.22 = (bf16[512,1024]{1,0:T(8,128)(2,1)}, bf16[512,1024]{1,0:T(8,128)(2,1)}, u32[]{:S(2)}, u32[]{:S(2)}) collective-permute-start(bf16[512,1024]{1,0:T(8,128)(2,1)} %get-tuple-element.161.refs_1_), channel_id=1, source_target_pairs={{0,16},{16,0},{1,17},{17,1},{2,18},{18,2},{3,19},{19,3},{4,20},{20... | collective-permute-start | bytes 3145736 | tf_op jit(solution)/shard_map/wk1/ppermute | solution.py:461
  134.8 25.0 %collective-permute-start.23 = (bf16[512,1024]{1,0:T(8,128)(2,1)}, bf16[512,1024]{1,0:T(8,128)(2,1)}, u32[]{:S(2)}, u32[]{:S(2)}) collective-permute-start(bf16[512,1024]{1,0:T(8,128)(2,1)} %get-tuple-element.162.refs_3_), channel_id=1, source_target_pairs={{0,8},{4,12},{8,0},{12,4},{1,9},{5,13},{9,1},{13,5},{2,10},{6,14},... | collective-permute-start | bytes 3145736 | tf_op jit(solution)/shard_map/wv1/ppermute | solution.py:461
  135.4 54.1 %collective-permute-start.27 = (bf16[512,2048]{1,0:T(8,128)(2,1)}, bf16[512,2048]{1,0:T(8,128)(2,1)}, u32[]{:S(2)}, u32[]{:S(2)}) collective-permute-start(bf16[512,2048]{1,0:T(8,128)(2,1)} %get-tuple-element.175), channel_id=1, source_target_pairs={{1,2},{2,1},{5,6},{6,5},{9,10},{10,9},{13,14},{14,13},{17,18},{18,... | collective-permute-start | bytes 6291464 | tf_op jit(solution)/shard_map/mr2/ppermute | solution.py:461
  140.7 43.9 %collective-permute-start.19 = (bf16[256,2048]{1,0:T(8,128)(2,1)}, bf16[256,2048]{1,0:T(8,128)(2,1)}, u32[]{:S(2)}, u32[]{:S(2)}) collective-permute-start(bf16[256,2048]{1,0:T(8,128)(2,1)} %get-tuple-element.149.refs_0_.refs_3_), channel_id=1, source_target_pairs={{0,1},{1,0},{2,3},{3,2},{4,5},{5,4},{6,7},{7,6},{8,9},{9,8},{10,11... | collective-permute-start | bytes 3145736 | tf_op jit(solution)/shard_map/ex3/ppermute | solution.py:461
  158.5 22.7 %collective-permute-start.21 = (f32[16,128]{1,0:T(8,128)}, f32[16,128]{1,0:T(8,128)S(1)}, u32[]{:S(2)}, u32[]{:S(2)}) collective-permute-start(f32[16,128]{1,0:T(8,128)} %get-tuple-element.158.refs_0_), channel_id=1, source_target_pairs={{0,1},{1,0},{2,3},{3,2},{4,5},{5,4},{6,7},{7,6},{8,9},{9,8},{10,11... | collective-permute-start | bytes 24584 | tf_op jit(solution)/shard_map/half/ppermute | solution.py:461
  167.6 48.9 %collective-permute-start.25 = (bf16[1024,1024]{1,0:T(8,128)(2,1)}, bf16[1024,1024]{1,0:T(8,128)(2,1)}, u32[]{:S(2)}, u32[]{:S(2)}) collective-permute-start(bf16[1024,1024]{1,0:T(8,128)(2,1)} %get-tuple-element.169.refs_2_), channel_id=1, source_target_pairs={{0,8},{4,12},{8,0},{12,4},{1,9},{5,13},{9,1},{13,5},{2,10},{6,14},... | collective-permute-start | bytes 6291464 | tf_op jit(solution)/shard_map/wk2/ppermute | solution.py:461
  168.3 48.2 %collective-permute-start.26 = (bf16[1024,1024]{1,0:T(8,128)(2,1)}, bf16[1024,1024]{1,0:T(8,128)(2,1)}, u32[]{:S(2)}, u32[]{:S(2)}) collective-permute-start(bf16[1024,1024]{1,0:T(8,128)(2,1)} %get-tuple-element.170.refs_3_), channel_id=1, source_target_pairs={{0,16},{16,0},{1,17},{17,1},{2,18},{18,2},{3,19},{19,3},{4,20},{20... | collective-permute-start | bytes 6291464 | tf_op jit(solution)/shard_map/wv2/ppermute | solution.py:461
  187.5 42.5 %collective-permute-start.29 = (bf16[512,2048]{1,0:T(8,128)(2,1)}, bf16[512,2048]{1,0:T(8,128)(2,1)}, u32[]{:S(2)}, u32[]{:S(2)}) collective-permute-start(bf16[512,2048]{1,0:T(8,128)(2,1)} %get-tuple-element.183), channel_id=1, source_target_pairs={{1,2},{2,1},{5,6},{6,5},{9,10},{10,9},{13,14},{14,13},{17,18},{18,... | collective-permute-start | bytes 6291464 | tf_op jit(solution)/shard_map/mr3/ppermute | solution.py:461
  189.5 28.3 %collective-permute-start.24 = (bf16[256,2048]{1,0:T(8,128)(2,1)}, bf16[256,2048]{1,0:T(8,128)(2,1)}, u32[]{:S(2)}, u32[]{:S(2)}) collective-permute-start(bf16[256,2048]{1,0:T(8,128)(2,1)} %get-tuple-element.168.refs_1_.refs_0_), channel_id=1, source_target_pairs={{0,1},{1,0},{2,3},{3,2},{4,5},{5,4},{6,7},{7,6},{8,9},{9,8},{10,11... | collective-permute-start | bytes 3145736 | tf_op jit(solution)/shard_map/ex4/ppermute | solution.py:461
  194.0 65.3 %collective-permute-start.34 = (bf16[512,2048]{1,0:T(8,128)(2,1)}, bf16[512,2048]{1,0:T(8,128)(2,1)}, u32[]{:S(2)}, u32[]{:S(2)}) collective-permute-start(bf16[512,2048]{1,0:T(8,128)(2,1)} %get-tuple-element.192.refs_1_), channel_id=1, source_target_pairs={{1,0},{2,3},{5,4},{6,7},{9,8},{10,11},{13,12},{14,15},{17,16},{18,... | collective-permute-start | bytes 6291464 | tf_op jit(solution)/shard_map/fw2/ppermute | solution.py:461
  216.5 42.7 %collective-permute-start.31 = (bf16[2048,1024]{1,0:T(8,128)(2,1)}, bf16[2048,1024]{1,0:T(8,128)(2,1)}, u32[]{:S(2)}, u32[]{:S(2)}) collective-permute-start(bf16[2048,1024]{1,0:T(8,128)(2,1)} %get-tuple-element.190), channel_id=1, source_target_pairs={{0,4},{4,0},{8,12},{12,8},{1,5},{5,1},{9,13},{13,9},{2,6},{6,2},{1... | collective-permute-start | bytes 12582920 | tf_op jit(solution)/shard_map/core/ppermute | solution.py:461
  216.6 42.6 %collective-permute-start.32 = (bf16[1024,1024]{1,0:T(8,128)(2,1)}, bf16[1024,1024]{1,0:T(8,128)(2,1)}, u32[]{:S(2)}, u32[]{:S(2)}) collective-permute-start(bf16[1024,1024]{1,0:T(8,128)(2,1)} %get-tuple-element.188.refs_4_), channel_id=1, source_target_pairs={{0,4},{4,0},{8,12},{12,8},{1,5},{5,1},{9,13},{13,9},{2,6},{6,2},{1... | collective-permute-start | bytes 6291464 | tf_op jit(solution)/shard_map/core/ppermute | solution.py:461
  217.8 41.5 %collective-permute-start.33 = (bf16[1024,1024]{1,0:T(8,128)(2,1)}, bf16[1024,1024]{1,0:T(8,128)(2,1)}, u32[]{:S(2)}, u32[]{:S(2)}) collective-permute-start(bf16[1024,1024]{1,0:T(8,128)(2,1)} %get-tuple-element.189.refs_5_), channel_id=1, source_target_pairs={{0,4},{4,0},{8,12},{12,8},{1,5},{5,1},{9,13},{13,9},{2,6},{6,2},{1... | collective-permute-start | bytes 6291464 | tf_op jit(solution)/shard_map/core/ppermute | solution.py:461
  232.9 46.3 %collective-permute-start.30 = (bf16[512,2048]{1,0:T(8,128)(2,1)}, bf16[512,2048]{1,0:T(8,128)(2,1)}, u32[]{:S(2)}, u32[]{:S(2)}) collective-permute-start(bf16[512,2048]{1,0:T(8,128)(2,1)} %get-tuple-element.187), channel_id=1, source_target_pairs={{1,2},{2,1},{5,6},{6,5},{9,10},{10,9},{13,14},{14,13},{17,18},{18,... | collective-permute-start | bytes 6291464 | tf_op jit(solution)/shard_map/mr4/ppermute | solution.py:461
  261.0 31.9 %collective-permute-start.36 = (bf16[256,2048]{1,0:T(8,128)(2,1)}, bf16[256,2048]{1,0:T(8,128)(2,1)}, u32[]{:S(2)}, u32[]{:S(2)}) collective-permute-start(bf16[256,2048]{1,0:T(8,128)(2,1)} %get-tuple-element.205), channel_id=1, source_target_pairs={{1,0},{2,3},{5,4},{6,7},{9,8},{10,11},{13,12},{14,15},{17,16},{18,... | collective-permute-start | bytes 3145736 | tf_op jit(solution)/shard_map/far3/ppermute | solution.py:461
  281.3 43.7 %collective-permute-start.35 = (bf16[256,2048]{1,0:T(8,128)(2,1)}, bf16[256,2048]{1,0:T(8,128)(2,1)}, u32[]{:S(2)}, u32[]{:S(2)}) collective-permute-start(bf16[256,2048]{1,0:T(8,128)(2,1)} %get-tuple-element.204), channel_id=1, source_target_pairs={{1,0},{2,3},{5,4},{6,7},{9,8},{10,11},{13,12},{14,15},{17,16},{18,... | collective-permute-start | bytes 3145736 | tf_op jit(solution)/shard_map/far4/ppermute | solution.py:461
  (24 other events, 177.9 us)

commit v2 on v1

--- a/solution.py
+++ b/solution.py
@@ -133,14 +133,30 @@
         c.wait()
 
 
-def cut_kernel(key_weight, value_weight, out, sems):
+def pack_kernel(per_row, table, cached, passed, *refs):
+    outs, sems = refs[:-1], refs[-1]
+    start, _ = in_row(table, (lax.axis_index("store") ^ 2) * per_row, per_row)
+    copies = []
+    for i, out in enumerate(outs):
+        src = pl.multiple_of(jnp.minimum(start + i + 1, table.shape[1] - 1) * BLOCK, 16)
+        copies.append(pltpu.make_async_copy(cached.at[pl.ds(src, BLOCK)], out.at[pl.ds(0, BLOCK)], sems.at[i, 0]))
+        here = passed.at[pl.ds(i * BLOCK, BLOCK)]
+        copies.append(pltpu.make_async_copy(here, out.at[pl.ds(BLOCK, BLOCK)], sems.at[i, 1]))
+    for c in copies:
+        c.start()
+    for c in copies:
+        c.wait()
+
+
+def cut_kernel(key_weight, value_weight, *refs):
+    outs, sems = refs[:-1], refs[-1]
     z, y, own_row = lax.axis_index("tensor"), lax.axis_index("groups"), lax.axis_index("store")
-    share = out.shape[0] // 2
+    share = outs[0].shape[0]
     slab = jnp.where(z == 0, 2 + y, 1 - y)
     at = pl.multiple_of((slab * 4 + own_row) * share, 128)
     copies = [
-        pltpu.make_async_copy(weight.at[pl.ds(at, share)], out.at[pl.ds(g * share, share)], sems.at[g])
-        for g, weight in enumerate((key_weight, value_weight))
+        pltpu.make_async_copy(weight.at[pl.ds(at, share)], out, sems.at[g])
+        for g, (weight, out) in enumerate(zip((key_weight, value_weight), outs))
     ]
     for c in copies:
         c.start()
@@ -148,29 +164,18 @@
         c.wait()
 
 
-def split_kernel(both, keys, values, sems):
-    share = keys.shape[0]
-    copies = [
-        pltpu.make_async_copy(both.at[pl.ds(g * share, share)], out, sems.at[g])
-        for g, out in enumerate((keys, values))
-    ]
-    for c in copies:
-        c.start()
-    for c in copies:
-        c.wait()
-
-
-def join_kernel(info, *refs):
-    all_out, sems = refs[6], refs[7]
+def join_kernel(axis, info, here, came, *refs):
+    before, outs, sems = refs[:axis], refs[axis:-1], refs[-1]
+    share = here.shape[0]
+    place = info[5 + axis]
     copies = []
-    for g, out in enumerate(refs[4:6]):
-        share = out.shape[0] // 2
-        place = info[5 + g]
-        for t, src in enumerate(refs[2 * g : 2 * g + 2]):
-            at = pl.multiple_of((place if t == 0 else 1 - place) * share, 128)
-            copies.append(pltpu.make_async_copy(src, out.at[pl.ds(at, share)], sems.at[0, g, t]))
-            there = all_out.at[pl.ds(at + 2 * g * share, share)]
-            copies.append(pltpu.make_async_copy(src, there, sems.at[1, g, t]))
+    for t, src in enumerate((here, came)):
+        at = pl.multiple_of((place if t == 0 else 1 - place) * share, 128)
+        copies.append(pltpu.make_async_copy(src, outs[0].at[pl.ds(at, share)], sems.at[0, t]))
+        if axis == 1:
+            copies.append(pltpu.make_async_copy(src, outs[1].at[pl.ds(at + 2 * share, share)], sems.at[1, t]))
+    if axis == 1:
+        copies.append(pltpu.make_async_copy(before[0], outs[1].at[pl.ds(0, 2 * share)], sems.at[2, 0]))
     for c in copies:
         c.start()
     for c in copies:
@@ -181,6 +186,7 @@
     arrived = refs[: len(pieces)]
     gain, y_out, ssq_out, held, sems = refs[len(pieces) :]
     width = held.shape[2]
+    z = lax.axis_index("tensor")
     for j in range(2):
         code = plan[first + j, 0]
 
@@ -203,7 +209,8 @@
         sums = jnp.zeros((rows, 128), jnp.float32)
         for c in range(0, width, 128):
             x = held[j, :, c : c + 128].astype(jnp.float32)
-            y_out[j * rows : (j + 1) * rows, c : c + 128] = (x * gain[:, c : c + 128]).astype(jnp.bfloat16)
+            here = gain[:, pl.ds(pl.multiple_of(z * width + c, 128), 128)]
+            y_out[j * rows : (j + 1) * rows, c : c + 128] = (x * here).astype(jnp.bfloat16)
             sums += x * x
         ssq_out[j : j + 1, :rows] = jnp.sum(sums.T, axis=0, keepdims=True)
 
@@ -433,7 +440,7 @@
     cached = cached_rows[0]
     width = cached.shape[1]
     whole, cols = key_weight.shape
-    part, share = width // 2, whole // 16
+    share = whole // 16
     dma = pltpu.SemaphoreType.DMA
     bf16 = functools.partial(jax.ShapeDtypeStruct, dtype=jnp.bfloat16)
     f32 = functools.partial(jax.ShapeDtypeStruct, dtype=jnp.float32)
@@ -449,8 +456,7 @@
     other = [jnp.where(inner, 3 - z, z ^ 2), jnp.where(inner, (3 - z) ^ 1, 3 - z)]
     chip, core = lax.axis_index("store") // 2, lax.rem(lax.axis_index("store"), 2)
     info = jnp.stack([z, z ^ 1, *other, inner.astype(jnp.int32), y, chip, core]).astype(jnp.int32)
-    gain = lax.dynamic_slice_in_dim(norm_gain, z * width, width, 0)[None, :]
-    cosine, sine = rope_tables(positions)
+    gain = norm_gain[None, :]
 
     call = Chain()
     came, own, ssq, ex, mr, fw, accs, far = {}, {}, {}, {}, {}, {}, {}, {}
@@ -472,7 +478,7 @@
             [dma((sum(len(p) for p in parts),))],
         )
 
-    def prep(c):
+    def prep(c, cost=COST):
         k, low, rows = CHUNKS[c]
         pieces, arrays = [], []
         for r in range(k + 1):
@@ -492,6 +498,7 @@
             [bf16((2 * rows, width)), f32((2, BLOCK))],
             [VMEM, VMEM],
             [pltpu.VMEM((2, rows, width), jnp.bfloat16), dma((2,))],
+            cost=cost,
         )
 
     def pass_own(c):
@@ -531,7 +538,7 @@
             functools.partial(near_kernel, sizes, first, handed),
             "near",
             (info, *slabs, key_weight, value_weight),
-            [HBM] * len(slabs) + [pl.BlockSpec((part, cols), weights)] * 2,
+            [HBM] * len(slabs) + [pl.BlockSpec((width // 2, cols), weights)] * 2,
             [f32((total, 2 * cols))],
             [pl.BlockSpec((total, 2 * cols), lambda i, info: (0, 0))],
             [pltpu.VMEM((last - first, total, width), jnp.bfloat16), dma((last - first, len(sizes)))],
@@ -600,8 +607,8 @@
         came[i] = {m: (move("a%d" % i, array, swap[m]), 0) for m, array in zip((2, 3), sent)}
 
     tables = [move("table", dest_table, swap[m]) for m in range(1, stores)]
-    *s0, bulk = send(*both_ways(0), [(k * BLOCK, 1, (k, 0, BLOCK)) for k in range(most)])
-    exchange(0, s0)
+    exchange(0, send(*both_ways(0)))
+    (bulk,) = send([(k * BLOCK, 1, (k, 0, BLOCK)) for k in range(most)])
     beside = move("beside", bulk, swap[1])
     (plan,) = call(
         functools.partial(plan_kernel, stores, per_row),
@@ -611,79 +618,99 @@
         [jax.ShapeDtypeStruct((per_row, 4), jnp.int32)],
         [SMEM],
     )
-    (lent,) = call(
-        cut_kernel, "cut", (key_weight, value_weight), [HBM] * 2, [bf16((2 * share, cols))], [VMEM], [dma((2,))]
+    def join(axis, here, hopped, *before):
+        return call(
+            functools.partial(join_kernel, axis),
+            "join",
+            (info, here, hopped, *before),
+            [SMEM] + [HBM] * (2 + axis),
+            [bf16((2 * share, cols)), bf16((4 * share, cols))][: 1 + axis],
+            [VMEM] * (1 + axis),
+            [dma((3, 2))],
+        )
+
+    onward = [((k - 1) * BLOCK, 3, (k, 0, BLOCK)) for k in range(1, most)]
+    *s1, passed = send(*both_ways(1), onward)
+    exchange(1, s1)
+    passed = move("pass", passed, swap[1])
+    prep(0, FAR)
+    pass_own(0)
+    packs = call(
+        functools.partial(pack_kernel, per_row),
+        "pack",
+        (dest_table, cached, passed),
+        [SMEM, HBM, HBM],
+        [bf16((2 * BLOCK, width))] * 3,
+        [VMEM] * 3,
+        [dma((3, 2))],
     )
-    both = [[(m % 2 * 2 * BLOCK + t * BLOCK, m, STEPS[3 + t]) for m in (2, 3) for t in range(2)]]
-    *s1, s2a, s2b, s3 = send(*both_ways(1), *both_ways(2), *both)
-    exchange(1, s1)
-    prep(0)
-    pass_own(0)
+
+    cuts = call(
+        cut_kernel, "cut", (key_weight, value_weight), [HBM] * 2, [bf16((share, cols))] * 2, [VMEM] * 2, [dma((2,))]
+    )
+
+    def hop(k, pack):
+        hopped = move("h%d" % k, pack, swap[2])
+        came[k + 1] = {2: (hopped, 0), 3: (hopped, BLOCK)}
+
     prep(1)
     pass_own(1)
-    s2a, s2b, lent = pin(s2a, s2b, lent)
-    exchange(2, (s2a, s2b))
-    lent = move("in", lent, inward)
+    pack, lent_k = pin(packs[0], cuts[0])
+    hop(1, pack)
+    lent_k = move("ink", lent_k, inward)
     relay(0)
     relay(1)
     prep(2)
     pass_own(2)
-    (s3,) = pin(s3)
-    late = move("h3", s3, swap[2])
-    (mr[0],) = pin(mr[0])
+    (pack,) = pin(packs[1])
+    hop(2, pack)
+    (positions,) = pin(positions)
+    cosine, sine = pin(*rope_tables(positions))
+    mr[0], lent_k, lent_v = pin(mr[0], lent_k, cuts[1])
     hand(0)
+    lent_v = move("inv", lent_v, inward)
     near((0, 1), 0, 2, True)
-    mr[1], fw[0], lent = pin(mr[1], fw[0], lent)
-    hand(1)
     relay(2)
-    (late,) = pin(late)
-    turned = move("c3", late, swap[1])
-    for t in range(2):
-        came[3 + t] = {2: (late, t * BLOCK), 3: (turned, 2 * BLOCK + t * BLOCK)}
-    lent_k, lent_v = call(
-        split_kernel, "split", (lent,), [HBM], [bf16((share, cols))] * 2, [VMEM] * 2, [dma((2,))]
-    )
-    came_k, came_v = move("wk1", lent_k, across), move("wv1", lent_v, swap[2])
     prep(3)
     pass_own(3)
+    mr[1], pack = pin(mr[1], packs[2])
+    hop(3, pack)
+    fw[0], lent_v, lent_k, mr[1] = pin(fw[0], lent_v, lent_k, mr[1])
+    hand(1)
+    came_k = move("wk1", lent_k, across)
+    (lent_v,) = pin(lent_v)
+    came_v = move("wv1", lent_v, swap[2])
+    near((2,), 0, 2, True)
+    relay(3)
+    (mr[2],) = pin(mr[2])
     prep(4)
-    (fw[1],) = pin(fw[1])
     squares = sums(0, *(ssq[c] for c in range(len(CHUNKS))))
     paired = move("half", squares, pair)
-    joined_k, joined_v, joined = call(
-        join_kernel,
-        "join",
-        (info, lent_k, came_k, lent_v, came_v),
-        [SMEM] + [HBM] * 4,
-        [bf16((2 * share, cols))] * 2 + [bf16((4 * share, cols))],
-        [VMEM] * 3,
-        [dma((2, 2, 2))],
-    )
-    came_k, came_v = move("wk2", joined_k, swap[2]), move("wv2", joined_v, across)
-    near((0, 1), 2, 4, True)
+    fw[1], own[4] = pin(fw[1], own[4])
+    pass_own(4)
+    (joined_k,) = join(0, lent_k, came_k)
+    came_k = move("wk2", joined_k, swap[2])
+    joined_v, joined = join(1, lent_v, came_v, joined_k)
+    came_v = move("wv2", joined_v, across)
+    mr[2], paired = pin(mr[2], paired)
+    hand(2)
+    near((3, 4), 0, 2, True)
+    (mr[3],) = pin(mr[3])
     squares = sums(1, squares, paired)
     rest = move("rest", squares, ends)
-    relay(3)
-    (own[4],) = pin(own[4])
-    pass_own(4)
-    mr[2], rest = pin(mr[2], rest)
-    hand(2)
-    total_squares = (squares, rest)
-    near((2, 3), 0, 2, True)
-    finish(0, 1)
+    relay(4)
+    near((0, 1), 2, 4, True)
     came_k, came_v, joined = pin(came_k, came_v, joined)
     beside_w = [move("core", w, swap[1]) for w in (joined, came_k, came_v)]
-    near((4,), 0, 2, True)
-    (mr[3],) = pin(mr[3])
-    relay(4)
+    total_squares = (squares, rest)
+    finish(0, 1)
     (fw[2],) = pin(fw[2], cost=FAR)
     reached = (joined_k, joined_v, came_k, came_v, *beside_w)
     reach(3)
     near((2,), 2, 4, True)
-    finish(2)
     reach(4)
     near((3, 4), 2, 4, False)
-    finish(3)
+    finish(2, 3)
     finish(4)
     return tuple(done)
 

time: 332 us -> 312 us (0.940)
  waiting for transfers between devices: 120 us -> 84.9 us
  starting transfers between devices: 51.7 us -> 64.4 us
    ppermute x37 -> x38, waiting for transfers between devices: 120 us -> 84.9 us  [move(): return lax.ppermute(array, *way)]
    ppermute x37 -> x38, starting transfers between devices: 51.7 us -> 64.4 us  [move(): return lax.ppermute(array, *way)]
    pallas_call x41 -> x45, Pallas kernels: 149 us -> 151 us  [__call__(): pl.pallas_call(body, out_shape=tuple(outs) + (TOKEN,), input_output_alias...]
  transfers between devices with their start and end apart: 37 -> 38, of which waited for: 13 -> 15; matrix products, arithmetic and copies ran while one was open for 2% -> 1% of each run, Pallas kernels for 41% -> 44%
where the time goes in v2:
time: 312 us; the launch traced here: 310 us
  Pallas kernels  151 us (48%)
  waiting for transfers between devices  84.9 us (27%)
  starting transfers between devices  64.4 us (21%)
  local copies, waits for them, and re-layouts  4.94 us (2%)
  other arithmetic  3.94 us (1%)
    pallas_call x45, Pallas kernels, __call__(): pl.pallas_call(body, out_shape=tuple(outs) + (TOKEN,), input_output_alias...  151 us
    ppermute x38, waiting for transfers between devices, move(): return lax.ppermute(array, *way)  84.9 us
    ppermute x38, starting transfers between devices, move(): return lax.ppermute(array, *way)  64.4 us
  transfers between devices with their start and end apart: 38, of which 15 were waited for; matrix products, arithmetic and copies ran while one was open for 1% of the time, Pallas kernels for 44%

profile of v2, /device:TPU:0, one launch (start us, length us, event | category | flops | bytes accessed | tf_op | source)
XLA Modules:
  0.0 310.3 jit_solution(7337136935406051891)
XLA Ops:
  4.5 3.7 %send.4 = (bf16[512,2048]{1,0:T(8,128)(2,1)}, s32[8,128]{1,0:T(8,128)}) custom-call(s32[1,16]{1,0:T(1,128)} %refs_0_.11, bf16[2048,2048]{1,0:T(8,128)(2,1)} %bitcast.13, s32[8,128]{1,0:T(8,128)} %get-tuple-element.118.refs_2_), custom_call_target="tpu_custom_call" | custom-call | flops 4000000000 | bytes 1 | tf_op jit(solution)/shard_map/send/pallas_call | solution.py:68
  31.3 4.3 %pack.1 = (bf16[256,2048]{1,0:T(8,128)(2,1)}, bf16[256,2048]{1,0:T(8,128)(2,1)}, bf16[256,2048]{1,0:T(8,128)(2,1)}, s32[8,128]{1,0:T(8,128)}) custom-call(s32[1,16]{1,0:T(1,128)} %refs_0_.11, bf16[2048,2048]{1,0:T(8,128)(2,1)} %bitcast.16, bf16[384,2048]{1,0:T(8,128)(2,1)} %collective-permute-done.8.refs_2_, s32[8,128]{1,0:T(8,128)} %get-tuple-element.129.refs_3_), custom_call_target="tpu_custom_call" | custom-call | flops 4000000000 | bytes 1 | tf_op jit(solution)/shard_map/pack/pallas_call | solution.py:68
  44.7 4.5 %collective-permute-start.15 = (bf16[512,1024]{1,0:T(8,128)(2,1)}, bf16[512,1024]{1,0:T(8,128)(2,1)}, u32[]{:S(2)}, u32[]{:S(2)}) collective-permute-start(bf16[512,1024]{1,0:T(8,128)(2,1)} %get-tuple-element.146), channel_id=1, source_target_pairs={{0,1},{3,2},{4,5},{7,6},{8,9},{11,10},{12,13},{15,14},{16,17},{19,... | collective-permute-start | bytes 3145736 | tf_op jit(solution)/shard_map/ink/ppermute | solution.py:467
  53.1 4.3 %collective-permute-done.10.refs_1_.refs_4_ = bf16[128,2048]{1,0:T(8,128)(2,1)} collective-permute-done((bf16[128,2048]{1,0:T(8,128)(2,1)S(1)}, bf16[128,2048]{1,0:T(8,128)(2,1)}, u32[]{:S(2)}, u32[]{:S(2)}) %collective-permute-start.10) | collective-permute-done | bytes 524320 | tf_op jit(solution)/shard_map/ex1/ppermute | solution.py:467
  61.3 6.3 %collective-permute-done.9.refs_8_.refs_9_.refs_10_.refs_11_ = bf16[256,2048]{1,0:T(8,128)(2,1)} collective-permute-done((bf16[256,2048]{1,0:T(8,128)(2,1)}, bf16[256,2048]{1,0:T(8,128)(2,1)}, u32[]{:S(2)}, u32[]{:S(2)}) %collective-permute-start.9) | collective-permute-done | bytes 1048608 | tf_op jit(solution)/shard_map/h1/ppermute | solution.py:467
  80.4 6.5 %collective-permute-start.18 = (bf16[512,1024]{1,0:T(8,128)(2,1)}, bf16[512,1024]{1,0:T(8,128)(2,1)}, u32[]{:S(2)}, u32[]{:S(2)}) collective-permute-start(bf16[512,1024]{1,0:T(8,128)(2,1)} %get-tuple-element.157), channel_id=1, source_target_pairs={{0,1},{3,2},{4,5},{7,6},{8,9},{11,10},{12,13},{15,14},{16,17},{19,... | collective-permute-start | bytes 3145736 | tf_op jit(solution)/shard_map/inv/ppermute | solution.py:467
  86.9 12.2 %near.6 = (f32[256,2048]{1,0:T(8,128)}, s32[8,128]{1,0:T(8,128)}) custom-call(s32[8]{0:T(128)} %stack.39.refs_0_, bf16[128,2048]{1,0:T(8,128)(2,1)} %get-tuple-element.138.refs_0_.refs_1_, bf16[128,2048]{1,0:T(8,128)(2,1)} %collective-permute-done.11.refs_1_.refs_2_, bf16[128,2048]{1,0:T(8,128)(2,1)} %get-tuple-element.137.refs_0_.refs_3_, ...), custom_call_target="tpu_custom_call" | custom-call | flops 4000000000 | bytes 1 | tf_op jit(solution)/shard_map/near/pallas_call | solution.py:68
  109.9 5.2 %collective-permute-start.16 = (bf16[256,2048]{1,0:T(8,128)(2,1)}, bf16[256,2048]{1,0:T(8,128)(2,1)}, u32[]{:S(2)}, u32[]{:S(2)}) collective-permute-start(bf16[256,2048]{1,0:T(8,128)(2,1)} %get-tuple-element.155.refs_0_.refs_1_), channel_id=1, source_target_pairs={{0,1},{1,0},{2,3},{3,2},{4,5},{5,4},{6,7},{7,6},{8,9},{9,8},{10,11... | collective-permute-start | bytes 3145736 | tf_op jit(solution)/shard_map/ex3/ppermute | solution.py:467
  116.0 4.5 %collective-permute-done.17.refs_0_ = bf16[256,2048]{1,0:T(8,128)(2,1)} collective-permute-done((bf16[256,2048]{1,0:T(8,128)(2,1)}, bf16[256,2048]{1,0:T(8,128)(2,1)}, u32[]{:S(2)}, u32[]{:S(2)}) %collective-permute-start.17) | collective-permute-done | bytes 1048608 | tf_op jit(solution)/shard_map/fw0/ppermute | solution.py:467
  126.9 12.2 %near.7 = (f32[256,2048]{1,0:T(8,128)}, s32[8,128]{1,0:T(8,128)}) custom-call(s32[8]{0:T(128)} %stack.39.refs_0_, bf16[256,2048]{1,0:T(8,128)(2,1)} %get-tuple-element.144.refs_0_.refs_1_, bf16[256,2048]{1,0:T(8,128)(2,1)} %collective-permute-done.13.refs_1_.refs_2_, bf16[8192,1024]{1,0:T(8,128)(2,1)} %refs_3_.5, bf16[8192,1024]{1,0:T(8,128)(2,1)} %refs_4_.5, ...), custom_call_target="tpu_custom_call" | custom-call | flops 4000000000 | bytes 1 | tf_op jit(solution)/shard_map/near/pallas_call | solution.py:68
  139.1 6.2 %collective-permute-done.16.refs_1_.refs_2_ = bf16[256,2048]{1,0:T(8,128)(2,1)} collective-permute-done((bf16[256,2048]{1,0:T(8,128)(2,1)}, bf16[256,2048]{1,0:T(8,128)(2,1)}, u32[]{:S(2)}, u32[]{:S(2)}) %collective-permute-start.16) | collective-permute-done | bytes 1048608 | tf_op jit(solution)/shard_map/ex3/ppermute | solution.py:467
  156.0 7.6 %collective-permute-start.24 = (f32[16,128]{1,0:T(8,128)}, f32[16,128]{1,0:T(8,128)S(1)}, u32[]{:S(2)}, u32[]{:S(2)}) collective-permute-start(f32[16,128]{1,0:T(8,128)} %get-tuple-element.183.refs_0_), channel_id=1, source_target_pairs={{0,1},{1,0},{2,3},{3,2},{4,5},{5,4},{6,7},{7,6},{8,9},{9,8},{10,11... | collective-permute-start | bytes 24584 | tf_op jit(solution)/shard_map/half/ppermute | solution.py:467
  170.6 6.3 %join.3 = (bf16[1024,1024]{1,0:T(8,128)(2,1)}, bf16[2048,1024]{1,0:T(8,128)(2,1)}, s32[8,128]{1,0:T(8,128)}) custom-call(s32[8]{0:T(128)} %stack.39.refs_0_, bf16[512,1024]{1,0:T(8,128)(2,1)} %get-tuple-element.184.refs_1_, bf16[512,1024]{1,0:T(8,128)(2,1)} %collective-permute-done.25.refs_2_, bf16[1024,1024]{1,0:T(8,128)(2,1)} %get-tuple-element.187.refs_3_.refs_2_, ...), custom_call_target="tpu_custom_call" | custom-call | flops 4000000000 | bytes 1 | tf_op jit(solution)/shard_map/join/pallas_call | solution.py:68
  180.6 9.6 %collective-permute-done.23.refs_4_.refs_1_ = bf16[256,2048]{1,0:T(8,128)(2,1)} collective-permute-done((bf16[256,2048]{1,0:T(8,128)(2,1)}, bf16[256,2048]{1,0:T(8,128)(2,1)}, u32[]{:S(2)}, u32[]{:S(2)}) %collective-permute-start.23) | collective-permute-done | bytes 1048608 | tf_op jit(solution)/shard_map/ex4/ppermute | solution.py:467
  190.1 16.5 %near.8 = (f32[512,2048]{1,0:T(8,128)}, s32[8,128]{1,0:T(8,128)}) custom-call(s32[8]{0:T(128)} %stack.39.refs_0_, bf16[256,2048]{1,0:T(8,128)(2,1)} %get-tuple-element.155.refs_0_.refs_1_, bf16[256,2048]{1,0:T(8,128)(2,1)} %collective-permute-done.16.refs_1_.refs_2_, bf16[256,2048]{1,0:T(8,128)(2,1)} %get-tuple-element.181.refs_3_.refs_0_, ...), custom_call_target="tpu_custom_call" | custom-call | flops 4000000000 | bytes 1 | tf_op jit(solution)/shard_map/near/pallas_call | solution.py:68
  215.4 12.2 %near.9 = (f32[256,2048]{1,0:T(8,128)}, s32[8,128]{1,0:T(8,128)}) custom-call(s32[8]{0:T(128)} %stack.39.refs_0_, bf16[256,2048]{1,0:T(8,128)(2,1)} %get-tuple-element.156.refs_1_, bf16[256,2048]{1,0:T(8,128)(2,1)} %get-tuple-element.201.refs_2_, bf16[256,2048]{1,0:T(8,128)(2,1)} %get-tuple-element.164.refs_3_, ...), custom_call_target="tpu_custom_call" | custom-call | flops 4000000000 | bytes 1 | tf_op jit(solution)/shard_map/near/pallas_call | solution.py:68
  228.8 4.5 %finish.3 = (bf16[1024,1024]{1,0:T(8,128)(2,1)}, bf16[1024,1024]{1,0:T(8,128)(2,1)}, s32[8,128]{1,0:T(8,128)}) custom-call(s32[8,4]{1,0:T(8,128)} %get-tuple-element.120.refs_0_, f32[256,2048]{1,0:T(8,128)} %get-tuple-element.209.refs_1_.refs_3_, f32[256,2048]{1,0:T(8,128)} %get-tuple-element.210.refs_2_.refs_4_, ...), custom_call_target="tpu_custom_call" | custom-call | flops 4000000000 | bytes 1 | tf_op jit(solution)/shard_map/finish/pallas_call | solution.py:68
  233.3 4.8 %collective-permute-done.32.refs_7_ = bf16[1024,1024]{1,0:T(8,128)(2,1)} collective-permute-done((bf16[1024,1024]{1,0:T(8,128)(2,1)}, bf16[1024,1024]{1,0:T(8,128)(2,1)}, u32[]{:S(2)}, u32[]{:S(2)}) %collective-permute-start.32) | collective-permute-done | bytes 2097184 | tf_op jit(solution)/shard_map/core/ppermute | solution.py:467
  244.2 12.2 %near.10 = (f32[256,2048]{1,0:T(8,128)}, s32[8,128]{1,0:T(8,128)}) custom-call(s32[8]{0:T(128)} %stack.39.refs_0_, bf16[512,2048]{1,0:T(8,128)(2,1)} %get-tuple-element.208.refs_1_, bf16[512,2048]{1,0:T(8,128)(2,1)} %get-tuple-element.216.refs_2_, bf16[8192,1024]{1,0:T(8,128)(2,1)} %refs_3_.5, bf16[8192,1024]{1,0:T(8,128)(2,1)} %refs_4_.5, ...), custom_call_target="tpu_custom_call" | custom-call | flops 4000000000 | bytes 1 | tf_op jit(solution)/shard_map/near/pallas_call | solution.py:68
  259.7 5.5 %near.11 = (f32[512,2048]{1,0:T(8,128)}, s32[8,128]{1,0:T(8,128)}) custom-call(s32[8]{0:T(128)} %stack.39.refs_0_, bf16[512,2048]{1,0:T(8,128)(2,1)} %get-tuple-element.194.refs_1_, bf16[512,2048]{1,0:T(8,128)(2,1)} %collective-permute-done.28.refs_1_.refs_2_, bf16[8192,1024]{1,0:T(8,128)(2,1)} %refs_3_.5, bf16[8192,1024]{1,0:T(8,128)(2,1)} %refs_4_.5, ...), custom_call_target="tpu_custom_call" | custom-call | flops 4000000000 | bytes 1 | tf_op jit(solution)/shard_map/near/pallas_call | solution.py:68
  265.3 12.4 %collective-permute-done.37.refs_5_ = bf16[256,2048]{1,0:T(8,128)(2,1)} collective-permute-done((bf16[256,2048]{1,0:T(8,128)(2,1)}, bf16[256,2048]{1,0:T(8,128)(2,1)}, u32[]{:S(2)}, u32[]{:S(2)}) %collective-permute-start.37) | collective-permute-done | bytes 1048608 | tf_op jit(solution)/shard_map/far3/ppermute | solution.py:467
  277.7 6.6 %finish.4 = (bf16[1024,1024]{1,0:T(8,128)(2,1)}, bf16[1024,1024]{1,0:T(8,128)(2,1)}, s32[8,128]{1,0:T(8,128)}) custom-call(s32[8,4]{1,0:T(8,128)} %get-tuple-element.120.refs_0_, f32[256,2048]{1,0:T(8,128)} %get-tuple-element.223.refs_1_, f32[256,2048]{1,0:T(8,128)} %get-tuple-element.224.refs_2_, ...), custom_call_target="tpu_custom_call", output_to_operand_aliasing={{0}: (12, {}), {1}: (13, {})} | custom-call | flops 4000000000 | bytes 1 | tf_op jit(solution)/shard_map/finish/pallas_call | solution.py:68
  284.4 20.7 %collective-permute-done.36.refs_3_ = bf16[256,2048]{1,0:T(8,128)(2,1)} collective-permute-done((bf16[256,2048]{1,0:T(8,128)(2,1)}, bf16[256,2048]{1,0:T(8,128)(2,1)}, u32[]{:S(2)}, u32[]{:S(2)}) %collective-permute-start.36) | collective-permute-done | bytes 1048608 | tf_op jit(solution)/shard_map/far4/ppermute | solution.py:467
  305.1 5.1 %finish.5 = (bf16[1024,1024]{1,0:T(8,128)(2,1)}, bf16[1024,1024]{1,0:T(8,128)(2,1)}, s32[8,128]{1,0:T(8,128)}) custom-call(s32[8,4]{1,0:T(8,128)} %get-tuple-element.120.refs_0_, f32[512,2048]{1,0:T(8,128)} %get-tuple-element.191.refs_3_.refs_1_, f32[512,2048]{1,0:T(8,128)} %get-tuple-element.221.refs_4_.refs_2_, ...), custom_call_target="tpu_custom_call", output_to_operand_aliasing={{0}: (10, {}), {1}: (11, {})} | custom-call | flops 4000000000 | bytes 1 | tf_op jit(solution)/shard_map/finish/pallas_call | solution.py:68
  (123 shorter events, 115.0 us)
Async XLA Ops:
  42.1 25.5 %collective-permute-start.9 = (bf16[256,2048]{1,0:T(8,128)(2,1)}, bf16[256,2048]{1,0:T(8,128)(2,1)}, u32[]{:S(2)}, u32[]{:S(2)}) collective-permute-start(bf16[256,2048]{1,0:T(8,128)(2,1)} %get-tuple-element.135), channel_id=1, source_target_pairs={{0,8},{4,12},{8,0},{12,4},{1,9},{5,13},{9,1},{13,5},{2,10},{6,14},... | collective-permute-start | bytes 3145736 | tf_op jit(solution)/shard_map/h1/ppermute | solution.py:467
  44.7 34.3 %collective-permute-start.15 = (bf16[512,1024]{1,0:T(8,128)(2,1)}, bf16[512,1024]{1,0:T(8,128)(2,1)}, u32[]{:S(2)}, u32[]{:S(2)}) collective-permute-start(bf16[512,1024]{1,0:T(8,128)(2,1)} %get-tuple-element.146), channel_id=1, source_target_pairs={{0,1},{3,2},{4,5},{7,6},{8,9},{11,10},{12,13},{15,14},{16,17},{19,... | collective-permute-start | bytes 3145736 | tf_op jit(solution)/shard_map/ink/ppermute | solution.py:467
  51.5 27.6 %collective-permute-start.14 = (bf16[256,2048]{1,0:T(8,128)(2,1)}, bf16[256,2048]{1,0:T(8,128)(2,1)}, u32[]{:S(2)}, u32[]{:S(2)}) collective-permute-start(bf16[256,2048]{1,0:T(8,128)(2,1)} %get-tuple-element.145), channel_id=1, source_target_pairs={{1,2},{2,1},{5,6},{6,5},{9,10},{10,9},{13,14},{14,13},{17,18},{18,... | collective-permute-start | bytes 3145736 | tf_op jit(solution)/shard_map/mr0/ppermute | solution.py:467
  59.6 55.4 %collective-permute-start.19 = (bf16[256,2048]{1,0:T(8,128)(2,1)}, bf16[256,2048]{1,0:T(8,128)(2,1)}, u32[]{:S(2)}, u32[]{:S(2)}) collective-permute-start(bf16[256,2048]{1,0:T(8,128)(2,1)} %get-tuple-element.159), channel_id=1, source_target_pairs={{1,2},{2,1},{5,6},{6,5},{9,10},{10,9},{13,14},{14,13},{17,18},{18,... | collective-permute-start | bytes 3145736 | tf_op jit(solution)/shard_map/mr1/ppermute | solution.py:467
  71.6 29.9 %collective-permute-start.13 = (bf16[256,2048]{1,0:T(8,128)(2,1)}, bf16[256,2048]{1,0:T(8,128)(2,1)}, u32[]{:S(2)}, u32[]{:S(2)}) collective-permute-start(bf16[256,2048]{1,0:T(8,128)(2,1)} %get-tuple-element.144.refs_0_.refs_1_), channel_id=1, source_target_pairs={{0,1},{1,0},{2,3},{3,2},{4,5},{5,4},{6,7},{7,6},{8,9},{9,8},{10,11... | collective-permute-start | bytes 3145736 | tf_op jit(solution)/shard_map/ex2/ppermute | solution.py:467
  72.1 34.3 %collective-permute-start.12 = (bf16[256,2048]{1,0:T(8,128)(2,1)}, bf16[256,2048]{1,0:T(8,128)(2,1)}, u32[]{:S(2)}, u32[]{:S(2)}) collective-permute-start(bf16[256,2048]{1,0:T(8,128)(2,1)} %get-tuple-element.143), channel_id=1, source_target_pairs={{0,8},{4,12},{8,0},{12,4},{1,9},{5,13},{9,1},{13,5},{2,10},{6,14},... | collective-permute-start | bytes 3145736 | tf_op jit(solution)/shard_map/h2/ppermute | solution.py:467
  79.1 41.4 %collective-permute-start.17 = (bf16[256,2048]{1,0:T(8,128)(2,1)}, bf16[256,2048]{1,0:T(8,128)(2,1)}, u32[]{:S(2)}, u32[]{:S(2)}) collective-permute-start(bf16[256,2048]{1,0:T(8,128)(2,1)} %get-tuple-element.156.refs_1_), channel_id=1, source_target_pairs={{1,0},{2,3},{5,4},{6,7},{9,8},{10,11},{13,12},{14,15},{17,16},{18,... | collective-permute-start | bytes 3145736 | tf_op jit(solution)/shard_map/fw0/ppermute | solution.py:467
  80.4 43.6 %collective-permute-start.18 = (bf16[512,1024]{1,0:T(8,128)(2,1)}, bf16[512,1024]{1,0:T(8,128)(2,1)}, u32[]{:S(2)}, u32[]{:S(2)}) collective-permute-start(bf16[512,1024]{1,0:T(8,128)(2,1)} %get-tuple-element.157), channel_id=1, source_target_pairs={{0,1},{3,2},{4,5},{7,6},{8,9},{11,10},{12,13},{15,14},{16,17},{19,... | collective-permute-start | bytes 3145736 | tf_op jit(solution)/shard_map/inv/ppermute | solution.py:467
  104.4 45.0 %collective-permute-start.22 = (bf16[512,2048]{1,0:T(8,128)(2,1)}, bf16[512,2048]{1,0:T(8,128)(2,1)}, u32[]{:S(2)}, u32[]{:S(2)}) collective-permute-start(bf16[512,2048]{1,0:T(8,128)(2,1)} %get-tuple-element.166), channel_id=1, source_target_pairs={{1,2},{2,1},{5,6},{6,5},{9,10},{10,9},{13,14},{14,13},{17,18},{18,... | collective-permute-start | bytes 6291464 | tf_op jit(solution)/shard_map/mr2/ppermute | solution.py:467
  109.9 35.4 %collective-permute-start.16 = (bf16[256,2048]{1,0:T(8,128)(2,1)}, bf16[256,2048]{1,0:T(8,128)(2,1)}, u32[]{:S(2)}, u32[]{:S(2)}) collective-permute-start(bf16[256,2048]{1,0:T(8,128)(2,1)} %get-tuple-element.155.refs_0_.refs_1_), channel_id=1, source_target_pairs={{0,1},{1,0},{2,3},{3,2},{4,5},{5,4},{6,7},{7,6},{8,9},{9,8},{10,11... | collective-permute-start | bytes 3145736 | tf_op jit(solution)/shard_map/ex3/ppermute | solution.py:467
  115.1 36.3 %collective-permute-start.21 = (bf16[256,2048]{1,0:T(8,128)(2,1)}, bf16[256,2048]{1,0:T(8,128)(2,1)}, u32[]{:S(2)}, u32[]{:S(2)}) collective-permute-start(bf16[256,2048]{1,0:T(8,128)(2,1)} %get-tuple-element.165), channel_id=1, source_target_pairs={{0,8},{4,12},{8,0},{12,4},{1,9},{5,13},{9,1},{13,5},{2,10},{6,14},... | collective-permute-start | bytes 3145736 | tf_op jit(solution)/shard_map/h3/ppermute | solution.py:467
  124.0 39.7 %collective-permute-start.20 = (bf16[256,2048]{1,0:T(8,128)(2,1)}, bf16[256,2048]{1,0:T(8,128)(2,1)}, u32[]{:S(2)}, u32[]{:S(2)}) collective-permute-start(bf16[256,2048]{1,0:T(8,128)(2,1)} %get-tuple-element.164.refs_3_), channel_id=1, source_target_pairs={{1,0},{2,3},{5,4},{6,7},{9,8},{10,11},{13,12},{14,15},{17,16},{18,... | collective-permute-start | bytes 3145736 | tf_op jit(solution)/shard_map/fw1/ppermute | solution.py:467
  125.3 38.4 %collective-permute-start.26 = (bf16[512,1024]{1,0:T(8,128)(2,1)}, bf16[512,1024]{1,0:T(8,128)(2,1)}, u32[]{:S(2)}, u32[]{:S(2)}) collective-permute-start(bf16[512,1024]{1,0:T(8,128)(2,1)} %get-tuple-element.185.refs_1_), channel_id=1, source_target_pairs={{0,16},{16,0},{1,17},{17,1},{2,18},{18,2},{3,19},{19,3},{4,20},{20... | collective-permute-start | bytes 3145736 | tf_op jit(solution)/shard_map/wk1/ppermute | solution.py:467
  145.3 25.3 %collective-permute-start.25 = (bf16[512,1024]{1,0:T(8,128)(2,1)}, bf16[512,1024]{1,0:T(8,128)(2,1)}, u32[]{:S(2)}, u32[]{:S(2)}) collective-permute-start(bf16[512,1024]{1,0:T(8,128)(2,1)} %get-tuple-element.184.refs_1_), channel_id=1, source_target_pairs={{0,8},{4,12},{8,0},{12,4},{1,9},{5,13},{9,1},{13,5},{2,10},{6,14},... | collective-permute-start | bytes 3145736 | tf_op jit(solution)/shard_map/wv1/ppermute | solution.py:467
  149.4 57.2 %collective-permute-start.27 = (bf16[512,2048]{1,0:T(8,128)(2,1)}, bf16[512,2048]{1,0:T(8,128)(2,1)}, u32[]{:S(2)}, u32[]{:S(2)}) collective-permute-start(bf16[512,2048]{1,0:T(8,128)(2,1)} %get-tuple-element.192), channel_id=1, source_target_pairs={{1,2},{2,1},{5,6},{6,5},{9,10},{10,9},{13,14},{14,13},{17,18},{18,... | collective-permute-start | bytes 6291464 | tf_op jit(solution)/shard_map/mr3/ppermute | solution.py:467
  156.0 22.5 %collective-permute-start.24 = (f32[16,128]{1,0:T(8,128)}, f32[16,128]{1,0:T(8,128)S(1)}, u32[]{:S(2)}, u32[]{:S(2)}) collective-permute-start(f32[16,128]{1,0:T(8,128)} %get-tuple-element.183.refs_0_), channel_id=1, source_target_pairs={{0,1},{1,0},{2,3},{3,2},{4,5},{5,4},{6,7},{7,6},{8,9},{9,8},{10,11... | collective-permute-start | bytes 24584 | tf_op jit(solution)/shard_map/half/ppermute | solution.py:467
  163.7 26.4 %collective-permute-start.23 = (bf16[256,2048]{1,0:T(8,128)(2,1)}, bf16[256,2048]{1,0:T(8,128)(2,1)}, u32[]{:S(2)}, u32[]{:S(2)}) collective-permute-start(bf16[256,2048]{1,0:T(8,128)(2,1)} %get-tuple-element.181.refs_3_.refs_0_), channel_id=1, source_target_pairs={{0,1},{1,0},{2,3},{3,2},{4,5},{5,4},{6,7},{7,6},{8,9},{9,8},{10,11... | collective-permute-start | bytes 3145736 | tf_op jit(solution)/shard_map/ex4/ppermute | solution.py:467
  167.3 60.3 %collective-permute-start.29 = (bf16[1024,1024]{1,0:T(8,128)(2,1)}, bf16[1024,1024]{1,0:T(8,128)(2,1)}, u32[]{:S(2)}, u32[]{:S(2)}) collective-permute-start(bf16[1024,1024]{1,0:T(8,128)(2,1)} %get-tuple-element.187.refs_3_.refs_2_), channel_id=1, source_target_pairs={{0,8},{4,12},{8,0},{12,4},{1,9},{5,13},{9,1},{13,5},{2,10},{6,14},... | collective-permute-start | bytes 6291464 | tf_op jit(solution)/shard_map/wk2/ppermute | solution.py:467
  176.9 50.7 %collective-permute-start.30 = (bf16[1024,1024]{1,0:T(8,128)(2,1)}, bf16[1024,1024]{1,0:T(8,128)(2,1)}, u32[]{:S(2)}, u32[]{:S(2)}) collective-permute-start(bf16[1024,1024]{1,0:T(8,128)(2,1)} %get-tuple-element.199.refs_3_), channel_id=1, source_target_pairs={{0,16},{16,0},{1,17},{17,1},{2,18},{18,2},{3,19},{19,3},{4,20},{20... | collective-permute-start | bytes 6291464 | tf_op jit(solution)/shard_map/wv2/ppermute | solution.py:467
  179.1 54.2 %collective-permute-start.34 = (bf16[512,2048]{1,0:T(8,128)(2,1)}, bf16[512,2048]{1,0:T(8,128)(2,1)}, u32[]{:S(2)}, u32[]{:S(2)}) collective-permute-start(bf16[512,2048]{1,0:T(8,128)(2,1)} %get-tuple-element.208.refs_1_), channel_id=1, source_target_pairs={{1,0},{2,3},{5,4},{6,7},{9,8},{10,11},{13,12},{14,15},{17,16},{18,... | collective-permute-start | bytes 6291464 | tf_op jit(solution)/shard_map/fw2/ppermute | solution.py:467
  208.0 20.2 %collective-permute-start.35 = (f32[16,128]{1,0:T(8,128)}, f32[16,128]{1,0:T(8,128)S(1)}, u32[]{:S(2)}, u32[]{:S(2)}) collective-permute-start(f32[16,128]{1,0:T(8,128)} %get-tuple-element.211.refs_5_.refs_6_.refs_4_), channel_id=1, source_target_pairs={{0,3},{1,2},{2,1},{3,0},{4,7},{5,6},{6,5},{7,4},{8,11},{9,10},{10,... | collective-permute-start | bytes 24584 | tf_op jit(solution)/shard_map/rest/ppermute | solution.py:467
  213.3 43.1 %collective-permute-start.28 = (bf16[512,2048]{1,0:T(8,128)(2,1)}, bf16[512,2048]{1,0:T(8,128)(2,1)}, u32[]{:S(2)}, u32[]{:S(2)}) collective-permute-start(bf16[512,2048]{1,0:T(8,128)(2,1)} %get-tuple-element.198), channel_id=1, source_target_pairs={{1,2},{2,1},{5,6},{6,5},{9,10},{10,9},{13,14},{14,13},{17,18},{18,... | collective-permute-start | bytes 6291464 | tf_op jit(solution)/shard_map/mr4/ppermute | solution.py:467
  242.9 34.8 %collective-permute-start.37 = (bf16[256,2048]{1,0:T(8,128)(2,1)}, bf16[256,2048]{1,0:T(8,128)(2,1)}, u32[]{:S(2)}, u32[]{:S(2)}) collective-permute-start(bf16[256,2048]{1,0:T(8,128)(2,1)} %get-tuple-element.225), channel_id=1, source_target_pairs={{1,0},{2,3},{5,4},{6,7},{9,8},{10,11},{13,12},{14,15},{17,16},{18,... | collective-permute-start | bytes 3145736 | tf_op jit(solution)/shard_map/far3/ppermute | solution.py:467
  258.4 46.6 %collective-permute-start.36 = (bf16[256,2048]{1,0:T(8,128)(2,1)}, bf16[256,2048]{1,0:T(8,128)(2,1)}, u32[]{:S(2)}, u32[]{:S(2)}) collective-permute-start(bf16[256,2048]{1,0:T(8,128)(2,1)} %get-tuple-element.222), channel_id=1, source_target_pairs={{1,0},{2,3},{5,4},{6,7},{9,8},{10,11},{13,12},{14,15},{17,16},{18,... | collective-permute-start | bytes 3145736 | tf_op jit(solution)/shard_map/far4/ppermute | solution.py:467
  (24 other events, 185.2 us)

commit v3 on v2

--- a/solution.py
+++ b/solution.py
@@ -236,73 +236,83 @@
         c.wait()
 
 
-def near_kernel(sizes, first, handed, info, *refs):
+def near_kernel(sizes, first, lead, counts, info, *refs):
     n = len(sizes)
     wk, wv, acc, acts, sems = refs[-5:]
-    arrays = refs[:-5]
-    per = len(arrays) // n
+    arrays = [refs[sum(counts[:c]) : sum(counts[: c + 1])] for c in range(n)]
     slabs = acts.shape[0]
     i = pl.program_id(0)
     slab, half = first + i // 2, lax.rem(i, 2)
     inner = info[4] == 1
-    full = (i >= 0) if handed else inner
     starts = [sum(sizes[:c]) for c in range(n)]
 
-    def copies(s, which, skip=0):
+    def copies(s, which, skip=0, rows=sum(sizes)):
         return [
             pltpu.make_async_copy(
-                arrays[per * c + which].at[pl.ds(skip * sizes[c], sizes[c])],
+                arrays[c][which].at[pl.ds(skip * sizes[c], sizes[c])],
                 acts.at[s - first, pl.ds(starts[c], sizes[c])],
                 sems.at[s - first, c],
             )
             for c in range(n)
+            if starts[c] < rows
         ]
+
+    def held(s, fetch):
+        if s < 2:
+            fetch(copies(s, s))
+        else:
+
+            @pl.when(inner)
+            def _():
+                fetch(copies(s, 2 - first, s - 2))
+
+            if lead:
+
+                @pl.when(jnp.logical_not(inner))
+                def _():
+                    fetch(copies(s, 3 - first, s - 2, lead))
+
+    def start(made):
+        for c in made:
+            c.start()
+
+    def wait(made):
+        for c in made:
+            c.wait()
 
     @pl.when(i == 0)
     def _():
         for s in range(first, first + slabs):
-            if s < 2:
-                for c in copies(s, s):
-                    c.start()
-            else:
-
-                @pl.when(inner)
-                def _():
-                    for c in copies(s, 2 - first, s - 2):
-                        c.start()
-
-                if handed:
-
-                    @pl.when(jnp.logical_not(inner))
-                    def _():
-                        for c in copies(s, 3 - first, s - 2):
-                            c.start()
+            held(s, start)
 
     for s in range(first, first + slabs):
 
-        @pl.when((half == 0) & (slab == s) & ((s < 2) | full))
+        @pl.when((half == 0) & (slab == s))
         def _():
-            for c in copies(s, 0):
-                c.wait()
+            held(s, wait)
 
     part, cols = wk.shape
 
     @pl.when(i == 0)
     def _():
-        if first >= 2 and not handed:
-            acc[...] = jnp.zeros_like(acc)
-
-        @pl.when((first < 2) | full)
+        acc[...] = jnp.zeros_like(acc)
+
+    def add(rows):
+        a = acts[slab - first, :rows, pl.ds(pl.multiple_of(half * part, part), part)]
+        acc[:rows, :cols] += jnp.dot(a, wk[...], preferred_element_type=jnp.float32)
+        acc[:rows, cols:] += jnp.dot(a, wv[...], preferred_element_type=jnp.float32)
+
+    whole_rows = (slab < 2) | inner if lead < sum(sizes) else i >= 0
+
+    @pl.when(whole_rows)
+    def _():
+        add(sum(sizes))
+
+    if 0 < lead < sum(sizes):
+
+        @pl.when(jnp.logical_not(whole_rows))
         def _():
-            a = acts[0, :, :part]
-            acc[:, :cols] = jnp.dot(a, wk[...], preferred_element_type=jnp.float32)
-            acc[:, cols:] = jnp.dot(a, wv[...], preferred_element_type=jnp.float32)
-
-    @pl.when((i > 0) & ((slab < 2) | full))
-    def _():
-        a = acts[slab - first, :, pl.ds(pl.multiple_of(half * part, part), part)]
-        acc[:, :cols] += jnp.dot(a, wk[...], preferred_element_type=jnp.float32)
-        acc[:, cols:] += jnp.dot(a, wv[...], preferred_element_type=jnp.float32)
+            add(lead)
 
 
 def far_kernel(sizes, info, *refs):
@@ -482,8 +492,8 @@
         k, low, rows = CHUNKS[c]
         pieces, arrays = [], []
         for r in range(k + 1):
-            pieces.append((r, 1, 0, BLOCK, r * BLOCK))
-            arrays.append(beside)
+            pieces.append((r, 1, 0, BLOCK, 0 if r == 0 else (most + r - 2) * BLOCK))
+            arrays.append(beside[min(r, 1)])
         for i, (r, p_low, p_rows) in enumerate(STEPS):
             if r <= k and p_low < low + rows and low < p_low + p_rows:
                 for m in (2, 3):
@@ -523,19 +533,24 @@
         )
         return out
 
-    def near(taken, first, last, handed):
+    handed = (0, 1, 2)
+
+    def near(taken, first, last):
         sizes = [2 * CHUNKS[c][2] for c in taken]
         total = sum(sizes)
-        kinds = ((own, ex) if first == 0 else ()) + ((mr,) if last == 4 else ()) + ((fw,) if last == 4 and handed else ())
-        slabs = [kind[c] for c in taken for kind in kinds]
+        rows_handed = sum(size for c, size in zip(taken, sizes) if last == 4 and c in handed)
+        kinds = ((own, ex) if first == 0 else ()) + ((mr,) if last == 4 else ())
+        groups = [[k[c] for k in kinds] + ([fw[c]] if last == 4 and c in handed else []) for c in taken]
+        slabs = [array for group in groups for array in group]
+        counts_in = [len(group) for group in groups]
 
         def weights(i, info):
             slab = first + i // 2
-            skip = (slab >= 2) & (info[4] == 0) & (not handed)
+            skip = (slab >= 2) & (info[4] == 0) & (rows_handed == 0)
             return (jnp.where(skip, info[1] * 2 + 1, info[slab] * 2 + lax.rem(i, 2)), 0)
 
         (acc,) = call(
-            functools.partial(near_kernel, sizes, first, handed),
+            functools.partial(near_kernel, sizes, first, rows_handed, counts_in),
             "near",
             (info, *slabs, key_weight, value_weight),
             [HBM] * len(slabs) + [pl.BlockSpec((width // 2, cols), weights)] * 2,
@@ -607,9 +622,9 @@
         came[i] = {m: (move("a%d" % i, array, swap[m]), 0) for m, array in zip((2, 3), sent)}
 
     tables = [move("table", dest_table, swap[m]) for m in range(1, stores)]
-    exchange(0, send(*both_ways(0)))
-    (bulk,) = send([(k * BLOCK, 1, (k, 0, BLOCK)) for k in range(most)])
-    beside = move("beside", bulk, swap[1])
+    *s0, close = send(*both_ways(0), [(0, 1, (0, 0, BLOCK))])
+    exchange(0, s0)
+    beside = [move("b0", close, swap[1])]
     (plan,) = call(
         functools.partial(plan_kernel, stores, per_row),
         "plan",
@@ -630,9 +645,11 @@
         )
 
     onward = [((k - 1) * BLOCK, 3, (k, 0, BLOCK)) for k in range(1, most)]
+    onward += [((most + k - 2) * BLOCK, 1, (k, 0, BLOCK)) for k in range(1, most)]
     *s1, passed = send(*both_ways(1), onward)
     exchange(1, s1)
     passed = move("pass", passed, swap[1])
+    beside.append(passed)
     prep(0, FAR)
     pass_own(0)
     packs = call(
@@ -669,7 +686,7 @@
     mr[0], lent_k, lent_v = pin(mr[0], lent_k, cuts[1])
     hand(0)
     lent_v = move("inv", lent_v, inward)
-    near((0, 1), 0, 2, True)
+    near((0, 1), 0, 2)
     relay(2)
     prep(3)
     pass_own(3)
@@ -680,7 +697,7 @@
     came_k = move("wk1", lent_k, across)
     (lent_v,) = pin(lent_v)
     came_v = move("wv1", lent_v, swap[2])
-    near((2,), 0, 2, True)
+    near((2,), 0, 2)
     relay(3)
     (mr[2],) = pin(mr[2])
     prep(4)
@@ -694,12 +711,12 @@
     came_v = move("wv2", joined_v, across)
     mr[2], paired = pin(mr[2], paired)
     hand(2)
-    near((3, 4), 0, 2, True)
+    near((3, 4), 0, 2)
     (mr[3],) = pin(mr[3])
     squares = sums(1, squares, paired)
     rest = move("rest", squares, ends)
     relay(4)
-    near((0, 1), 2, 4, True)
+    near((0, 1), 2, 4)
     came_k, came_v, joined = pin(came_k, came_v, joined)
     beside_w = [move("core", w, swap[1]) for w in (joined, came_k, came_v)]
     total_squares = (squares, rest)
@@ -707,9 +724,8 @@
     (fw[2],) = pin(fw[2], cost=FAR)
     reached = (joined_k, joined_v, came_k, came_v, *beside_w)
     reach(3)
-    near((2,), 2, 4, True)
     reach(4)
-    near((3, 4), 2, 4, False)
+    near((2, 3, 4), 2, 4)
     finish(2, 3)
     finish(4)
     return tuple(done)

time: 312 us -> 305 us (0.978)
  Pallas kernels: 151 us -> 145 us
    pallas_call x45 -> x43, Pallas kernels: 151 us -> 145 us  [__call__(): pl.pallas_call(body, out_shape=tuple(outs) + (TOKEN,), input_output_alias...]
  transfers between devices with their start and end apart: 38 -> 38, of which waited for: 15 -> 16; matrix products, arithmetic and copies ran while one was open for 1% -> 2% of each run, Pallas kernels for 44% -> 44%
where the time goes in v3:
time: 305 us; the launch traced here: 304 us
  Pallas kernels  145 us (48%)
  waiting for transfers between devices  85.5 us (28%)
  starting transfers between devices  62.5 us (20%)
  local copies, waits for them, and re-layouts  5.18 us (2%)
  other arithmetic  3.94 us (1%)
    pallas_call x43, Pallas kernels, __call__(): pl.pallas_call(body, out_shape=tuple(outs) + (TOKEN,), input_output_alias...  145 us
    ppermute x38, waiting for transfers between devices, move(): return lax.ppermute(array, *way)  85.5 us
    ppermute x38, starting transfers between devices, move(): return lax.ppermute(array, *way)  62.5 us
  transfers between devices with their start and end apart: 38, of which 16 were waited for; matrix products, arithmetic and copies ran while one was open for 2% of the time, Pallas kernels for 44%

profile of v3, /device:TPU:0, one launch (start us, length us, event | category | flops | bytes accessed | tf_op | source)
XLA Modules:
  0.0 303.7 jit_solution(3141223927828626333)
XLA Ops:
  12.5 4.6 %send.3 = (bf16[64,2048]{1,0:T(8,128)(2,1)}, bf16[64,2048]{1,0:T(8,128)(2,1)}, bf16[768,2048]{1,0:T(8,128)(2,1)}, s32[8,128]{1,0:T(8,128)}) custom-call(s32[1,16]{1,0:T(1,128)} %refs_0_.9, bf16[2048,2048]{1,0:T(8,128)(2,1)} %bitcast.13, s32[8,128]{1,0:T(8,128)} %get-tuple-element.118.refs_2_), custom_call_target="tpu_custom_call" | custom-call | flops 4000000000 | bytes 1 | tf_op jit(solution)/shard_map/send/pallas_call | solution.py:68
  19.3 3.5 %collective-permute-done.6.refs_4_.refs_5_.refs_6_.refs_7_ = bf16[64,2048]{1,0:T(8,128)(2,1)} collective-permute-done((bf16[64,2048]{1,0:T(8,128)(2,1)}, bf16[64,2048]{1,0:T(8,128)(2,1)}, u32[]{:S(2)}, u32[]{:S(2)}) %collective-permute-start.6) | collective-permute-done | bytes 262176 | tf_op jit(solution)/shard_map/a0/ppermute | solution.py:477
  28.2 4.2 %pack.1 = (bf16[256,2048]{1,0:T(8,128)(2,1)}, bf16[256,2048]{1,0:T(8,128)(2,1)}, bf16[256,2048]{1,0:T(8,128)(2,1)}, s32[8,128]{1,0:T(8,128)}) custom-call(s32[1,16]{1,0:T(1,128)} %refs_0_.9, bf16[2048,2048]{1,0:T(8,128)(2,1)} %bitcast.15, bf16[768,2048]{1,0:T(8,128)(2,1)} %collective-permute-done.4.refs_2_.refs_3_.refs_4_.refs_5_, ...), custom_call_target="tpu_custom_call" | custom-call | flops 4000000000 | bytes 1 | tf_op jit(solution)/shard_map/pack/pallas_call | solution.py:68
  45.8 6.5 %collective-permute-start.15 = (bf16[512,1024]{1,0:T(8,128)(2,1)}, bf16[512,1024]{1,0:T(8,128)(2,1)}, u32[]{:S(2)}, u32[]{:S(2)}) collective-permute-start(bf16[512,1024]{1,0:T(8,128)(2,1)} %get-tuple-element.142), channel_id=1, source_target_pairs={{0,1},{3,2},{4,5},{7,6},{8,9},{11,10},{12,13},{15,14},{16,17},{19,... | collective-permute-start | bytes 3145736 | tf_op jit(solution)/shard_map/ink/ppermute | solution.py:477
  57.9 6.0 %collective-permute-done.9.refs_8_.refs_9_.refs_10_.refs_11_ = bf16[256,2048]{1,0:T(8,128)(2,1)} collective-permute-done((bf16[256,2048]{1,0:T(8,128)(2,1)}, bf16[256,2048]{1,0:T(8,128)(2,1)}, u32[]{:S(2)}, u32[]{:S(2)}) %collective-permute-start.9) | collective-permute-done | bytes 1048608 | tf_op jit(solution)/shard_map/h1/ppermute | solution.py:477
  76.4 6.6 %collective-permute-start.18 = (bf16[512,1024]{1,0:T(8,128)(2,1)}, bf16[512,1024]{1,0:T(8,128)(2,1)}, u32[]{:S(2)}, u32[]{:S(2)}) collective-permute-start(bf16[512,1024]{1,0:T(8,128)(2,1)} %get-tuple-element.153), channel_id=1, source_target_pairs={{0,1},{3,2},{4,5},{7,6},{8,9},{11,10},{12,13},{15,14},{16,17},{19,... | collective-permute-start | bytes 3145736 | tf_op jit(solution)/shard_map/inv/ppermute | solution.py:477
  83.1 12.3 %near.5 = (f32[256,2048]{1,0:T(8,128)}, s32[8,128]{1,0:T(8,128)}) custom-call(s32[8]{0:T(128)} %stack.39.refs_0_, bf16[128,2048]{1,0:T(8,128)(2,1)} %get-tuple-element.134.refs_0_.refs_1_, bf16[128,2048]{1,0:T(8,128)(2,1)} %copy-done.2, bf16[128,2048]{1,0:T(8,128)(2,1)} %get-tuple-element.133.refs_0_.refs_3_, ...), custom_call_target="tpu_custom_call" | custom-call | flops 4000000000 | bytes 1 | tf_op jit(solution)/shard_map/near/pallas_call | solution.py:68
  105.9 4.6 %collective-permute-start.16 = (bf16[256,2048]{1,0:T(8,128)(2,1)}, bf16[256,2048]{1,0:T(8,128)(2,1)}, u32[]{:S(2)}, u32[]{:S(2)}) collective-permute-start(bf16[256,2048]{1,0:T(8,128)(2,1)} %get-tuple-element.151.refs_0_.refs_1_), channel_id=1, source_target_pairs={{0,1},{1,0},{2,3},{3,2},{4,5},{5,4},{6,7},{7,6},{8,9},{9,8},{10,11... | collective-permute-start | bytes 3145736 | tf_op jit(solution)/shard_map/ex3/ppermute | solution.py:477
  111.8 4.9 %collective-permute-done.17.refs_0_ = bf16[256,2048]{1,0:T(8,128)(2,1)} collective-permute-done((bf16[256,2048]{1,0:T(8,128)(2,1)}, bf16[256,2048]{1,0:T(8,128)(2,1)}, u32[]{:S(2)}, u32[]{:S(2)}) %collective-permute-start.17) | collective-permute-done | bytes 1048608 | tf_op jit(solution)/shard_map/fw0/ppermute | solution.py:477
  123.0 12.4 %near.6 = (f32[256,2048]{1,0:T(8,128)}, s32[8,128]{1,0:T(8,128)}) custom-call(s32[8]{0:T(128)} %stack.39.refs_0_, bf16[256,2048]{1,0:T(8,128)(2,1)} %get-tuple-element.140.refs_0_.refs_1_, bf16[256,2048]{1,0:T(8,128)(2,1)} %collective-permute-done.13.refs_1_.refs_2_, bf16[8192,1024]{1,0:T(8,128)(2,1)} %refs_5_.7, bf16[8192,1024]{1,0:T(8,128)(2,1)} %refs_6_.7, ...), custom_call_target="tpu_custom_call" | custom-call | flops 4000000000 | bytes 1 | tf_op jit(solution)/shard_map/near/pallas_call | solution.py:68
  135.3 6.7 %collective-permute-done.16.refs_1_.refs_2_ = bf16[256,2048]{1,0:T(8,128)(2,1)} collective-permute-done((bf16[256,2048]{1,0:T(8,128)(2,1)}, bf16[256,2048]{1,0:T(8,128)(2,1)}, u32[]{:S(2)}, u32[]{:S(2)}) %collective-permute-start.16) | collective-permute-done | bytes 1048608 | tf_op jit(solution)/shard_map/ex3/ppermute | solution.py:477
  152.2 9.4 %collective-permute-start.24 = (f32[16,128]{1,0:T(8,128)}, f32[16,128]{1,0:T(8,128)S(1)}, u32[]{:S(2)}, u32[]{:S(2)}) collective-permute-start(f32[16,128]{1,0:T(8,128)} %get-tuple-element.179.refs_0_), channel_id=1, source_target_pairs={{0,1},{1,0},{2,3},{3,2},{4,5},{5,4},{6,7},{7,6},{8,9},{9,8},{10,11... | collective-permute-start | bytes 24584 | tf_op jit(solution)/shard_map/half/ppermute | solution.py:477
  161.7 3.6 %join.2 = (bf16[1024,1024]{1,0:T(8,128)(2,1)}, s32[8,128]{1,0:T(8,128)}) custom-call(s32[8]{0:T(128)} %stack.39.refs_0_, bf16[512,1024]{1,0:T(8,128)(2,1)} %get-tuple-element.181.refs_1_, bf16[512,1024]{1,0:T(8,128)(2,1)} %collective-permute-done.26.refs_2_, s32[8,128]{1,0:T(8,128)} %get-tuple-element.182.refs_3_), custom_call_target="tpu_custom_call" | custom-call | flops 4000000000 | bytes 1 | tf_op jit(solution)/shard_map/join/pallas_call | solution.py:68
  166.9 6.5 %join.3 = (bf16[1024,1024]{1,0:T(8,128)(2,1)}, bf16[2048,1024]{1,0:T(8,128)(2,1)}, s32[8,128]{1,0:T(8,128)}) custom-call(s32[8]{0:T(128)} %stack.39.refs_0_, bf16[512,1024]{1,0:T(8,128)(2,1)} %get-tuple-element.180.refs_1_, bf16[512,1024]{1,0:T(8,128)(2,1)} %collective-permute-done.25.refs_2_, bf16[1024,1024]{1,0:T(8,128)(2,1)} %get-tuple-element.183.refs_3_.refs_2_, ...), custom_call_target="tpu_custom_call" | custom-call | flops 4000000000 | bytes 1 | tf_op jit(solution)/shard_map/join/pallas_call | solution.py:68
  176.7 11.3 %collective-permute-done.23.refs_4_.refs_1_ = bf16[256,2048]{1,0:T(8,128)(2,1)} collective-permute-done((bf16[256,2048]{1,0:T(8,128)(2,1)}, bf16[256,2048]{1,0:T(8,128)(2,1)}, u32[]{:S(2)}, u32[]{:S(2)}) %collective-permute-start.23) | collective-permute-done | bytes 1048608 | tf_op jit(solution)/shard_map/ex4/ppermute | solution.py:477
  188.0 16.8 %near.7 = (f32[512,2048]{1,0:T(8,128)}, s32[8,128]{1,0:T(8,128)}) custom-call(s32[8]{0:T(128)} %stack.39.refs_0_, bf16[256,2048]{1,0:T(8,128)(2,1)} %get-tuple-element.151.refs_0_.refs_1_, bf16[256,2048]{1,0:T(8,128)(2,1)} %collective-permute-done.16.refs_1_.refs_2_, bf16[256,2048]{1,0:T(8,128)(2,1)} %get-tuple-element.177.refs_3_.refs_0_, ...), custom_call_target="tpu_custom_call" | custom-call | flops 4000000000 | bytes 1 | tf_op jit(solution)/shard_map/near/pallas_call | solution.py:68
  212.3 12.3 %near.8 = (f32[256,2048]{1,0:T(8,128)}, s32[8,128]{1,0:T(8,128)}) custom-call(s32[8]{0:T(128)} %stack.39.refs_0_, bf16[256,2048]{1,0:T(8,128)(2,1)} %get-tuple-element.152.refs_1_, bf16[256,2048]{1,0:T(8,128)(2,1)} %get-tuple-element.190.refs_2_, bf16[256,2048]{1,0:T(8,128)(2,1)} %get-tuple-element.160.refs_3_, ...), custom_call_target="tpu_custom_call" | custom-call | flops 4000000000 | bytes 1 | tf_op jit(solution)/shard_map/near/pallas_call | solution.py:68
  225.9 4.5 %finish.3 = (bf16[1024,1024]{1,0:T(8,128)(2,1)}, bf16[1024,1024]{1,0:T(8,128)(2,1)}, s32[8,128]{1,0:T(8,128)}) custom-call(s32[8,4]{1,0:T(8,128)} %get-tuple-element.116.refs_0_, f32[256,2048]{1,0:T(8,128)} %get-tuple-element.189.refs_1_.refs_3_, f32[256,2048]{1,0:T(8,128)} %get-tuple-element.198.refs_2_.refs_4_, ...), custom_call_target="tpu_custom_call" | custom-call | flops 4000000000 | bytes 1 | tf_op jit(solution)/shard_map/finish/pallas_call | solution.py:68
  231.0 4.3 %collective-permute-done.34.refs_7_ = bf16[1024,1024]{1,0:T(8,128)(2,1)} collective-permute-done((bf16[1024,1024]{1,0:T(8,128)(2,1)}, bf16[1024,1024]{1,0:T(8,128)(2,1)}, u32[]{:S(2)}, u32[]{:S(2)}) %collective-permute-start.34) | collective-permute-done | bytes 2097184 | tf_op jit(solution)/shard_map/core/ppermute | solution.py:477
  244.6 14.0 %near.9 = (f32[768,2048]{1,0:T(8,128)}, s32[8,128]{1,0:T(8,128)}) custom-call(s32[8]{0:T(128)} %stack.39.refs_0_, bf16[512,2048]{1,0:T(8,128)(2,1)} %get-tuple-element.188.refs_1_, bf16[512,2048]{1,0:T(8,128)(2,1)} %get-tuple-element.207.refs_2_, bf16[512,2048]{1,0:T(8,128)(2,1)} %get-tuple-element.208.refs_1_.refs_3_, ...), custom_call_target="tpu_custom_call" | custom-call | flops 4000000000 | bytes 1 | tf_op jit(solution)/shard_map/near/pallas_call | solution.py:68
  258.6 18.0 %collective-permute-done.37.refs_5_ = bf16[256,2048]{1,0:T(8,128)(2,1)} collective-permute-done((bf16[256,2048]{1,0:T(8,128)(2,1)}, bf16[256,2048]{1,0:T(8,128)(2,1)}, u32[]{:S(2)}, u32[]{:S(2)}) %collective-permute-start.37) | collective-permute-done | bytes 1048608 | tf_op jit(solution)/shard_map/far3/ppermute | solution.py:477
  276.5 6.7 %finish.4 = (bf16[1024,1024]{1,0:T(8,128)(2,1)}, bf16[1024,1024]{1,0:T(8,128)(2,1)}, s32[8,128]{1,0:T(8,128)}) custom-call(s32[8,4]{1,0:T(8,128)} %get-tuple-element.116.refs_0_, f32[256,2048]{1,0:T(8,128)} %get-tuple-element.218.refs_1_, f32[768,2048]{1,0:T(8,128)} %get-tuple-element.216.refs_2_.refs_4_, ...), custom_call_target="tpu_custom_call", output_to_operand_aliasing={{0}: (12, {}), {1}: (13, {})} | custom-call | flops 4000000000 | bytes 1 | tf_op jit(solution)/shard_map/finish/pallas_call | solution.py:68
  283.3 15.3 %collective-permute-done.36.refs_3_ = bf16[256,2048]{1,0:T(8,128)(2,1)} collective-permute-done((bf16[256,2048]{1,0:T(8,128)(2,1)}, bf16[256,2048]{1,0:T(8,128)(2,1)}, u32[]{:S(2)}, u32[]{:S(2)}) %collective-permute-start.36) | collective-permute-done | bytes 1048608 | tf_op jit(solution)/shard_map/far4/ppermute | solution.py:477
  298.5 5.0 %finish.5 = (bf16[1024,1024]{1,0:T(8,128)(2,1)}, bf16[1024,1024]{1,0:T(8,128)(2,1)}, s32[8,128]{1,0:T(8,128)}) custom-call(s32[8,4]{1,0:T(8,128)} %get-tuple-element.116.refs_0_, f32[512,2048]{1,0:T(8,128)} %get-tuple-element.187.refs_3_.refs_1_, f32[768,2048]{1,0:T(8,128)} %get-tuple-element.216.refs_2_.refs_4_, ...), custom_call_target="tpu_custom_call", output_to_operand_aliasing={{0}: (10, {}), {1}: (11, {})} | custom-call | flops 4000000000 | bytes 1 | tf_op jit(solution)/shard_map/finish/pallas_call | solution.py:68
  (117 shorter events, 102.4 us)
Async XLA Ops:
  38.2 25.7 %collective-permute-start.9 = (bf16[256,2048]{1,0:T(8,128)(2,1)}, bf16[256,2048]{1,0:T(8,128)(2,1)}, u32[]{:S(2)}, u32[]{:S(2)}) collective-permute-start(bf16[256,2048]{1,0:T(8,128)(2,1)} %get-tuple-element.131), channel_id=1, source_target_pairs={{0,8},{4,12},{8,0},{12,4},{1,9},{5,13},{9,1},{13,5},{2,10},{6,14},... | collective-permute-start | bytes 3145736 | tf_op jit(solution)/shard_map/h1/ppermute | solution.py:477
  44.1 28.6 %collective-permute-start.14 = (bf16[256,2048]{1,0:T(8,128)(2,1)}, bf16[256,2048]{1,0:T(8,128)(2,1)}, u32[]{:S(2)}, u32[]{:S(2)}) collective-permute-start(bf16[256,2048]{1,0:T(8,128)(2,1)} %get-tuple-element.141), channel_id=1, source_target_pairs={{1,2},{2,1},{5,6},{6,5},{9,10},{10,9},{13,14},{14,13},{17,18},{18,... | collective-permute-start | bytes 3145736 | tf_op jit(solution)/shard_map/mr0/ppermute | solution.py:477
  45.8 29.4 %collective-permute-start.15 = (bf16[512,1024]{1,0:T(8,128)(2,1)}, bf16[512,1024]{1,0:T(8,128)(2,1)}, u32[]{:S(2)}, u32[]{:S(2)}) collective-permute-start(bf16[512,1024]{1,0:T(8,128)(2,1)} %get-tuple-element.142), channel_id=1, source_target_pairs={{0,1},{3,2},{4,5},{7,6},{8,9},{11,10},{12,13},{15,14},{16,17},{19,... | collective-permute-start | bytes 3145736 | tf_op jit(solution)/shard_map/ink/ppermute | solution.py:477
  56.3 54.3 %collective-permute-start.19 = (bf16[256,2048]{1,0:T(8,128)(2,1)}, bf16[256,2048]{1,0:T(8,128)(2,1)}, u32[]{:S(2)}, u32[]{:S(2)}) collective-permute-start(bf16[256,2048]{1,0:T(8,128)(2,1)} %get-tuple-element.155), channel_id=1, source_target_pairs={{1,2},{2,1},{5,6},{6,5},{9,10},{10,9},{13,14},{14,13},{17,18},{18,... | collective-permute-start | bytes 3145736 | tf_op jit(solution)/shard_map/mr1/ppermute | solution.py:477
  67.9 29.7 %collective-permute-start.13 = (bf16[256,2048]{1,0:T(8,128)(2,1)}, bf16[256,2048]{1,0:T(8,128)(2,1)}, u32[]{:S(2)}, u32[]{:S(2)}) collective-permute-start(bf16[256,2048]{1,0:T(8,128)(2,1)} %get-tuple-element.140.refs_0_.refs_1_), channel_id=1, source_target_pairs={{0,1},{1,0},{2,3},{3,2},{4,5},{5,4},{6,7},{7,6},{8,9},{9,8},{10,11... | collective-permute-start | bytes 3145736 | tf_op jit(solution)/shard_map/ex2/ppermute | solution.py:477
  68.3 34.2 %collective-permute-start.12 = (bf16[256,2048]{1,0:T(8,128)(2,1)}, bf16[256,2048]{1,0:T(8,128)(2,1)}, u32[]{:S(2)}, u32[]{:S(2)}) collective-permute-start(bf16[256,2048]{1,0:T(8,128)(2,1)} %get-tuple-element.139), channel_id=1, source_target_pairs={{0,8},{4,12},{8,0},{12,4},{1,9},{5,13},{9,1},{13,5},{2,10},{6,14},... | collective-permute-start | bytes 3145736 | tf_op jit(solution)/shard_map/h2/ppermute | solution.py:477
  75.1 41.6 %collective-permute-start.17 = (bf16[256,2048]{1,0:T(8,128)(2,1)}, bf16[256,2048]{1,0:T(8,128)(2,1)}, u32[]{:S(2)}, u32[]{:S(2)}) collective-permute-start(bf16[256,2048]{1,0:T(8,128)(2,1)} %get-tuple-element.152.refs_1_), channel_id=1, source_target_pairs={{1,0},{2,3},{5,4},{6,7},{9,8},{10,11},{13,12},{14,15},{17,16},{18,... | collective-permute-start | bytes 3145736 | tf_op jit(solution)/shard_map/fw0/ppermute | solution.py:477
  76.4 43.7 %collective-permute-start.18 = (bf16[512,1024]{1,0:T(8,128)(2,1)}, bf16[512,1024]{1,0:T(8,128)(2,1)}, u32[]{:S(2)}, u32[]{:S(2)}) collective-permute-start(bf16[512,1024]{1,0:T(8,128)(2,1)} %get-tuple-element.153), channel_id=1, source_target_pairs={{0,1},{3,2},{4,5},{7,6},{8,9},{11,10},{12,13},{15,14},{16,17},{19,... | collective-permute-start | bytes 3145736 | tf_op jit(solution)/shard_map/inv/ppermute | solution.py:477
  100.5 45.1 %collective-permute-start.22 = (bf16[512,2048]{1,0:T(8,128)(2,1)}, bf16[512,2048]{1,0:T(8,128)(2,1)}, u32[]{:S(2)}, u32[]{:S(2)}) collective-permute-start(bf16[512,2048]{1,0:T(8,128)(2,1)} %get-tuple-element.162), channel_id=1, source_target_pairs={{1,2},{2,1},{5,6},{6,5},{9,10},{10,9},{13,14},{14,13},{17,18},{18,... | collective-permute-start | bytes 6291464 | tf_op jit(solution)/shard_map/mr2/ppermute | solution.py:477
  105.9 36.1 %collective-permute-start.16 = (bf16[256,2048]{1,0:T(8,128)(2,1)}, bf16[256,2048]{1,0:T(8,128)(2,1)}, u32[]{:S(2)}, u32[]{:S(2)}) collective-permute-start(bf16[256,2048]{1,0:T(8,128)(2,1)} %get-tuple-element.151.refs_0_.refs_1_), channel_id=1, source_target_pairs={{0,1},{1,0},{2,3},{3,2},{4,5},{5,4},{6,7},{7,6},{8,9},{9,8},{10,11... | collective-permute-start | bytes 3145736 | tf_op jit(solution)/shard_map/ex3/ppermute | solution.py:477
  110.5 37.0 %collective-permute-start.21 = (bf16[256,2048]{1,0:T(8,128)(2,1)}, bf16[256,2048]{1,0:T(8,128)(2,1)}, u32[]{:S(2)}, u32[]{:S(2)}) collective-permute-start(bf16[256,2048]{1,0:T(8,128)(2,1)} %get-tuple-element.161), channel_id=1, source_target_pairs={{0,8},{4,12},{8,0},{12,4},{1,9},{5,13},{9,1},{13,5},{2,10},{6,14},... | collective-permute-start | bytes 3145736 | tf_op jit(solution)/shard_map/h3/ppermute | solution.py:477
  120.1 41.5 %collective-permute-start.20 = (bf16[256,2048]{1,0:T(8,128)(2,1)}, bf16[256,2048]{1,0:T(8,128)(2,1)}, u32[]{:S(2)}, u32[]{:S(2)}) collective-permute-start(bf16[256,2048]{1,0:T(8,128)(2,1)} %get-tuple-element.160.refs_3_), channel_id=1, source_target_pairs={{1,0},{2,3},{5,4},{6,7},{9,8},{10,11},{13,12},{14,15},{17,16},{18,... | collective-permute-start | bytes 3145736 | tf_op jit(solution)/shard_map/fw1/ppermute | solution.py:477
  121.4 40.3 %collective-permute-start.26 = (bf16[512,1024]{1,0:T(8,128)(2,1)}, bf16[512,1024]{1,0:T(8,128)(2,1)}, u32[]{:S(2)}, u32[]{:S(2)}) collective-permute-start(bf16[512,1024]{1,0:T(8,128)(2,1)} %get-tuple-element.181.refs_1_), channel_id=1, source_target_pairs={{0,16},{16,0},{1,17},{17,1},{2,18},{18,2},{3,19},{19,3},{4,20},{20... | collective-permute-start | bytes 3145736 | tf_op jit(solution)/shard_map/wk1/ppermute | solution.py:477
  142.0 24.9 %collective-permute-start.25 = (bf16[512,1024]{1,0:T(8,128)(2,1)}, bf16[512,1024]{1,0:T(8,128)(2,1)}, u32[]{:S(2)}, u32[]{:S(2)}) collective-permute-start(bf16[512,1024]{1,0:T(8,128)(2,1)} %get-tuple-element.180.refs_1_), channel_id=1, source_target_pairs={{0,8},{4,12},{8,0},{12,4},{1,9},{5,13},{9,1},{13,5},{2,10},{6,14},... | collective-permute-start | bytes 3145736 | tf_op jit(solution)/shard_map/wv1/ppermute | solution.py:477
  145.6 59.3 %collective-permute-start.28 = (bf16[512,2048]{1,0:T(8,128)(2,1)}, bf16[512,2048]{1,0:T(8,128)(2,1)}, u32[]{:S(2)}, u32[]{:S(2)}) collective-permute-start(bf16[512,2048]{1,0:T(8,128)(2,1)} %get-tuple-element.193), channel_id=1, source_target_pairs={{1,2},{2,1},{5,6},{6,5},{9,10},{10,9},{13,14},{14,13},{17,18},{18,... | collective-permute-start | bytes 6291464 | tf_op jit(solution)/shard_map/mr3/ppermute | solution.py:477
  152.2 22.5 %collective-permute-start.24 = (f32[16,128]{1,0:T(8,128)}, f32[16,128]{1,0:T(8,128)S(1)}, u32[]{:S(2)}, u32[]{:S(2)}) collective-permute-start(f32[16,128]{1,0:T(8,128)} %get-tuple-element.179.refs_0_), channel_id=1, source_target_pairs={{0,1},{1,0},{2,3},{3,2},{4,5},{5,4},{6,7},{7,6},{8,9},{9,8},{10,11... | collective-permute-start | bytes 24584 | tf_op jit(solution)/shard_map/half/ppermute | solution.py:477
  161.6 26.4 %collective-permute-start.23 = (bf16[256,2048]{1,0:T(8,128)(2,1)}, bf16[256,2048]{1,0:T(8,128)(2,1)}, u32[]{:S(2)}, u32[]{:S(2)}) collective-permute-start(bf16[256,2048]{1,0:T(8,128)(2,1)} %get-tuple-element.177.refs_3_.refs_0_), channel_id=1, source_target_pairs={{0,1},{1,0},{2,3},{3,2},{4,5},{5,4},{6,7},{7,6},{8,9},{9,8},{10,11... | collective-permute-start | bytes 3145736 | tf_op jit(solution)/shard_map/ex4/ppermute | solution.py:477
  165.2 59.4 %collective-permute-start.30 = (bf16[1024,1024]{1,0:T(8,128)(2,1)}, bf16[1024,1024]{1,0:T(8,128)(2,1)}, u32[]{:S(2)}, u32[]{:S(2)}) collective-permute-start(bf16[1024,1024]{1,0:T(8,128)(2,1)} %get-tuple-element.183.refs_3_.refs_2_), channel_id=1, source_target_pairs={{0,8},{4,12},{8,0},{12,4},{1,9},{5,13},{9,1},{13,5},{2,10},{6,14},... | collective-permute-start | bytes 6291464 | tf_op jit(solution)/shard_map/wk2/ppermute | solution.py:477
  173.4 51.2 %collective-permute-start.31 = (bf16[1024,1024]{1,0:T(8,128)(2,1)}, bf16[1024,1024]{1,0:T(8,128)(2,1)}, u32[]{:S(2)}, u32[]{:S(2)}) collective-permute-start(bf16[1024,1024]{1,0:T(8,128)(2,1)} %get-tuple-element.202.refs_3_), channel_id=1, source_target_pairs={{0,16},{16,0},{1,17},{17,1},{2,18},{18,2},{3,19},{19,3},{4,20},{20... | collective-permute-start | bytes 6291464 | tf_op jit(solution)/shard_map/wv2/ppermute | solution.py:477
  175.2 55.7 %collective-permute-start.27 = (bf16[512,2048]{1,0:T(8,128)(2,1)}, bf16[512,2048]{1,0:T(8,128)(2,1)}, u32[]{:S(2)}, u32[]{:S(2)}) collective-permute-start(bf16[512,2048]{1,0:T(8,128)(2,1)} %get-tuple-element.188.refs_1_), channel_id=1, source_target_pairs={{1,0},{2,3},{5,4},{6,7},{9,8},{10,11},{13,12},{14,15},{17,16},{18,... | collective-permute-start | bytes 6291464 | tf_op jit(solution)/shard_map/fw2/ppermute | solution.py:477
  206.2 19.1 %collective-permute-start.29 = (f32[16,128]{1,0:T(8,128)}, f32[16,128]{1,0:T(8,128)S(1)}, u32[]{:S(2)}, u32[]{:S(2)}) collective-permute-start(f32[16,128]{1,0:T(8,128)} %get-tuple-element.199.refs_5_.refs_6_.refs_4_), channel_id=1, source_target_pairs={{0,3},{1,2},{2,1},{3,0},{4,7},{5,6},{6,5},{7,4},{8,11},{9,10},{10,... | collective-permute-start | bytes 24584 | tf_op jit(solution)/shard_map/rest/ppermute | solution.py:477
  210.2 31.1 %collective-permute-start.32 = (bf16[512,2048]{1,0:T(8,128)(2,1)}, bf16[512,2048]{1,0:T(8,128)(2,1)}, u32[]{:S(2)}, u32[]{:S(2)}) collective-permute-start(bf16[512,2048]{1,0:T(8,128)(2,1)} %get-tuple-element.209), channel_id=1, source_target_pairs={{1,2},{2,1},{5,6},{6,5},{9,10},{10,9},{13,14},{14,13},{17,18},{18,... | collective-permute-start | bytes 6291464 | tf_op jit(solution)/shard_map/mr4/ppermute | solution.py:477
  240.0 36.6 %collective-permute-start.37 = (bf16[256,2048]{1,0:T(8,128)(2,1)}, bf16[256,2048]{1,0:T(8,128)(2,1)}, u32[]{:S(2)}, u32[]{:S(2)}) collective-permute-start(bf16[256,2048]{1,0:T(8,128)(2,1)} %get-tuple-element.219), channel_id=1, source_target_pairs={{1,0},{2,3},{5,4},{6,7},{9,8},{10,11},{13,12},{14,15},{17,16},{18,... | collective-permute-start | bytes 3145736 | tf_op jit(solution)/shard_map/far3/ppermute | solution.py:477
  243.1 55.5 %collective-permute-start.36 = (bf16[256,2048]{1,0:T(8,128)(2,1)}, bf16[256,2048]{1,0:T(8,128)(2,1)}, u32[]{:S(2)}, u32[]{:S(2)}) collective-permute-start(bf16[256,2048]{1,0:T(8,128)(2,1)} %get-tuple-element.217), channel_id=1, source_target_pairs={{1,0},{2,3},{5,4},{6,7},{9,8},{10,11},{13,12},{14,15},{17,16},{18,... | collective-permute-start | bytes 3145736 | tf_op jit(solution)/shard_map/far4/ppermute | solution.py:477
  (22 other events, 180.0 us)

commit v4 on v3

--- a/solution.py
+++ b/solution.py
@@ -215,6 +215,10 @@
         ssq_out[j : j + 1, :rows] = jnp.sum(sums.T, axis=0, keepdims=True)
 
 
+def copy_kernel(given, out):
+    out[...] = given[...]
+
+
 def sums_kernel(step, *refs):
     out = refs[-1]
     if step == 0:
@@ -329,22 +333,9 @@
 
     @pl.when(info[4] == 1)
     def _():
-        loads = [
-            pltpu.make_async_copy(
-                slabs[c].at[pl.ds(s * sizes[c], sizes[c])], acts.at[s, pl.ds(starts[c], sizes[c])], act_sems.at[s, c]
-            )
-            for c in range(n)
-            for s in range(2)
-        ]
-        copies = [pltpu.make_async_copy(w, held.at[i], sems.at[i]) for i, w in enumerate(weights)]
-        for c in loads + copies:
-            c.start()
-        for c in loads:
-            c.wait()
+        loads = []
         for g in range(2):
-            total = None
             for i in range(4):
-                copies[4 * g + i].wait()
                 here = core if i < 2 else 1 - core
                 for t in range(2):
                     if g == 0:
@@ -352,10 +343,28 @@
                     else:
                         slab, chip = (y if i % 2 == 0 else 1 - y), t
                     at = pl.multiple_of((2 * chip + here) * share, 128)
-                    a = acts[slab, :, pl.ds(at, share)]
-                    w = held[4 * g + i, t * share : (t + 1) * share, :]
-                    term = jnp.dot(a, w, preferred_element_type=jnp.float32)
-                    total = term if total is None else total + term
+                    for c in range(n):
+                        row = pl.multiple_of(slab * sizes[c], 16)
+                        loads.append(
+                            pltpu.make_async_copy(
+                                slabs[c].at[pl.ds(row, sizes[c]), pl.ds(at, share)],
+                                acts.at[4 * g + i, pl.ds(starts[c], sizes[c]), pl.ds(t * share, share)],
+                                act_sems.at[4 * g + i, t, c],
+                            )
+                        )
+        copies = [pltpu.make_async_copy(w, held.at[i], sems.at[i]) for i, w in enumerate(weights)]
+        for i, c in enumerate(copies):
+            for load in loads[2 * n * i : 2 * n * (i + 1)]:
+                load.start()
+            c.start()
+        for g in range(2):
+            total = None
+            for i in range(4 * g, 4 * g + 4):
+                for load in loads[2 * n * i : 2 * n * (i + 1)]:
+                    load.wait()
+                copies[i].wait()
+                term = jnp.dot(acts[i], held[i], preferred_element_type=jnp.float32)
+                total = term if total is None else total + term
             out[:, g * cols : (g + 1) * cols] = total.astype(jnp.bfloat16)
 
 
@@ -573,9 +582,9 @@
             [bf16((total, 2 * cols))],
             [VMEM],
             [
-                pltpu.VMEM((2, total, width), jnp.bfloat16),
+                pltpu.VMEM((8, total, 2 * share), jnp.bfloat16),
                 pltpu.VMEM((8, *reached[0].shape), jnp.bfloat16),
-                dma((2, len(sizes))),
+                dma((8, 2, len(sizes))),
                 dma((8,)),
             ],
         )
@@ -662,26 +671,27 @@
         [dma((3, 2))],
     )
 
+    def hop(k, pack):
+        hopped = move("h%d" % k, pack, swap[2])
+        came[k + 1] = {2: (hopped, 0), 3: (hopped, BLOCK)}
+
+    prep(1)
+    pass_own(1)
+    hop(1, packs[0])
     cuts = call(
         cut_kernel, "cut", (key_weight, value_weight), [HBM] * 2, [bf16((share, cols))] * 2, [VMEM] * 2, [dma((2,))]
     )
 
-    def hop(k, pack):
-        hopped = move("h%d" % k, pack, swap[2])
-        came[k + 1] = {2: (hopped, 0), 3: (hopped, BLOCK)}
-
-    prep(1)
-    pass_own(1)
-    pack, lent_k = pin(packs[0], cuts[0])
-    hop(1, pack)
-    lent_k = move("ink", lent_k, inward)
+    lent_k = move("ink", cuts[0], inward)
     relay(0)
     relay(1)
     prep(2)
     pass_own(2)
     (pack,) = pin(packs[1])
     hop(2, pack)
-    (positions,) = pin(positions)
+    (positions,) = call(
+        copy_kernel, "copy", (positions,), [VMEM], [jax.ShapeDtypeStruct(positions.shape, jnp.int32)], [VMEM]
+    )
     cosine, sine = pin(*rope_tables(positions))
     mr[0], lent_k, lent_v = pin(mr[0], lent_k, cuts[1])
     hand(0)

time: 305 us -> 301 us (0.987)
  waiting for transfers between devices: 85.5 us -> 81.5 us
    ppermute x38, waiting for transfers between devices: 85.5 us -> 81.5 us  [move(): return lax.ppermute(array, *way)]
    pallas_call x43 -> x42, Pallas kernels: 145 us -> 147 us  [__call__(): pl.pallas_call(body, out_shape=tuple(outs) + (TOKEN,), input_output_alias...]
  transfers between devices with their start and end apart: 38 -> 38, of which waited for: 16 -> 15; matrix products, arithmetic and copies ran while one was open for 2% -> 2% of each run, Pallas kernels for 44% -> 45%
where the time goes in v4:
time: 301 us; the launch traced here: 300 us
  Pallas kernels  147 us (49%)
  waiting for transfers between devices  81.5 us (27%)
  starting transfers between devices  61.9 us (21%)
  other arithmetic  4.53 us (2%)
  local copies, waits for them, and re-layouts  3.98 us (1%)
    pallas_call x42, Pallas kernels, __call__(): pl.pallas_call(body, out_shape=tuple(outs) + (TOKEN,), input_output_alias...  147 us
    ppermute x38, waiting for transfers between devices, move(): return lax.ppermute(array, *way)  81.5 us
    ppermute x38, starting transfers between devices, move(): return lax.ppermute(array, *way)  61.9 us
  transfers between devices with their start and end apart: 38, of which 15 were waited for; matrix products, arithmetic and copies ran while one was open for 2% of the time, Pallas kernels for 45%

profile of v4, /device:TPU:0, one launch (start us, length us, event | category | flops | bytes accessed | tf_op | source)
XLA Modules:
  0.0 300.0 jit_solution(486101901175269732)
XLA Ops:
  12.5 4.6 %send.3 = (bf16[64,2048]{1,0:T(8,128)(2,1)}, bf16[64,2048]{1,0:T(8,128)(2,1)}, bf16[768,2048]{1,0:T(8,128)(2,1)}, s32[8,128]{1,0:T(8,128)}) custom-call(s32[1,16]{1,0:T(1,128)} %refs_0_.9, bf16[2048,2048]{1,0:T(8,128)(2,1)} %bitcast.13, s32[8,128]{1,0:T(8,128)} %get-tuple-element.115.refs_2_), custom_call_target="tpu_custom_call" | custom-call | flops 4000000000 | bytes 1 | tf_op jit(solution)/shard_map/send/pallas_call | solution.py:68
  26.8 4.3 %pack.1 = (bf16[256,2048]{1,0:T(8,128)(2,1)}, bf16[256,2048]{1,0:T(8,128)(2,1)}, bf16[256,2048]{1,0:T(8,128)(2,1)}, s32[8,128]{1,0:T(8,128)}) custom-call(s32[1,16]{1,0:T(1,128)} %refs_0_.9, bf16[2048,2048]{1,0:T(8,128)(2,1)} %bitcast.15, bf16[768,2048]{1,0:T(8,128)(2,1)} %collective-permute-done.4.refs_2_.refs_3_.refs_4_.refs_5_, ...), custom_call_target="tpu_custom_call" | custom-call | flops 4000000000 | bytes 1 | tf_op jit(solution)/shard_map/pack/pallas_call | solution.py:68
  45.7 6.4 %collective-permute-start.15 = (bf16[512,1024]{1,0:T(8,128)(2,1)}, bf16[512,1024]{1,0:T(8,128)(2,1)}, u32[]{:S(2)}, u32[]{:S(2)}) collective-permute-start(bf16[512,1024]{1,0:T(8,128)(2,1)} %get-tuple-element.136), channel_id=1, source_target_pairs={{0,1},{3,2},{4,5},{7,6},{8,9},{11,10},{12,13},{15,14},{16,17},{19,... | collective-permute-start | bytes 3145736 | tf_op jit(solution)/shard_map/ink/ppermute | solution.py:486
  56.0 6.5 %collective-permute-done.9.refs_8_.refs_9_.refs_10_.refs_11_ = bf16[256,2048]{1,0:T(8,128)(2,1)} collective-permute-done((bf16[256,2048]{1,0:T(8,128)(2,1)}, bf16[256,2048]{1,0:T(8,128)(2,1)}, u32[]{:S(2)}, u32[]{:S(2)}) %collective-permute-start.9) | collective-permute-done | bytes 1048608 | tf_op jit(solution)/shard_map/h1/ppermute | solution.py:486
  76.2 6.5 %collective-permute-start.18 = (bf16[512,1024]{1,0:T(8,128)(2,1)}, bf16[512,1024]{1,0:T(8,128)(2,1)}, u32[]{:S(2)}, u32[]{:S(2)}) collective-permute-start(bf16[512,1024]{1,0:T(8,128)(2,1)} %get-tuple-element.147), channel_id=1, source_target_pairs={{0,1},{3,2},{4,5},{7,6},{8,9},{11,10},{12,13},{15,14},{16,17},{19,... | collective-permute-start | bytes 3145736 | tf_op jit(solution)/shard_map/inv/ppermute | solution.py:486
  82.7 12.3 %near.5 = (f32[256,2048]{1,0:T(8,128)}, s32[8,128]{1,0:T(8,128)}) custom-call(s32[8]{0:T(128)} %stack.39.refs_0_, bf16[128,2048]{1,0:T(8,128)(2,1)} %get-tuple-element.127.refs_0_.refs_1_, bf16[128,2048]{1,0:T(8,128)(2,1)} %copy-done.2, bf16[128,2048]{1,0:T(8,128)(2,1)} %get-tuple-element.126.refs_0_.refs_3_, ...), custom_call_target="tpu_custom_call" | custom-call | flops 4000000000 | bytes 1 | tf_op jit(solution)/shard_map/near/pallas_call | solution.py:68
  102.2 3.4 %prep.8 = (bf16[256,2048]{1,0:T(8,128)(2,1)}, f32[2,128]{1,0:T(2,128)}, s32[8,128]{1,0:T(8,128)}) custom-call(s32[8,4]{1,0:T(8,128)} %get-tuple-element.113.refs_0_, bf16[2048,2048]{1,0:T(8,128)(2,1)} %bitcast.18, bf16[128,2048]{1,0:T(8,128)(2,1)} %copy-done, bf16[768,2048]{1,0:T(8,128)(2,1)} %collective-permute-done.4.refs_2_.refs_3_.refs_4_.refs_5_, ...), custom_call_target="tpu_custom_call" | custom-call | flops 4000000000 | bytes 1 | tf_op jit(solution)/shard_map/prep/pallas_call | solution.py:68
  108.8 7.8 %collective-permute-done.17.refs_0_ = bf16[256,2048]{1,0:T(8,128)(2,1)} collective-permute-done((bf16[256,2048]{1,0:T(8,128)(2,1)}, bf16[256,2048]{1,0:T(8,128)(2,1)}, u32[]{:S(2)}, u32[]{:S(2)}) %collective-permute-start.17) | collective-permute-done | bytes 1048608 | tf_op jit(solution)/shard_map/fw0/ppermute | solution.py:486
  122.7 12.4 %near.6 = (f32[256,2048]{1,0:T(8,128)}, s32[8,128]{1,0:T(8,128)}) custom-call(s32[8]{0:T(128)} %stack.39.refs_0_, bf16[256,2048]{1,0:T(8,128)(2,1)} %get-tuple-element.134.refs_0_.refs_1_, bf16[256,2048]{1,0:T(8,128)(2,1)} %collective-permute-done.13.refs_1_.refs_2_, bf16[8192,1024]{1,0:T(8,128)(2,1)} %refs_5_.7, bf16[8192,1024]{1,0:T(8,128)(2,1)} %refs_6_.7, ...), custom_call_target="tpu_custom_call" | custom-call | flops 4000000000 | bytes 1 | tf_op jit(solution)/shard_map/near/pallas_call | solution.py:68
  135.1 6.2 %collective-permute-done.16.refs_1_.refs_2_ = bf16[256,2048]{1,0:T(8,128)(2,1)} collective-permute-done((bf16[256,2048]{1,0:T(8,128)(2,1)}, bf16[256,2048]{1,0:T(8,128)(2,1)}, u32[]{:S(2)}, u32[]{:S(2)}) %collective-permute-start.16) | collective-permute-done | bytes 1048608 | tf_op jit(solution)/shard_map/ex3/ppermute | solution.py:486
  146.7 3.3 %prep.9 = (bf16[256,2048]{1,0:T(8,128)(2,1)}, f32[2,128]{1,0:T(2,128)}, s32[8,128]{1,0:T(8,128)}) custom-call(s32[8,4]{1,0:T(8,128)} %get-tuple-element.113.refs_0_, bf16[2048,2048]{1,0:T(8,128)(2,1)} %bitcast.19, bf16[128,2048]{1,0:T(8,128)(2,1)} %copy-done, bf16[768,2048]{1,0:T(8,128)(2,1)} %collective-permute-done.4.refs_2_.refs_3_.refs_4_.refs_5_, ...), custom_call_target="tpu_custom_call" | custom-call | flops 4000000000 | bytes 1 | tf_op jit(solution)/shard_map/prep/pallas_call | solution.py:68
  151.3 7.1 %collective-permute-start.24 = (f32[16,128]{1,0:T(8,128)}, f32[16,128]{1,0:T(8,128)S(1)}, u32[]{:S(2)}, u32[]{:S(2)}) collective-permute-start(f32[16,128]{1,0:T(8,128)} %get-tuple-element.173.refs_0_), channel_id=1, source_target_pairs={{0,1},{1,0},{2,3},{3,2},{4,5},{5,4},{6,7},{7,6},{8,9},{9,8},{10,11... | collective-permute-start | bytes 24584 | tf_op jit(solution)/shard_map/half/ppermute | solution.py:486
  160.3 3.6 %join.2 = (bf16[1024,1024]{1,0:T(8,128)(2,1)}, s32[8,128]{1,0:T(8,128)}) custom-call(s32[8]{0:T(128)} %stack.39.refs_0_, bf16[512,1024]{1,0:T(8,128)(2,1)} %get-tuple-element.175.refs_1_, bf16[512,1024]{1,0:T(8,128)(2,1)} %collective-permute-done.26.refs_2_, s32[8,128]{1,0:T(8,128)} %get-tuple-element.176.refs_3_), custom_call_target="tpu_custom_call" | custom-call | flops 4000000000 | bytes 1 | tf_op jit(solution)/shard_map/join/pallas_call | solution.py:68
  165.8 6.4 %join.3 = (bf16[1024,1024]{1,0:T(8,128)(2,1)}, bf16[2048,1024]{1,0:T(8,128)(2,1)}, s32[8,128]{1,0:T(8,128)}) custom-call(s32[8]{0:T(128)} %stack.39.refs_0_, bf16[512,1024]{1,0:T(8,128)(2,1)} %get-tuple-element.174.refs_1_, bf16[512,1024]{1,0:T(8,128)(2,1)} %collective-permute-done.25.refs_2_, bf16[1024,1024]{1,0:T(8,128)(2,1)} %get-tuple-element.177.refs_3_.refs_2_, ...), custom_call_target="tpu_custom_call" | custom-call | flops 4000000000 | bytes 1 | tf_op jit(solution)/shard_map/join/pallas_call | solution.py:68
  175.8 10.9 %collective-permute-done.23.refs_4_.refs_1_ = bf16[256,2048]{1,0:T(8,128)(2,1)} collective-permute-done((bf16[256,2048]{1,0:T(8,128)(2,1)}, bf16[256,2048]{1,0:T(8,128)(2,1)}, u32[]{:S(2)}, u32[]{:S(2)}) %collective-permute-start.23) | collective-permute-done | bytes 1048608 | tf_op jit(solution)/shard_map/ex4/ppermute | solution.py:486
  186.7 16.8 %near.7 = (f32[512,2048]{1,0:T(8,128)}, s32[8,128]{1,0:T(8,128)}) custom-call(s32[8]{0:T(128)} %stack.39.refs_0_, bf16[256,2048]{1,0:T(8,128)(2,1)} %get-tuple-element.145.refs_0_.refs_1_, bf16[256,2048]{1,0:T(8,128)(2,1)} %collective-permute-done.16.refs_1_.refs_2_, bf16[256,2048]{1,0:T(8,128)(2,1)} %get-tuple-element.171.refs_3_.refs_0_, ...), custom_call_target="tpu_custom_call" | custom-call | flops 4000000000 | bytes 1 | tf_op jit(solution)/shard_map/near/pallas_call | solution.py:68
  212.3 12.3 %near.8 = (f32[256,2048]{1,0:T(8,128)}, s32[8,128]{1,0:T(8,128)}) custom-call(s32[8]{0:T(128)} %stack.39.refs_0_, bf16[256,2048]{1,0:T(8,128)(2,1)} %get-tuple-element.146.refs_1_, bf16[256,2048]{1,0:T(8,128)(2,1)} %get-tuple-element.184.refs_2_, bf16[256,2048]{1,0:T(8,128)(2,1)} %get-tuple-element.154.refs_3_, ...), custom_call_target="tpu_custom_call" | custom-call | flops 4000000000 | bytes 1 | tf_op jit(solution)/shard_map/near/pallas_call | solution.py:68
  225.9 4.5 %finish.3 = (bf16[1024,1024]{1,0:T(8,128)(2,1)}, bf16[1024,1024]{1,0:T(8,128)(2,1)}, s32[8,128]{1,0:T(8,128)}) custom-call(s32[8,4]{1,0:T(8,128)} %get-tuple-element.113.refs_0_, f32[256,2048]{1,0:T(8,128)} %get-tuple-element.183.refs_1_.refs_3_, f32[256,2048]{1,0:T(8,128)} %get-tuple-element.192.refs_2_.refs_4_, ...), custom_call_target="tpu_custom_call" | custom-call | flops 4000000000 | bytes 1 | tf_op jit(solution)/shard_map/finish/pallas_call | solution.py:68
  230.4 4.8 %collective-permute-done.34.refs_7_ = bf16[1024,1024]{1,0:T(8,128)(2,1)} collective-permute-done((bf16[1024,1024]{1,0:T(8,128)(2,1)}, bf16[1024,1024]{1,0:T(8,128)(2,1)}, u32[]{:S(2)}, u32[]{:S(2)}) %collective-permute-start.34) | collective-permute-done | bytes 2097184 | tf_op jit(solution)/shard_map/core/ppermute | solution.py:486
  244.9 14.0 %near.9 = (f32[768,2048]{1,0:T(8,128)}, s32[8,128]{1,0:T(8,128)}) custom-call(s32[8]{0:T(128)} %stack.39.refs_0_, bf16[512,2048]{1,0:T(8,128)(2,1)} %get-tuple-element.182.refs_1_, bf16[512,2048]{1,0:T(8,128)(2,1)} %get-tuple-element.201.refs_2_, bf16[512,2048]{1,0:T(8,128)(2,1)} %get-tuple-element.202.refs_1_.refs_3_, ...), custom_call_target="tpu_custom_call" | custom-call | flops 4000000000 | bytes 1 | tf_op jit(solution)/shard_map/near/pallas_call | solution.py:68
  258.9 13.9 %collective-permute-done.37.refs_5_ = bf16[256,2048]{1,0:T(8,128)(2,1)} collective-permute-done((bf16[256,2048]{1,0:T(8,128)(2,1)}, bf16[256,2048]{1,0:T(8,128)(2,1)}, u32[]{:S(2)}, u32[]{:S(2)}) %collective-permute-start.37) | collective-permute-done | bytes 1048608 | tf_op jit(solution)/shard_map/far3/ppermute | solution.py:486
  272.7 6.7 %finish.4 = (bf16[1024,1024]{1,0:T(8,128)(2,1)}, bf16[1024,1024]{1,0:T(8,128)(2,1)}, s32[8,128]{1,0:T(8,128)}) custom-call(s32[8,4]{1,0:T(8,128)} %get-tuple-element.113.refs_0_, f32[256,2048]{1,0:T(8,128)} %get-tuple-element.212.refs_1_, f32[768,2048]{1,0:T(8,128)} %get-tuple-element.210.refs_2_.refs_4_, ...), custom_call_target="tpu_custom_call", output_to_operand_aliasing={{0}: (12, {}), {1}: (13, {})} | custom-call | flops 4000000000 | bytes 1 | tf_op jit(solution)/shard_map/finish/pallas_call | solution.py:68
  279.5 15.3 %collective-permute-done.36.refs_3_ = bf16[256,2048]{1,0:T(8,128)(2,1)} collective-permute-done((bf16[256,2048]{1,0:T(8,128)(2,1)}, bf16[256,2048]{1,0:T(8,128)(2,1)}, u32[]{:S(2)}, u32[]{:S(2)}) %collective-permute-start.36) | collective-permute-done | bytes 1048608 | tf_op jit(solution)/shard_map/far4/ppermute | solution.py:486
  294.7 5.1 %finish.5 = (bf16[1024,1024]{1,0:T(8,128)(2,1)}, bf16[1024,1024]{1,0:T(8,128)(2,1)}, s32[8,128]{1,0:T(8,128)}) custom-call(s32[8,4]{1,0:T(8,128)} %get-tuple-element.113.refs_0_, f32[512,2048]{1,0:T(8,128)} %get-tuple-element.181.refs_3_.refs_1_, f32[768,2048]{1,0:T(8,128)} %get-tuple-element.210.refs_2_.refs_4_, ...), custom_call_target="tpu_custom_call", output_to_operand_aliasing={{0}: (10, {}), {1}: (11, {})} | custom-call | flops 4000000000 | bytes 1 | tf_op jit(solution)/shard_map/finish/pallas_call | solution.py:68
  (117 shorter events, 103.6 us)
Async XLA Ops:
  36.6 25.9 %collective-permute-start.9 = (bf16[256,2048]{1,0:T(8,128)(2,1)}, bf16[256,2048]{1,0:T(8,128)(2,1)}, u32[]{:S(2)}, u32[]{:S(2)}) collective-permute-start(bf16[256,2048]{1,0:T(8,128)(2,1)} %get-tuple-element.123), channel_id=1, source_target_pairs={{0,8},{4,12},{8,0},{12,4},{1,9},{5,13},{9,1},{13,5},{2,10},{6,14},... | collective-permute-start | bytes 3145736 | tf_op jit(solution)/shard_map/h1/ppermute | solution.py:486
  44.0 28.9 %collective-permute-start.14 = (bf16[256,2048]{1,0:T(8,128)(2,1)}, bf16[256,2048]{1,0:T(8,128)(2,1)}, u32[]{:S(2)}, u32[]{:S(2)}) collective-permute-start(bf16[256,2048]{1,0:T(8,128)(2,1)} %get-tuple-element.135), channel_id=1, source_target_pairs={{1,2},{2,1},{5,6},{6,5},{9,10},{10,9},{13,14},{14,13},{17,18},{18,... | collective-permute-start | bytes 3145736 | tf_op jit(solution)/shard_map/mr0/ppermute | solution.py:486
  45.7 29.2 %collective-permute-start.15 = (bf16[512,1024]{1,0:T(8,128)(2,1)}, bf16[512,1024]{1,0:T(8,128)(2,1)}, u32[]{:S(2)}, u32[]{:S(2)}) collective-permute-start(bf16[512,1024]{1,0:T(8,128)(2,1)} %get-tuple-element.136), channel_id=1, source_target_pairs={{0,1},{3,2},{4,5},{7,6},{8,9},{11,10},{12,13},{15,14},{16,17},{19,... | collective-permute-start | bytes 3145736 | tf_op jit(solution)/shard_map/ink/ppermute | solution.py:486
  54.3 53.9 %collective-permute-start.19 = (bf16[256,2048]{1,0:T(8,128)(2,1)}, bf16[256,2048]{1,0:T(8,128)(2,1)}, u32[]{:S(2)}, u32[]{:S(2)}) collective-permute-start(bf16[256,2048]{1,0:T(8,128)(2,1)} %get-tuple-element.149), channel_id=1, source_target_pairs={{1,2},{2,1},{5,6},{6,5},{9,10},{10,9},{13,14},{14,13},{17,18},{18,... | collective-permute-start | bytes 3145736 | tf_op jit(solution)/shard_map/mr1/ppermute | solution.py:486
  67.7 29.6 %collective-permute-start.13 = (bf16[256,2048]{1,0:T(8,128)(2,1)}, bf16[256,2048]{1,0:T(8,128)(2,1)}, u32[]{:S(2)}, u32[]{:S(2)}) collective-permute-start(bf16[256,2048]{1,0:T(8,128)(2,1)} %get-tuple-element.134.refs_0_.refs_1_), channel_id=1, source_target_pairs={{0,1},{1,0},{2,3},{3,2},{4,5},{5,4},{6,7},{7,6},{8,9},{9,8},{10,11... | collective-permute-start | bytes 3145736 | tf_op jit(solution)/shard_map/ex2/ppermute | solution.py:486
  68.1 34.2 %collective-permute-start.12 = (bf16[256,2048]{1,0:T(8,128)(2,1)}, bf16[256,2048]{1,0:T(8,128)(2,1)}, u32[]{:S(2)}, u32[]{:S(2)}) collective-permute-start(bf16[256,2048]{1,0:T(8,128)(2,1)} %get-tuple-element.133), channel_id=1, source_target_pairs={{0,8},{4,12},{8,0},{12,4},{1,9},{5,13},{9,1},{13,5},{2,10},{6,14},... | collective-permute-start | bytes 3145736 | tf_op jit(solution)/shard_map/h2/ppermute | solution.py:486
  74.9 41.7 %collective-permute-start.17 = (bf16[256,2048]{1,0:T(8,128)(2,1)}, bf16[256,2048]{1,0:T(8,128)(2,1)}, u32[]{:S(2)}, u32[]{:S(2)}) collective-permute-start(bf16[256,2048]{1,0:T(8,128)(2,1)} %get-tuple-element.146.refs_1_), channel_id=1, source_target_pairs={{1,0},{2,3},{5,4},{6,7},{9,8},{10,11},{13,12},{14,15},{17,16},{18,... | collective-permute-start | bytes 3145736 | tf_op jit(solution)/shard_map/fw0/ppermute | solution.py:486
  76.2 43.7 %collective-permute-start.18 = (bf16[512,1024]{1,0:T(8,128)(2,1)}, bf16[512,1024]{1,0:T(8,128)(2,1)}, u32[]{:S(2)}, u32[]{:S(2)}) collective-permute-start(bf16[512,1024]{1,0:T(8,128)(2,1)} %get-tuple-element.147), channel_id=1, source_target_pairs={{0,1},{3,2},{4,5},{7,6},{8,9},{11,10},{12,13},{15,14},{16,17},{19,... | collective-permute-start | bytes 3145736 | tf_op jit(solution)/shard_map/inv/ppermute | solution.py:486
  100.2 44.5 %collective-permute-start.22 = (bf16[512,2048]{1,0:T(8,128)(2,1)}, bf16[512,2048]{1,0:T(8,128)(2,1)}, u32[]{:S(2)}, u32[]{:S(2)}) collective-permute-start(bf16[512,2048]{1,0:T(8,128)(2,1)} %get-tuple-element.156), channel_id=1, source_target_pairs={{1,2},{2,1},{5,6},{6,5},{9,10},{10,9},{13,14},{14,13},{17,18},{18,... | collective-permute-start | bytes 6291464 | tf_op jit(solution)/shard_map/mr2/ppermute | solution.py:486
  105.7 35.6 %collective-permute-start.16 = (bf16[256,2048]{1,0:T(8,128)(2,1)}, bf16[256,2048]{1,0:T(8,128)(2,1)}, u32[]{:S(2)}, u32[]{:S(2)}) collective-permute-start(bf16[256,2048]{1,0:T(8,128)(2,1)} %get-tuple-element.145.refs_0_.refs_1_), channel_id=1, source_target_pairs={{0,1},{1,0},{2,3},{3,2},{4,5},{5,4},{6,7},{7,6},{8,9},{9,8},{10,11... | collective-permute-start | bytes 3145736 | tf_op jit(solution)/shard_map/ex3/ppermute | solution.py:486
  108.2 38.5 %collective-permute-start.21 = (bf16[256,2048]{1,0:T(8,128)(2,1)}, bf16[256,2048]{1,0:T(8,128)(2,1)}, u32[]{:S(2)}, u32[]{:S(2)}) collective-permute-start(bf16[256,2048]{1,0:T(8,128)(2,1)} %get-tuple-element.155), channel_id=1, source_target_pairs={{0,8},{4,12},{8,0},{12,4},{1,9},{5,13},{9,1},{13,5},{2,10},{6,14},... | collective-permute-start | bytes 3145736 | tf_op jit(solution)/shard_map/h3/ppermute | solution.py:486
  119.8 40.5 %collective-permute-start.20 = (bf16[256,2048]{1,0:T(8,128)(2,1)}, bf16[256,2048]{1,0:T(8,128)(2,1)}, u32[]{:S(2)}, u32[]{:S(2)}) collective-permute-start(bf16[256,2048]{1,0:T(8,128)(2,1)} %get-tuple-element.154.refs_3_), channel_id=1, source_target_pairs={{1,0},{2,3},{5,4},{6,7},{9,8},{10,11},{13,12},{14,15},{17,16},{18,... | collective-permute-start | bytes 3145736 | tf_op jit(solution)/shard_map/fw1/ppermute | solution.py:486
  121.1 39.2 %collective-permute-start.26 = (bf16[512,1024]{1,0:T(8,128)(2,1)}, bf16[512,1024]{1,0:T(8,128)(2,1)}, u32[]{:S(2)}, u32[]{:S(2)}) collective-permute-start(bf16[512,1024]{1,0:T(8,128)(2,1)} %get-tuple-element.175.refs_1_), channel_id=1, source_target_pairs={{0,16},{16,0},{1,17},{17,1},{2,18},{18,2},{3,19},{19,3},{4,20},{20... | collective-permute-start | bytes 3145736 | tf_op jit(solution)/shard_map/wk1/ppermute | solution.py:486
  141.3 24.5 %collective-permute-start.25 = (bf16[512,1024]{1,0:T(8,128)(2,1)}, bf16[512,1024]{1,0:T(8,128)(2,1)}, u32[]{:S(2)}, u32[]{:S(2)}) collective-permute-start(bf16[512,1024]{1,0:T(8,128)(2,1)} %get-tuple-element.174.refs_1_), channel_id=1, source_target_pairs={{0,8},{4,12},{8,0},{12,4},{1,9},{5,13},{9,1},{13,5},{2,10},{6,14},... | collective-permute-start | bytes 3145736 | tf_op jit(solution)/shard_map/wv1/ppermute | solution.py:486
  144.7 58.9 %collective-permute-start.28 = (bf16[512,2048]{1,0:T(8,128)(2,1)}, bf16[512,2048]{1,0:T(8,128)(2,1)}, u32[]{:S(2)}, u32[]{:S(2)}) collective-permute-start(bf16[512,2048]{1,0:T(8,128)(2,1)} %get-tuple-element.187), channel_id=1, source_target_pairs={{1,2},{2,1},{5,6},{6,5},{9,10},{10,9},{13,14},{14,13},{17,18},{18,... | collective-permute-start | bytes 6291464 | tf_op jit(solution)/shard_map/mr3/ppermute | solution.py:486
  151.3 22.5 %collective-permute-start.24 = (f32[16,128]{1,0:T(8,128)}, f32[16,128]{1,0:T(8,128)S(1)}, u32[]{:S(2)}, u32[]{:S(2)}) collective-permute-start(f32[16,128]{1,0:T(8,128)} %get-tuple-element.173.refs_0_), channel_id=1, source_target_pairs={{0,1},{1,0},{2,3},{3,2},{4,5},{5,4},{6,7},{7,6},{8,9},{9,8},{10,11... | collective-permute-start | bytes 24584 | tf_op jit(solution)/shard_map/half/ppermute | solution.py:486
  160.3 26.4 %collective-permute-start.23 = (bf16[256,2048]{1,0:T(8,128)(2,1)}, bf16[256,2048]{1,0:T(8,128)(2,1)}, u32[]{:S(2)}, u32[]{:S(2)}) collective-permute-start(bf16[256,2048]{1,0:T(8,128)(2,1)} %get-tuple-element.171.refs_3_.refs_0_), channel_id=1, source_target_pairs={{0,1},{1,0},{2,3},{3,2},{4,5},{5,4},{6,7},{7,6},{8,9},{9,8},{10,11... | collective-permute-start | bytes 3145736 | tf_op jit(solution)/shard_map/ex4/ppermute | solution.py:486
  163.9 60.8 %collective-permute-start.30 = (bf16[1024,1024]{1,0:T(8,128)(2,1)}, bf16[1024,1024]{1,0:T(8,128)(2,1)}, u32[]{:S(2)}, u32[]{:S(2)}) collective-permute-start(bf16[1024,1024]{1,0:T(8,128)(2,1)} %get-tuple-element.177.refs_3_.refs_2_), channel_id=1, source_target_pairs={{0,8},{4,12},{8,0},{12,4},{1,9},{5,13},{9,1},{13,5},{2,10},{6,14},... | collective-permute-start | bytes 6291464 | tf_op jit(solution)/shard_map/wk2/ppermute | solution.py:486
  172.2 52.5 %collective-permute-start.31 = (bf16[1024,1024]{1,0:T(8,128)(2,1)}, bf16[1024,1024]{1,0:T(8,128)(2,1)}, u32[]{:S(2)}, u32[]{:S(2)}) collective-permute-start(bf16[1024,1024]{1,0:T(8,128)(2,1)} %get-tuple-element.196.refs_3_), channel_id=1, source_target_pairs={{0,16},{16,0},{1,17},{17,1},{2,18},{18,2},{3,19},{19,3},{4,20},{20... | collective-permute-start | bytes 6291464 | tf_op jit(solution)/shard_map/wv2/ppermute | solution.py:486
  174.4 56.1 %collective-permute-start.27 = (bf16[512,2048]{1,0:T(8,128)(2,1)}, bf16[512,2048]{1,0:T(8,128)(2,1)}, u32[]{:S(2)}, u32[]{:S(2)}) collective-permute-start(bf16[512,2048]{1,0:T(8,128)(2,1)} %get-tuple-element.182.refs_1_), channel_id=1, source_target_pairs={{1,0},{2,3},{5,4},{6,7},{9,8},{10,11},{13,12},{14,15},{17,16},{18,... | collective-permute-start | bytes 6291464 | tf_op jit(solution)/shard_map/fw2/ppermute | solution.py:486
  204.9 20.4 %collective-permute-start.29 = (f32[16,128]{1,0:T(8,128)}, f32[16,128]{1,0:T(8,128)S(1)}, u32[]{:S(2)}, u32[]{:S(2)}) collective-permute-start(f32[16,128]{1,0:T(8,128)} %get-tuple-element.193.refs_5_.refs_6_.refs_4_), channel_id=1, source_target_pairs={{0,3},{1,2},{2,1},{3,0},{4,7},{5,6},{6,5},{7,4},{8,11},{9,10},{10,... | collective-permute-start | bytes 24584 | tf_op jit(solution)/shard_map/rest/ppermute | solution.py:486
  210.2 31.2 %collective-permute-start.32 = (bf16[512,2048]{1,0:T(8,128)(2,1)}, bf16[512,2048]{1,0:T(8,128)(2,1)}, u32[]{:S(2)}, u32[]{:S(2)}) collective-permute-start(bf16[512,2048]{1,0:T(8,128)(2,1)} %get-tuple-element.203), channel_id=1, source_target_pairs={{1,2},{2,1},{5,6},{6,5},{9,10},{10,9},{13,14},{14,13},{17,18},{18,... | collective-permute-start | bytes 6291464 | tf_op jit(solution)/shard_map/mr4/ppermute | solution.py:486
  240.2 32.6 %collective-permute-start.37 = (bf16[256,2048]{1,0:T(8,128)(2,1)}, bf16[256,2048]{1,0:T(8,128)(2,1)}, u32[]{:S(2)}, u32[]{:S(2)}) collective-permute-start(bf16[256,2048]{1,0:T(8,128)(2,1)} %get-tuple-element.213), channel_id=1, source_target_pairs={{1,0},{2,3},{5,4},{6,7},{9,8},{10,11},{13,12},{14,15},{17,16},{18,... | collective-permute-start | bytes 3145736 | tf_op jit(solution)/shard_map/far3/ppermute | solution.py:486
  243.3 51.4 %collective-permute-start.36 = (bf16[256,2048]{1,0:T(8,128)(2,1)}, bf16[256,2048]{1,0:T(8,128)(2,1)}, u32[]{:S(2)}, u32[]{:S(2)}) collective-permute-start(bf16[256,2048]{1,0:T(8,128)(2,1)} %get-tuple-element.211), channel_id=1, source_target_pairs={{1,0},{2,3},{5,4},{6,7},{9,8},{10,11},{13,12},{14,15},{17,16},{18,... | collective-permute-start | bytes 3145736 | tf_op jit(solution)/shard_map/far4/ppermute | solution.py:486
  (23 other events, 180.2 us)

commit v5 on v4

--- a/solution.py
+++ b/solution.py
@@ -14,7 +14,7 @@
 EPS = 1e-06
 MIB = 1 << 20
 VMEM_LIMIT = 63 * MIB
-COST = 4 * 10**9
+COST = 35 * 10**8
 FAR = 10**11
 HBM = pl.BlockSpec(memory_space=pltpu.HBM)
 SMEM = pl.BlockSpec(memory_space=pltpu.SMEM)
@@ -730,13 +730,13 @@
     came_k, came_v, joined = pin(came_k, came_v, joined)
     beside_w = [move("core", w, swap[1]) for w in (joined, came_k, came_v)]
     total_squares = (squares, rest)
-    finish(0, 1)
+    near((3,), 2, 4)
     (fw[2],) = pin(fw[2], cost=FAR)
     reached = (joined_k, joined_v, came_k, came_v, *beside_w)
     reach(3)
     reach(4)
-    near((2, 3, 4), 2, 4)
-    finish(2, 3)
+    near((2, 4), 2, 4)
+    finish(0, 1, 2, 3)
     finish(4)
     return tuple(done)
 

time: 301 us -> 301 us (level)
  transfers between devices with their start and end apart: 38 -> 38, of which waited for: 15 -> 17; matrix products, arithmetic and copies ran while one was open for 2% -> 2% of each run, Pallas kernels for 45% -> 45%
where the time goes in v5:
time: 301 us; the launch traced here: 299 us
  Pallas kernels  148 us (49%)
  waiting for transfers between devices  78.5 us (26%)
  starting transfers between devices  63.7 us (21%)
  other arithmetic  3.93 us (1%)
  local copies, waits for them, and re-layouts  3.48 us (1%)
    pallas_call x42, Pallas kernels, __call__(): pl.pallas_call(body, out_shape=tuple(outs) + (TOKEN,), input_output_alias...  148 us
    ppermute x38, waiting for transfers between devices, move(): return lax.ppermute(array, *way)  78.5 us
    ppermute x38, starting transfers between devices, move(): return lax.ppermute(array, *way)  63.7 us
  transfers between devices with their start and end apart: 38, of which 17 were waited for; matrix products, arithmetic and copies ran while one was open for 2% of the time, Pallas kernels for 45%

profile of v5, /device:TPU:0, one launch (start us, length us, event | category | flops | bytes accessed | tf_op | source)
XLA Modules:
  0.0 299.0 jit_solution(14382755095186972043)
XLA Ops:
  11.9 4.6 %send.3 = (bf16[64,2048]{1,0:T(8,128)(2,1)}, bf16[64,2048]{1,0:T(8,128)(2,1)}, bf16[768,2048]{1,0:T(8,128)(2,1)}, s32[8,128]{1,0:T(8,128)}) custom-call(s32[1,16]{1,0:T(1,128)} %refs_0_.9, bf16[2048,2048]{1,0:T(8,128)(2,1)} %bitcast.13, s32[8,128]{1,0:T(8,128)} %get-tuple-element.114.refs_2_), custom_call_target="tpu_custom_call" | custom-call | flops 3500000000 | bytes 1 | tf_op jit(solution)/shard_map/send/pallas_call | solution.py:68
  26.8 4.3 %pack.1 = (bf16[256,2048]{1,0:T(8,128)(2,1)}, bf16[256,2048]{1,0:T(8,128)(2,1)}, bf16[256,2048]{1,0:T(8,128)(2,1)}, s32[8,128]{1,0:T(8,128)}) custom-call(s32[1,16]{1,0:T(1,128)} %refs_0_.9, bf16[2048,2048]{1,0:T(8,128)(2,1)} %bitcast.15, bf16[768,2048]{1,0:T(8,128)(2,1)} %collective-permute-done.4.refs_2_.refs_3_.refs_4_.refs_5_, ...), custom_call_target="tpu_custom_call" | custom-call | flops 3500000000 | bytes 1 | tf_op jit(solution)/shard_map/pack/pallas_call | solution.py:68
  44.9 6.4 %collective-permute-start.15 = (bf16[512,1024]{1,0:T(8,128)(2,1)}, bf16[512,1024]{1,0:T(8,128)(2,1)}, u32[]{:S(2)}, u32[]{:S(2)}) collective-permute-start(bf16[512,1024]{1,0:T(8,128)(2,1)} %get-tuple-element.135), channel_id=1, source_target_pairs={{0,1},{3,2},{4,5},{7,6},{8,9},{11,10},{12,13},{15,14},{16,17},{19,... | collective-permute-start | bytes 3145736 | tf_op jit(solution)/shard_map/ink/ppermute | solution.py:486
  68.0 6.1 %collective-permute-done.15.refs_1_ = bf16[512,1024]{1,0:T(8,128)(2,1)} collective-permute-done((bf16[512,1024]{1,0:T(8,128)(2,1)}, bf16[512,1024]{1,0:T(8,128)(2,1)}, u32[]{:S(2)}, u32[]{:S(2)}) %collective-permute-start.15) | collective-permute-done | bytes 1048608 | tf_op jit(solution)/shard_map/ink/ppermute | solution.py:486
  75.4 6.5 %collective-permute-start.18 = (bf16[512,1024]{1,0:T(8,128)(2,1)}, bf16[512,1024]{1,0:T(8,128)(2,1)}, u32[]{:S(2)}, u32[]{:S(2)}) collective-permute-start(bf16[512,1024]{1,0:T(8,128)(2,1)} %get-tuple-element.146), channel_id=1, source_target_pairs={{0,1},{3,2},{4,5},{7,6},{8,9},{11,10},{12,13},{15,14},{16,17},{19,... | collective-permute-start | bytes 3145736 | tf_op jit(solution)/shard_map/inv/ppermute | solution.py:486
  81.9 12.3 %near.6 = (f32[256,2048]{1,0:T(8,128)}, s32[8,128]{1,0:T(8,128)}) custom-call(s32[8]{0:T(128)} %stack.39.refs_0_, bf16[128,2048]{1,0:T(8,128)(2,1)} %get-tuple-element.126.refs_0_.refs_1_, bf16[128,2048]{1,0:T(8,128)(2,1)} %copy-done.2, bf16[128,2048]{1,0:T(8,128)(2,1)} %get-tuple-element.125.refs_0_.refs_3_, ...), custom_call_target="tpu_custom_call" | custom-call | flops 3500000000 | bytes 1 | tf_op jit(solution)/shard_map/near/pallas_call | solution.py:68
  111.2 7.9 %collective-permute-done.18.refs_1_ = bf16[512,1024]{1,0:T(8,128)(2,1)} collective-permute-done((bf16[512,1024]{1,0:T(8,128)(2,1)}, bf16[512,1024]{1,0:T(8,128)(2,1)}, u32[]{:S(2)}, u32[]{:S(2)}) %collective-permute-start.18) | collective-permute-done | bytes 1048608 | tf_op jit(solution)/shard_map/inv/ppermute | solution.py:486
  121.9 12.4 %near.7 = (f32[256,2048]{1,0:T(8,128)}, s32[8,128]{1,0:T(8,128)}) custom-call(s32[8]{0:T(128)} %stack.39.refs_0_, bf16[256,2048]{1,0:T(8,128)(2,1)} %get-tuple-element.133.refs_0_.refs_1_, bf16[256,2048]{1,0:T(8,128)(2,1)} %collective-permute-done.13.refs_1_.refs_2_, bf16[8192,1024]{1,0:T(8,128)(2,1)} %refs_4_.3, bf16[8192,1024]{1,0:T(8,128)(2,1)} %refs_5_.7, ...), custom_call_target="tpu_custom_call" | custom-call | flops 3500000000 | bytes 1 | tf_op jit(solution)/shard_map/near/pallas_call | solution.py:68
  134.3 6.1 %collective-permute-done.16.refs_1_.refs_2_ = bf16[256,2048]{1,0:T(8,128)(2,1)} collective-permute-done((bf16[256,2048]{1,0:T(8,128)(2,1)}, bf16[256,2048]{1,0:T(8,128)(2,1)}, u32[]{:S(2)}, u32[]{:S(2)}) %collective-permute-start.16) | collective-permute-done | bytes 1048608 | tf_op jit(solution)/shard_map/ex3/ppermute | solution.py:486
  151.3 3.6 %collective-permute-done.20.refs_0_ = bf16[256,2048]{1,0:T(8,128)(2,1)} collective-permute-done((bf16[256,2048]{1,0:T(8,128)(2,1)}, bf16[256,2048]{1,0:T(8,128)(2,1)}, u32[]{:S(2)}, u32[]{:S(2)}) %collective-permute-start.20) | collective-permute-done | bytes 1048608 | tf_op jit(solution)/shard_map/fw1/ppermute | solution.py:486
  154.9 3.8 %collective-permute-start.23 = (bf16[256,2048]{1,0:T(8,128)(2,1)}, bf16[256,2048]{1,0:T(8,128)(2,1)}, u32[]{:S(2)}, u32[]{:S(2)}) collective-permute-start(bf16[256,2048]{1,0:T(8,128)(2,1)} %get-tuple-element.170.refs_3_.refs_0_), channel_id=1, source_target_pairs={{0,1},{1,0},{2,3},{3,2},{4,5},{5,4},{6,7},{7,6},{8,9},{9,8},{10,11... | collective-permute-start | bytes 3145736 | tf_op jit(solution)/shard_map/ex4/ppermute | solution.py:486
  158.7 3.6 %join.2 = (bf16[1024,1024]{1,0:T(8,128)(2,1)}, s32[8,128]{1,0:T(8,128)}) custom-call(s32[8]{0:T(128)} %stack.39.refs_0_, bf16[512,1024]{1,0:T(8,128)(2,1)} %get-tuple-element.174.refs_1_, bf16[512,1024]{1,0:T(8,128)(2,1)} %collective-permute-done.26.refs_2_, s32[8,128]{1,0:T(8,128)} %get-tuple-element.175.refs_3_), custom_call_target="tpu_custom_call" | custom-call | flops 3500000000 | bytes 1 | tf_op jit(solution)/shard_map/join/pallas_call | solution.py:68
  165.0 6.4 %join.3 = (bf16[1024,1024]{1,0:T(8,128)(2,1)}, bf16[2048,1024]{1,0:T(8,128)(2,1)}, s32[8,128]{1,0:T(8,128)}) custom-call(s32[8]{0:T(128)} %stack.39.refs_0_, bf16[512,1024]{1,0:T(8,128)(2,1)} %get-tuple-element.173.refs_1_, bf16[512,1024]{1,0:T(8,128)(2,1)} %collective-permute-done.25.refs_2_, bf16[1024,1024]{1,0:T(8,128)(2,1)} %get-tuple-element.176.refs_3_.refs_2_, ...), custom_call_target="tpu_custom_call" | custom-call | flops 3500000000 | bytes 1 | tf_op jit(solution)/shard_map/join/pallas_call | solution.py:68
  177.2 3.9 %collective-permute-done.24.refs_1_ = f32[16,128]{1,0:T(8,128)S(1)} collective-permute-done((f32[16,128]{1,0:T(8,128)S(1)}, f32[16,128]{1,0:T(8,128)S(1)}, u32[]{:S(2)}, u32[]{:S(2)}) %collective-permute-start.24) | collective-permute-done | bytes 8224 | tf_op jit(solution)/shard_map/half/ppermute | solution.py:486
  183.2 16.8 %near.8 = (f32[512,2048]{1,0:T(8,128)}, s32[8,128]{1,0:T(8,128)}) custom-call(s32[8]{0:T(128)} %stack.39.refs_0_, bf16[256,2048]{1,0:T(8,128)(2,1)} %get-tuple-element.144.refs_0_.refs_1_, bf16[256,2048]{1,0:T(8,128)(2,1)} %collective-permute-done.16.refs_1_.refs_2_, bf16[256,2048]{1,0:T(8,128)(2,1)} %get-tuple-element.170.refs_3_.refs_0_, ...), custom_call_target="tpu_custom_call" | custom-call | flops 3500000000 | bytes 1 | tf_op jit(solution)/shard_map/near/pallas_call | solution.py:68
  206.3 12.3 %near.9 = (f32[256,2048]{1,0:T(8,128)}, s32[8,128]{1,0:T(8,128)}) custom-call(s32[8]{0:T(128)} %stack.39.refs_0_, bf16[256,2048]{1,0:T(8,128)(2,1)} %get-tuple-element.145.refs_1_, bf16[256,2048]{1,0:T(8,128)(2,1)} %get-tuple-element.187.refs_2_, bf16[256,2048]{1,0:T(8,128)(2,1)} %get-tuple-element.153.refs_3_, ...), custom_call_target="tpu_custom_call" | custom-call | flops 3500000000 | bytes 1 | tf_op jit(solution)/shard_map/near/pallas_call | solution.py:68
  219.8 4.6 %near.10 = (f32[256,2048]{1,0:T(8,128)}, s32[8,128]{1,0:T(8,128)}) custom-call(s32[8]{0:T(128)} %stack.39.refs_0_, bf16[512,2048]{1,0:T(8,128)(2,1)} %get-tuple-element.184.refs_1_, bf16[8192,1024]{1,0:T(8,128)(2,1)} %refs_4_.3, bf16[8192,1024]{1,0:T(8,128)(2,1)} %refs_5_.7, s32[8,128]{1,0:T(8,128)} %get-tuple-element.194.refs_4_), custom_call_target="tpu_custom_call" | custom-call | flops 3500000000 | bytes 1 | tf_op jit(solution)/shard_map/near/pallas_call | solution.py:68
  224.4 5.1 %collective-permute-done.27.refs_0_ = bf16[512,2048]{1,0:T(8,128)(2,1)} collective-permute-done((bf16[512,2048]{1,0:T(8,128)(2,1)}, bf16[512,2048]{1,0:T(8,128)(2,1)}, u32[]{:S(2)}, u32[]{:S(2)}) %collective-permute-start.27) | collective-permute-done | bytes 2097184 | tf_op jit(solution)/shard_map/fw2/ppermute | solution.py:486
  239.5 3.7 %collective-permute-start.36 = (f32[16,128]{1,0:T(8,128)S(1)}, f32[16,128]{1,0:T(8,128)S(1)}, u32[]{:S(2)}, u32[]{:S(2)}) collective-permute-start(f32[16,128]{1,0:T(8,128)S(1)} %copy-done.3), channel_id=1, source_target_pairs={{0,3},{1,2},{2,1},{3,0},{4,7},{5,6},{6,5},{7,4},{8,11},{9,10},{10,... | collective-permute-start | bytes 24584 | tf_op jit(solution)/shard_map/rest/ppermute | solution.py:486
  243.2 13.2 %near.11 = (f32[512,2048]{1,0:T(8,128)}, s32[8,128]{1,0:T(8,128)}) custom-call(s32[8]{0:T(128)} %stack.39.refs_0_, bf16[512,2048]{1,0:T(8,128)(2,1)} %get-tuple-element.181.refs_1_, bf16[512,2048]{1,0:T(8,128)(2,1)} %get-tuple-element.196.refs_2_, bf16[512,2048]{1,0:T(8,128)(2,1)} %collective-permute-done.31.refs_1_.refs_3_, bf16[8192,1024]{1,0:T(8,128)(2,1)} %refs_4_.3, ...), custom_call_target="tpu_custom_call" | custom-call | flops 3500000000 | bytes 1 | tf_op jit(solution)/shard_map/near/pallas_call | solution.py:68
  256.5 15.2 %collective-permute-done.37.refs_9_ = bf16[256,2048]{1,0:T(8,128)(2,1)} collective-permute-done((bf16[256,2048]{1,0:T(8,128)(2,1)}, bf16[256,2048]{1,0:T(8,128)(2,1)}, u32[]{:S(2)}, u32[]{:S(2)}) %collective-permute-start.37) | collective-permute-done | bytes 1048608 | tf_op jit(solution)/shard_map/far3/ppermute | solution.py:486
  271.6 8.4 %finish.2 = (bf16[1024,1024]{1,0:T(8,128)(2,1)}, bf16[1024,1024]{1,0:T(8,128)(2,1)}, s32[8,128]{1,0:T(8,128)}) custom-call(s32[8,4]{1,0:T(8,128)} %get-tuple-element.112.refs_0_, f32[256,2048]{1,0:T(8,128)} %get-tuple-element.209.refs_1_.refs_3_, f32[256,2048]{1,0:T(8,128)} %get-tuple-element.210.refs_2_.refs_4_, ...), custom_call_target="tpu_custom_call" | custom-call | flops 3500000000 | bytes 1 | tf_op jit(solution)/shard_map/finish/pallas_call | solution.py:68
  280.1 13.6 %collective-permute-done.35.refs_3_ = bf16[256,2048]{1,0:T(8,128)(2,1)} collective-permute-done((bf16[256,2048]{1,0:T(8,128)(2,1)}, bf16[256,2048]{1,0:T(8,128)(2,1)}, u32[]{:S(2)}, u32[]{:S(2)}) %collective-permute-start.35) | collective-permute-done | bytes 1048608 | tf_op jit(solution)/shard_map/far4/ppermute | solution.py:486
  293.6 5.2 %finish.3 = (bf16[1024,1024]{1,0:T(8,128)(2,1)}, bf16[1024,1024]{1,0:T(8,128)(2,1)}, s32[8,128]{1,0:T(8,128)}) custom-call(s32[8,4]{1,0:T(8,128)} %get-tuple-element.112.refs_0_, f32[512,2048]{1,0:T(8,128)} %get-tuple-element.180.refs_7_.refs_1_, f32[512,2048]{1,0:T(8,128)} %get-tuple-element.204.refs_6_.refs_2_, ...), custom_call_target="tpu_custom_call", output_to_operand_aliasing={{0}: (10, {}), {1}: (11, {})} | custom-call | flops 3500000000 | bytes 1 | tf_op jit(solution)/shard_map/finish/pallas_call | solution.py:68
  (119 shorter events, 111.7 us)
Async XLA Ops:
  31.1 26.0 %collective-permute-start.9 = (bf16[256,2048]{1,0:T(8,128)(2,1)}, bf16[256,2048]{1,0:T(8,128)(2,1)}, u32[]{:S(2)}, u32[]{:S(2)}) collective-permute-start(bf16[256,2048]{1,0:T(8,128)(2,1)} %get-tuple-element.122), channel_id=1, source_target_pairs={{0,8},{4,12},{8,0},{12,4},{1,9},{5,13},{9,1},{13,5},{2,10},{6,14},... | collective-permute-start | bytes 3145736 | tf_op jit(solution)/shard_map/h1/ppermute | solution.py:486
  34.9 16.3 %collective-permute-start.10 = (bf16[128,2048]{1,0:T(8,128)(2,1)}, bf16[128,2048]{1,0:T(8,128)(2,1)}, u32[]{:S(2)}, u32[]{:S(2)}) collective-permute-start(bf16[128,2048]{1,0:T(8,128)(2,1)} %get-tuple-element.125.refs_0_.refs_3_), channel_id=1, source_target_pairs={{0,1},{1,0},{2,3},{3,2},{4,5},{5,4},{6,7},{7,6},{8,9},{9,8},{10,11... | collective-permute-start | bytes 1572872 | tf_op jit(solution)/shard_map/ex1/ppermute | solution.py:486
  43.2 24.7 %collective-permute-start.14 = (bf16[256,2048]{1,0:T(8,128)(2,1)}, bf16[256,2048]{1,0:T(8,128)(2,1)}, u32[]{:S(2)}, u32[]{:S(2)}) collective-permute-start(bf16[256,2048]{1,0:T(8,128)(2,1)} %get-tuple-element.134), channel_id=1, source_target_pairs={{1,2},{2,1},{5,6},{6,5},{9,10},{10,9},{13,14},{14,13},{17,18},{18,... | collective-permute-start | bytes 3145736 | tf_op jit(solution)/shard_map/mr0/ppermute | solution.py:486
  44.9 29.2 %collective-permute-start.15 = (bf16[512,1024]{1,0:T(8,128)(2,1)}, bf16[512,1024]{1,0:T(8,128)(2,1)}, u32[]{:S(2)}, u32[]{:S(2)}) collective-permute-start(bf16[512,1024]{1,0:T(8,128)(2,1)} %get-tuple-element.135), channel_id=1, source_target_pairs={{0,1},{3,2},{4,5},{7,6},{8,9},{11,10},{12,13},{15,14},{16,17},{19,... | collective-permute-start | bytes 3145736 | tf_op jit(solution)/shard_map/ink/ppermute | solution.py:486
  53.5 54.4 %collective-permute-start.19 = (bf16[256,2048]{1,0:T(8,128)(2,1)}, bf16[256,2048]{1,0:T(8,128)(2,1)}, u32[]{:S(2)}, u32[]{:S(2)}) collective-permute-start(bf16[256,2048]{1,0:T(8,128)(2,1)} %get-tuple-element.148), channel_id=1, source_target_pairs={{1,2},{2,1},{5,6},{6,5},{9,10},{10,9},{13,14},{14,13},{17,18},{18,... | collective-permute-start | bytes 3145736 | tf_op jit(solution)/shard_map/mr1/ppermute | solution.py:486
  62.3 34.3 %collective-permute-start.13 = (bf16[256,2048]{1,0:T(8,128)(2,1)}, bf16[256,2048]{1,0:T(8,128)(2,1)}, u32[]{:S(2)}, u32[]{:S(2)}) collective-permute-start(bf16[256,2048]{1,0:T(8,128)(2,1)} %get-tuple-element.133.refs_0_.refs_1_), channel_id=1, source_target_pairs={{0,1},{1,0},{2,3},{3,2},{4,5},{5,4},{6,7},{7,6},{8,9},{9,8},{10,11... | collective-permute-start | bytes 3145736 | tf_op jit(solution)/shard_map/ex2/ppermute | solution.py:486
  64.1 37.3 %collective-permute-start.12 = (bf16[256,2048]{1,0:T(8,128)(2,1)}, bf16[256,2048]{1,0:T(8,128)(2,1)}, u32[]{:S(2)}, u32[]{:S(2)}) collective-permute-start(bf16[256,2048]{1,0:T(8,128)(2,1)} %get-tuple-element.132), channel_id=1, source_target_pairs={{0,8},{4,12},{8,0},{12,4},{1,9},{5,13},{9,1},{13,5},{2,10},{6,14},... | collective-permute-start | bytes 3145736 | tf_op jit(solution)/shard_map/h2/ppermute | solution.py:486
  74.1 37.1 %collective-permute-start.17 = (bf16[256,2048]{1,0:T(8,128)(2,1)}, bf16[256,2048]{1,0:T(8,128)(2,1)}, u32[]{:S(2)}, u32[]{:S(2)}) collective-permute-start(bf16[256,2048]{1,0:T(8,128)(2,1)} %get-tuple-element.145.refs_1_), channel_id=1, source_target_pairs={{1,0},{2,3},{5,4},{6,7},{9,8},{10,11},{13,12},{14,15},{17,16},{18,... | collective-permute-start | bytes 3145736 | tf_op jit(solution)/shard_map/fw0/ppermute | solution.py:486
  75.4 43.7 %collective-permute-start.18 = (bf16[512,1024]{1,0:T(8,128)(2,1)}, bf16[512,1024]{1,0:T(8,128)(2,1)}, u32[]{:S(2)}, u32[]{:S(2)}) collective-permute-start(bf16[512,1024]{1,0:T(8,128)(2,1)} %get-tuple-element.146), channel_id=1, source_target_pairs={{0,1},{3,2},{4,5},{7,6},{8,9},{11,10},{12,13},{15,14},{16,17},{19,... | collective-permute-start | bytes 3145736 | tf_op jit(solution)/shard_map/inv/ppermute | solution.py:486
  99.5 45.1 %collective-permute-start.22 = (bf16[512,2048]{1,0:T(8,128)(2,1)}, bf16[512,2048]{1,0:T(8,128)(2,1)}, u32[]{:S(2)}, u32[]{:S(2)}) collective-permute-start(bf16[512,2048]{1,0:T(8,128)(2,1)} %get-tuple-element.155), channel_id=1, source_target_pairs={{1,2},{2,1},{5,6},{6,5},{9,10},{10,9},{13,14},{14,13},{17,18},{18,... | collective-permute-start | bytes 6291464 | tf_op jit(solution)/shard_map/mr2/ppermute | solution.py:486
  104.8 35.6 %collective-permute-start.16 = (bf16[256,2048]{1,0:T(8,128)(2,1)}, bf16[256,2048]{1,0:T(8,128)(2,1)}, u32[]{:S(2)}, u32[]{:S(2)}) collective-permute-start(bf16[256,2048]{1,0:T(8,128)(2,1)} %get-tuple-element.144.refs_0_.refs_1_), channel_id=1, source_target_pairs={{0,1},{1,0},{2,3},{3,2},{4,5},{5,4},{6,7},{7,6},{8,9},{9,8},{10,11... | collective-permute-start | bytes 3145736 | tf_op jit(solution)/shard_map/ex3/ppermute | solution.py:486
  107.9 38.7 %collective-permute-start.21 = (bf16[256,2048]{1,0:T(8,128)(2,1)}, bf16[256,2048]{1,0:T(8,128)(2,1)}, u32[]{:S(2)}, u32[]{:S(2)}) collective-permute-start(bf16[256,2048]{1,0:T(8,128)(2,1)} %get-tuple-element.154), channel_id=1, source_target_pairs={{0,8},{4,12},{8,0},{12,4},{1,9},{5,13},{9,1},{13,5},{2,10},{6,14},... | collective-permute-start | bytes 3145736 | tf_op jit(solution)/shard_map/h3/ppermute | solution.py:486
  119.1 35.8 %collective-permute-start.20 = (bf16[256,2048]{1,0:T(8,128)(2,1)}, bf16[256,2048]{1,0:T(8,128)(2,1)}, u32[]{:S(2)}, u32[]{:S(2)}) collective-permute-start(bf16[256,2048]{1,0:T(8,128)(2,1)} %get-tuple-element.153.refs_3_), channel_id=1, source_target_pairs={{1,0},{2,3},{5,4},{6,7},{9,8},{10,11},{13,12},{14,15},{17,16},{18,... | collective-permute-start | bytes 3145736 | tf_op jit(solution)/shard_map/fw1/ppermute | solution.py:486
  120.3 38.4 %collective-permute-start.26 = (bf16[512,1024]{1,0:T(8,128)(2,1)}, bf16[512,1024]{1,0:T(8,128)(2,1)}, u32[]{:S(2)}, u32[]{:S(2)}) collective-permute-start(bf16[512,1024]{1,0:T(8,128)(2,1)} %get-tuple-element.174.refs_1_), channel_id=1, source_target_pairs={{0,16},{16,0},{1,17},{17,1},{2,18},{18,2},{3,19},{19,3},{4,20},{20... | collective-permute-start | bytes 3145736 | tf_op jit(solution)/shard_map/wk1/ppermute | solution.py:486
  140.4 24.6 %collective-permute-start.25 = (bf16[512,1024]{1,0:T(8,128)(2,1)}, bf16[512,1024]{1,0:T(8,128)(2,1)}, u32[]{:S(2)}, u32[]{:S(2)}) collective-permute-start(bf16[512,1024]{1,0:T(8,128)(2,1)} %get-tuple-element.173.refs_1_), channel_id=1, source_target_pairs={{0,8},{4,12},{8,0},{12,4},{1,9},{5,13},{9,1},{13,5},{2,10},{6,14},... | collective-permute-start | bytes 3145736 | tf_op jit(solution)/shard_map/wv1/ppermute | solution.py:486
  144.6 55.4 %collective-permute-start.28 = (bf16[512,2048]{1,0:T(8,128)(2,1)}, bf16[512,2048]{1,0:T(8,128)(2,1)}, u32[]{:S(2)}, u32[]{:S(2)}) collective-permute-start(bf16[512,2048]{1,0:T(8,128)(2,1)} %get-tuple-element.182), channel_id=1, source_target_pairs={{1,2},{2,1},{5,6},{6,5},{9,10},{10,9},{13,14},{14,13},{17,18},{18,... | collective-permute-start | bytes 6291464 | tf_op jit(solution)/shard_map/mr3/ppermute | solution.py:486
  154.9 28.3 %collective-permute-start.23 = (bf16[256,2048]{1,0:T(8,128)(2,1)}, bf16[256,2048]{1,0:T(8,128)(2,1)}, u32[]{:S(2)}, u32[]{:S(2)}) collective-permute-start(bf16[256,2048]{1,0:T(8,128)(2,1)} %get-tuple-element.170.refs_3_.refs_0_), channel_id=1, source_target_pairs={{0,1},{1,0},{2,3},{3,2},{4,5},{5,4},{6,7},{7,6},{8,9},{9,8},{10,11... | collective-permute-start | bytes 3145736 | tf_op jit(solution)/shard_map/ex4/ppermute | solution.py:486
  171.4 47.3 %collective-permute-start.30 = (bf16[1024,1024]{1,0:T(8,128)(2,1)}, bf16[1024,1024]{1,0:T(8,128)(2,1)}, u32[]{:S(2)}, u32[]{:S(2)}) collective-permute-start(bf16[1024,1024]{1,0:T(8,128)(2,1)} %get-tuple-element.185.refs_3_), channel_id=1, source_target_pairs={{0,16},{16,0},{1,17},{17,1},{2,18},{18,2},{3,19},{19,3},{4,20},{20... | collective-permute-start | bytes 6291464 | tf_op jit(solution)/shard_map/wv2/ppermute | solution.py:486
  172.9 46.3 %collective-permute-start.29 = (bf16[1024,1024]{1,0:T(8,128)(2,1)}, bf16[1024,1024]{1,0:T(8,128)(2,1)}, u32[]{:S(2)}, u32[]{:S(2)}) collective-permute-start(bf16[1024,1024]{1,0:T(8,128)(2,1)} %get-tuple-element.176.refs_3_.refs_2_), channel_id=1, source_target_pairs={{0,8},{4,12},{8,0},{12,4},{1,9},{5,13},{9,1},{13,5},{2,10},{6,14},... | collective-permute-start | bytes 6291464 | tf_op jit(solution)/shard_map/wk2/ppermute | solution.py:486
  181.7 47.8 %collective-permute-start.27 = (bf16[512,2048]{1,0:T(8,128)(2,1)}, bf16[512,2048]{1,0:T(8,128)(2,1)}, u32[]{:S(2)}, u32[]{:S(2)}) collective-permute-start(bf16[512,2048]{1,0:T(8,128)(2,1)} %get-tuple-element.181.refs_1_), channel_id=1, source_target_pairs={{1,0},{2,3},{5,4},{6,7},{9,8},{10,11},{13,12},{14,15},{17,16},{18,... | collective-permute-start | bytes 6291464 | tf_op jit(solution)/shard_map/fw2/ppermute | solution.py:486
  204.2 31.7 %collective-permute-start.31 = (bf16[512,2048]{1,0:T(8,128)(2,1)}, bf16[512,2048]{1,0:T(8,128)(2,1)}, u32[]{:S(2)}, u32[]{:S(2)}) collective-permute-start(bf16[512,2048]{1,0:T(8,128)(2,1)} %get-tuple-element.197), channel_id=1, source_target_pairs={{1,2},{2,1},{5,6},{6,5},{9,10},{10,9},{13,14},{14,13},{17,18},{18,... | collective-permute-start | bytes 6291464 | tf_op jit(solution)/shard_map/mr4/ppermute | solution.py:486
  234.6 37.0 %collective-permute-start.37 = (bf16[256,2048]{1,0:T(8,128)(2,1)}, bf16[256,2048]{1,0:T(8,128)(2,1)}, u32[]{:S(2)}, u32[]{:S(2)}) collective-permute-start(bf16[256,2048]{1,0:T(8,128)(2,1)} %get-tuple-element.213), channel_id=1, source_target_pairs={{1,0},{2,3},{5,4},{6,7},{9,8},{10,11},{13,12},{14,15},{17,16},{18,... | collective-permute-start | bytes 3145736 | tf_op jit(solution)/shard_map/far3/ppermute | solution.py:486
  238.0 55.7 %collective-permute-start.35 = (bf16[256,2048]{1,0:T(8,128)(2,1)}, bf16[256,2048]{1,0:T(8,128)(2,1)}, u32[]{:S(2)}, u32[]{:S(2)}) collective-permute-start(bf16[256,2048]{1,0:T(8,128)(2,1)} %get-tuple-element.205), channel_id=1, source_target_pairs={{1,0},{2,3},{5,4},{6,7},{9,8},{10,11},{13,12},{14,15},{17,16},{18,... | collective-permute-start | bytes 3145736 | tf_op jit(solution)/shard_map/far4/ppermute | solution.py:486
  239.5 17.0 %collective-permute-start.36 = (f32[16,128]{1,0:T(8,128)S(1)}, f32[16,128]{1,0:T(8,128)S(1)}, u32[]{:S(2)}, u32[]{:S(2)}) collective-permute-start(f32[16,128]{1,0:T(8,128)S(1)} %copy-done.3), channel_id=1, source_target_pairs={{0,3},{1,2},{2,1},{3,0},{4,7},{5,6},{6,5},{7,4},{8,11},{9,10},{10,... | collective-permute-start | bytes 24584 | tf_op jit(solution)/shard_map/rest/ppermute | solution.py:486
  (24 other events, 194.4 us)
